TPU v7x, 128 devices: a whole 4x4x4 slice. The times are simulated.
128 devices in a mesh: dp: 16 (over y, x), tensor: 8 (over z, core).
Axes of the slice: x: 4, y: 4, z: 4, core: 2. Of those that a mesh axis runs over, the one named last changes fastest.
Arguments:
- tokens: bfloat16 [16384, 1536], P('dp'), may hold values from -6 to 6
- norm_gain: float32 [1536], replicated, may hold values from 0.5 to 1.5
- in_gate: bfloat16 [1536, 3072], P(None, 'tensor'), may hold values from -0.15625 to 0.15625
- in_value: bfloat16 [1536, 3072], P(None, 'tensor'), may hold values from -0.15625 to 0.15625
- in_state: bfloat16 [1536, 256], replicated, may hold values from -0.15625 to 0.15625
- in_step: bfloat16 [1536, 48], P(None, 'tensor'), may hold values from -0.15625 to 0.15625
- step_bias: float32 [48], P('tensor'), may hold values from -6.5 to -3
- decay_log: float32 [48], P('tensor'), may hold values from 0 to 2.5
- skip_gain: float32 [48], P('tensor'), may hold values from 0.5 to 2
- conv_value_kernel: float32 [4, 3072], P(None, 'tensor'), may hold values from -3 to 3
- conv_value_bias: float32 [3072], P('tensor'), may hold values from -0.5 to 0.5
- conv_state_kernel: float32 [4, 256], replicated, may hold values from -3 to 3
- conv_state_bias: float32 [256], replicated, may hold values from -0.5 to 0.5
- gate_gain: float32 [3072], P('tensor'), may hold values from 0.5 to 1.5
- out_weight: bfloat16 [3072, 1536], P('tensor'), may hold values from -0.109375 to 0.109375
- cotangent: bfloat16 [16384, 1536], P('dp'), may hold values from -6 to 6
Outputs:
- block_output: bfloat16 [16384, 1536], P('dp')
- grad_tokens: bfloat16 [16384, 1536], P('dp')
- grad_norm_gain: float32 [1536], replicated
- grad_in_gate: float32 [1536, 3072], P(None, 'tensor')
- grad_in_value: float32 [1536, 3072], P(None, 'tensor')
- grad_in_state: float32 [1536, 256], replicated
- grad_in_step: float32 [1536, 48], P(None, 'tensor')
- grad_step_bias: float32 [48], P('tensor')
- grad_decay_log: float32 [48], P('tensor')
- grad_skip_gain: float32 [48], P('tensor')
- grad_conv_value_kernel: float32 [4, 3072], P(None, 'tensor')
- grad_conv_value_bias: float32 [3072], P('tensor')
- grad_conv_state_kernel: float32 [4, 256], replicated
- grad_conv_state_bias: float32 [256], replicated
- grad_gate_gain: float32 [3072], P('tensor')
- grad_out_weight: float32 [3072, 1536], P('tensor')
All inputs are finite; a program needn't handle non-finite values.
Results may differ from a plain program's by a relative error of at most 0.012.
The roundings to bfloat16 on the way count: a program that leaves them out, or rounds other values in their place, can miss the bound.
Values may be sent and summed in bfloat16 or wider, within the bound.
No kernel may reach another device: no remote copies, remote signals or barrier semaphores. Data moves between devices by JAX's collectives and lax.ppermute only.
A program may use at most 128 MiB of HBM per device.

v0:
```python
from functools import partial

import jax
import jax.numpy as jnp
from jax import lax
from jax.sharding import PartitionSpec as P

STATE = 128
CONV = 4
BLOCK = 256
LEN = 1024


epsilon = 1e-05
scan_precision = lax.Precision.HIGH


def causal_conv(inputs, kernel, offset_bias):
    padded = jnp.pad(inputs, ((0, 0), (CONV - 1, 0), (0, 0)))
    result = offset_bias + padded[:, 0:LEN, :] * kernel[0]
    for position in range(1, CONV):
        result = result + padded[:, position : position + LEN, :] * kernel[position]
    return result


def conv_silu(seq_count, inputs, kernel, offset_bias):
    shaped = inputs.reshape(seq_count, LEN, inputs.shape[1])
    return jax.nn.silu(causal_conv(shaped, kernel, offset_bias)).reshape(inputs.shape)


def scan_sequence(values, step_sizes, keys_in, reads_in, decay_rates):
    blocks = LEN // BLOCK
    head_count = step_sizes.shape[1]
    causal = jnp.arange(BLOCK)[:, None] >= jnp.arange(BLOCK)[None, :]

    def advance(carried, pieces):
        block_values, block_steps, block_keys, block_reads = pieces
        log_decay = jnp.cumsum(block_steps * decay_rates, axis=0)
        spread = log_decay[:, None, :] - log_decay[None, :, :]
        decays = jnp.where(
            causal[:, :, None], jnp.exp(jnp.where(causal[:, :, None], spread, 0.0)), 0.0
        )
        intersections = jnp.dot(block_reads, block_keys.T, precision=scan_precision)
        mixing = intersections[:, :, None] * decays * block_steps[None, :, :]
        inside = jnp.einsum("ijh,jhp->ihp", mixing, block_values, precision=scan_precision)
        carried_in = (
            jnp.einsum("in,hnp->ihp", block_reads, carried, precision=scan_precision)
            * jnp.exp(log_decay)[:, :, None]
        )
        weights_end = jnp.exp(log_decay[-1][None, :] - log_decay) * block_steps
        updated = carried * jnp.exp(log_decay[-1])[:, None, None] + jnp.einsum(
            "jn,jh,jhp->hnp", block_keys, weights_end, block_values, precision=scan_precision
        )
        return (updated, inside + carried_in)

    start_state = jnp.zeros((head_count, keys_in.shape[1], values.shape[2]), jnp.float32)
    shaped = (
        values.reshape(blocks, BLOCK, head_count, values.shape[2]),
        step_sizes.reshape(blocks, BLOCK, head_count),
        keys_in.reshape(blocks, BLOCK, keys_in.shape[1]),
        reads_in.reshape(blocks, BLOCK, reads_in.shape[1]),
    )
    final_state, outputs = lax.scan(jax.checkpoint(advance), start_state, shaped)
    return outputs.reshape(LEN, head_count, values.shape[2])


def mixer_rows(seq_count, values, states, step_pre, gate_pre, step_bias, decay_log, skip_gain):
    head_count = step_bias.shape[0]
    head_width = values.shape[1] // head_count
    step_sizes = jax.nn.softplus(step_pre + step_bias)
    decay_rates = -jnp.exp(decay_log)
    per_head = values.reshape(seq_count, LEN, head_count, head_width)
    keys_in = states[:, :STATE].reshape(seq_count, LEN, STATE)
    reads_in = states[:, STATE:].reshape(seq_count, LEN, STATE)
    scanned = jax.vmap(scan_sequence, in_axes=(0, 0, 0, 0, None))(
        per_head, step_sizes.reshape(seq_count, LEN, head_count), keys_in, reads_in, decay_rates
    )
    scanned = scanned + skip_gain[:, None] * per_head
    return scanned.reshape(values.shape) * jax.nn.silu(gate_pre)


def dot_transposed(left, right):
    return lax.dot_general(
        left, right, (((1,), (1,)), ((), ())), preferred_element_type=jnp.float32
    )


def dot_leading(left, right):
    return lax.dot_general(
        left, right, (((0,), (0,)), ((), ())), preferred_element_type=jnp.float32
    )


def norm_back(token_rows, grad_normed, norm_gain, inverse):
    scaled = grad_normed * norm_gain
    moment = jnp.mean(scaled * token_rows, axis=1, keepdims=True)
    grad_rows = inverse * scaled - token_rows * inverse**3 * moment
    gain_part = jnp.sum(grad_normed * token_rows * inverse, axis=0)
    return (grad_rows, gain_part)


def on_device(
    tokens,
    norm_gain,
    in_gate,
    in_value,
    in_state,
    in_step,
    step_bias,
    decay_log,
    skip_gain,
    conv_value_kernel,
    conv_value_bias,
    conv_state_kernel,
    conv_state_bias,
    gate_gain,
    out_weight,
    cotangent,
):
    rows_wide = tokens.astype(jnp.float32)
    row_count = rows_wide.shape[0]
    seq_count = row_count // LEN
    group_size = lax.axis_size("tensor")
    total_inner = in_gate.shape[1] * group_size
    inverse = lax.rsqrt(jnp.mean(rows_wide * rows_wide, axis=1, keepdims=True) + epsilon)
    normed = (rows_wide * inverse * norm_gain).astype(jnp.bfloat16)
    gate_pre = jnp.dot(normed, in_gate, preferred_element_type=jnp.float32)
    value_pre = jnp.dot(normed, in_value, preferred_element_type=jnp.float32)
    state_pre = jnp.dot(normed, in_state, preferred_element_type=jnp.float32)
    step_pre = jnp.dot(normed, in_step, preferred_element_type=jnp.float32)
    value_act, value_pullback = jax.vjp(
        partial(conv_silu, seq_count), value_pre, conv_value_kernel, conv_value_bias
    )
    state_act, state_pullback = jax.vjp(
        partial(conv_silu, seq_count), state_pre, conv_state_kernel, conv_state_bias
    )
    values = lax.optimization_barrier(value_act.astype(jnp.bfloat16)).astype(jnp.float32)
    states = lax.optimization_barrier(state_act.astype(jnp.bfloat16)).astype(jnp.float32)
    gated_rows, mixer_pullback = jax.vjp(
        partial(mixer_rows, seq_count),
        values,
        states,
        step_pre,
        gate_pre,
        step_bias,
        decay_log,
        skip_gain,
    )
    squares = lax.psum(jnp.sum(gated_rows * gated_rows, axis=1), "tensor")
    gate_scale = lax.rsqrt(squares / total_inner + epsilon)[:, None]
    outgoing = (gated_rows * gate_scale * gate_gain).astype(jnp.bfloat16)
    summed = lax.psum(
        jnp.dot(outgoing, out_weight, preferred_element_type=jnp.float32).astype(jnp.bfloat16),
        "tensor",
    ).astype(jnp.float32)
    block_output = (rows_wide + summed).astype(jnp.bfloat16)
    grad_out_weight = dot_leading(outgoing, cotangent)
    grad_outgoing = dot_transposed(cotangent, out_weight)
    grad_gate_gain = jnp.sum(grad_outgoing * gated_rows * gate_scale, axis=0)
    scaled = grad_outgoing * gate_gain
    gate_moment = lax.psum(jnp.sum(scaled * gated_rows, axis=1), "tensor")
    grad_gated = (
        gate_scale * scaled - gated_rows * gate_scale**3 * (gate_moment / total_inner)[:, None]
    )
    (
        grad_values,
        grad_states,
        grad_step_pre,
        grad_gate_pre,
        grad_step_bias,
        grad_decay_log,
        grad_skip_gain,
    ) = mixer_pullback(grad_gated)
    grad_states = lax.psum(grad_states, "tensor")
    grad_value_pre, grad_conv_value_kernel, grad_conv_value_bias = value_pullback(grad_values)
    grad_state_pre, grad_conv_state_kernel, grad_conv_state_bias = state_pullback(grad_states)
    round_gate = grad_gate_pre.astype(jnp.bfloat16)
    round_value = grad_value_pre.astype(jnp.bfloat16)
    round_state = grad_state_pre.astype(jnp.bfloat16)
    round_step = grad_step_pre.astype(jnp.bfloat16)
    grad_in_gate = dot_leading(normed, round_gate)
    grad_in_value = dot_leading(normed, round_value)
    grad_in_state = dot_leading(normed, round_state)
    grad_in_step = dot_leading(normed, round_step)
    partial_sum = (
        dot_transposed(round_gate, in_gate)
        + dot_transposed(round_value, in_value)
        + dot_transposed(round_step, in_step)
    )
    grad_normed = lax.psum(partial_sum, "tensor") + dot_transposed(round_state, in_state)
    grad_rows, grad_norm_gain = norm_back(rows_wide, grad_normed, norm_gain, inverse)
    grad_tokens = (cotangent.astype(jnp.float32) + grad_rows).astype(jnp.bfloat16)
    (
        grad_norm_gain,
        grad_in_gate,
        grad_in_value,
        grad_in_state,
        grad_in_step,
        grad_step_bias,
        grad_decay_log,
        grad_skip_gain,
        grad_conv_value_kernel,
        grad_conv_value_bias,
        grad_conv_state_kernel,
        grad_conv_state_bias,
        grad_gate_gain,
        grad_out_weight,
    ) = lax.psum(
        (
            grad_norm_gain,
            grad_in_gate,
            grad_in_value,
            grad_in_state,
            grad_in_step,
            grad_step_bias,
            grad_decay_log,
            grad_skip_gain,
            grad_conv_value_kernel,
            grad_conv_value_bias,
            grad_conv_state_kernel,
            grad_conv_state_bias,
            grad_gate_gain,
            grad_out_weight,
        ),
        "dp",
    )
    return (
        block_output,
        grad_tokens,
        grad_norm_gain,
        grad_in_gate,
        grad_in_value,
        grad_in_state,
        grad_in_step,
        grad_step_bias,
        grad_decay_log,
        grad_skip_gain,
        grad_conv_value_kernel,
        grad_conv_value_bias,
        grad_conv_state_kernel,
        grad_conv_state_bias,
        grad_gate_gain,
        grad_out_weight,
    )


def solution(mesh):
    placed = (
        P("dp", None),
        P(),
        P(None, "tensor"),
        P(None, "tensor"),
        P(),
        P(None, "tensor"),
        P("tensor"),
        P("tensor"),
        P("tensor"),
        P(None, "tensor"),
        P("tensor"),
        P(),
        P(),
        P("tensor"),
        P("tensor", None),
        P("dp", None),
    )
    return jax.shard_map(
        on_device,
        mesh=mesh,
        in_specs=placed,
        out_specs=(
            P("dp", None),
            P("dp", None),
            P(),
            P(None, "tensor"),
            P(None, "tensor"),
            P(),
            P(None, "tensor"),
            P("tensor"),
            P("tensor"),
            P("tensor"),
            P(None, "tensor"),
            P("tensor"),
            P(),
            P(),
            P("tensor"),
            P("tensor", None),
        ),
        check_vma=False,
    )
```

profile of v0, /device:TPU:1, one launch (start us, length us, event | category | flops | bytes accessed | tf_op | source)
XLA Modules:
  0.0 680.7 jit_solution(17434903103820272547)
XLA Ops:
  30.2 70.0 %while.44 = (s32[]{:T(128)}, f32[1,6,128,64]{2,3,1,0:T(8,128)S(1)}, f32[4,1,256,6,64]{2,0,4,3,1:T(4,128)}, f32[4,1,6,128,64]{3,4,2,1,0:T(8,128)}, f32[4,1,256,6]...) while((s32[]{:T(128)}, f32[1,6,128,64]{2,3,1,0:T(8,128)S(1)}, ...), condition=%wide.region_4.5_spmd.clone.clone, body=%wide.region_1.4_spmd.clone.clone.sunk | while | flops 354931200 | bytes 6275443 | solution.py:63
  36.5 9.5 %dynamic_update_slice.75 = f32[4,1,256,6,64]{2,0,4,3,1:T(4,128)} dynamic-update-slice(f32[4,1,256,6,64]{2,0,4,3,1:T(4,128)} %get-tuple-element.1082, f32[1,1,256,6,64]{2,0,4,3,1:T(1,128)S(1)} %copy.331, s32[]{:T(128)} %get-tuple-element.1080, s32[]{:T(128)} %constant.124.clone.1..sunk.1, s32[]{:T(128)} %constant.124.clone.1..sunk.1, s32[]{:T(128)} %constant.124.clone.1..sunk.1, ...) | dynamic-update-slice | bytes 786436 | tf_op jit(solution)/shard_map/jvp(vmap())/while/body/jit(dynamic_update_index_in_dim)/dynamic_update_slice | solution.py:63
  54.1 9.5 %dynamic_update_slice.75 = f32[4,1,256,6,64]{2,0,4,3,1:T(4,128)} dynamic-update-slice(f32[4,1,256,6,64]{2,0,4,3,1:T(4,128)} %get-tuple-element.1082, f32[1,1,256,6,64]{2,0,4,3,1:T(1,128)S(1)} %copy.331, s32[]{:T(128)} %get-tuple-element.1080, s32[]{:T(128)} %constant.124.clone.1..sunk.1, s32[]{:T(128)} %constant.124.clone.1..sunk.1, s32[]{:T(128)} %constant.124.clone.1..sunk.1, ...) | dynamic-update-slice | bytes 786436 | tf_op jit(solution)/shard_map/jvp(vmap())/while/body/jit(dynamic_update_index_in_dim)/dynamic_update_slice | solution.py:63
  71.6 9.5 %dynamic_update_slice.75 = f32[4,1,256,6,64]{2,0,4,3,1:T(4,128)} dynamic-update-slice(f32[4,1,256,6,64]{2,0,4,3,1:T(4,128)} %get-tuple-element.1082, f32[1,1,256,6,64]{2,0,4,3,1:T(1,128)S(1)} %copy.331, s32[]{:T(128)} %get-tuple-element.1080, s32[]{:T(128)} %constant.124.clone.1..sunk.1, s32[]{:T(128)} %constant.124.clone.1..sunk.1, s32[]{:T(128)} %constant.124.clone.1..sunk.1, ...) | dynamic-update-slice | bytes 786436 | tf_op jit(solution)/shard_map/jvp(vmap())/while/body/jit(dynamic_update_index_in_dim)/dynamic_update_slice | solution.py:63
  89.1 9.5 %dynamic_update_slice.75 = f32[4,1,256,6,64]{2,0,4,3,1:T(4,128)} dynamic-update-slice(f32[4,1,256,6,64]{2,0,4,3,1:T(4,128)} %get-tuple-element.1082, f32[1,1,256,6,64]{2,0,4,3,1:T(1,128)S(1)} %copy.331, s32[]{:T(128)} %get-tuple-element.1080, s32[]{:T(128)} %constant.124.clone.1..sunk.1, s32[]{:T(128)} %constant.124.clone.1..sunk.1, s32[]{:T(128)} %constant.124.clone.1..sunk.1, ...) | dynamic-update-slice | bytes 786436 | tf_op jit(solution)/shard_map/jvp(vmap())/while/body/jit(dynamic_update_index_in_dim)/dynamic_update_slice | solution.py:63
  103.4 3.1 copy.215
  106.6 6.0 multiply_reduce_fusion.10
  112.6 14.4 %psum.133 = f32[1024]{0:T(1024)S(1)} all-reduce(f32[1024]{0:T(1024)S(1)} %get-tuple-element.811), channel_id=1, replica_groups=mesh['dp'=16,'tensor'=8] {'tensor'}, use_global_device_ids=true, to_apply=%region_6.7 | all-reduce | flops 1024 | bytes 8192 | tf_op jit(solution)/shard_map/psum | solution.py:149
  127.1 6.4 multiply_reduce_fusion.3
  133.5 14.7 %psum.135 = f32[1024]{0:T(1024)S(1)} all-reduce(f32[1024]{0:T(1024)S(1)} %get-tuple-element.720), channel_id=1, replica_groups=mesh['dp'=16,'tensor'=8] {'tensor'}, use_global_device_ids=true, to_apply=%region_9.10 | all-reduce | flops 1024 | bytes 8192 | tf_op jit(solution)/shard_map/psum | solution.py:161
  148.1 5.3 multiply_reduce_fusion.8
  161.6 167.7 %while.43 = (s32[]{:T(128)}, f32[6]{0:T(128)}, f32[1,6,128,64]{2,3,1,0:T(8,128)S(1)}, f32[4,1,256,6,64]{2,0,4,3,1:T(4,128)}, f32[4,1,256,6]{2,3,1,0:T(8,128)}, /...) while((s32[]{:T(128)}, f32[6]{0:T(128)}, ...), condition=%wide.region_23.24_spmd.clone, body=%wide.region_10.23_spmd.clone.sunk | while | flops 839958016 | bytes 16872780 | solution.py:63
  181.1 7.6 %reduce-window.74 = f32[1,6,2,128]{3,2,1,0:T(2,128)S(1)} reduce-window(f32[1,6,2,128]{3,2,1,0:T(2,128)S(1)} %bitcast.560, f32[]{:T(128)} %constant.125.clone.1..sunk), window={size=1x1x1x128 pad=0_0x0_0x0_0x0_127}, to_apply=%region_18.18 | reduce-window | flops 195072 | bytes 12292 | tf_op jit(solution)/shard_map/reduce-window.32
  192.9 9.5 %dynamic_update_slice.73 = f32[4,1,256,6,64]{2,0,4,3,1:T(4,128)} dynamic-update-slice(f32[4,1,256,6,64]{2,0,4,3,1:T(4,128)} %get-tuple-element.1127, f32[1,1,256,6,64]{2,0,4,3,1:T(1,128)S(1)} %copy.325, s32[]{:T(128)S(6)} %sub.329, s32[]{:T(128)} %constant.124.clone.1..sunk, s32[]{:T(128)} %constant.124.clone.1..sunk, s32[]{:T(128)} %constant.124.clone.1..sunk, s32[]{:T(128)} %constant.124.clone.1..sunk) | dynamic-update-slice | bytes 786436 | tf_op jit(solution)/shard_map/transpose(jvp(vmap()))/while/body/jit(dynamic_update_index_in_dim)/dynamic_update_slice | solution.py:63
  223.1 7.6 %reduce-window.74 = f32[1,6,2,128]{3,2,1,0:T(2,128)S(1)} reduce-window(f32[1,6,2,128]{3,2,1,0:T(2,128)S(1)} %bitcast.560, f32[]{:T(128)} %constant.125.clone.1..sunk), window={size=1x1x1x128 pad=0_0x0_0x0_0x0_127}, to_apply=%region_18.18 | reduce-window | flops 195072 | bytes 12292 | tf_op jit(solution)/shard_map/reduce-window.32
  234.9 9.5 %dynamic_update_slice.73 = f32[4,1,256,6,64]{2,0,4,3,1:T(4,128)} dynamic-update-slice(f32[4,1,256,6,64]{2,0,4,3,1:T(4,128)} %get-tuple-element.1127, f32[1,1,256,6,64]{2,0,4,3,1:T(1,128)S(1)} %copy.325, s32[]{:T(128)S(6)} %sub.329, s32[]{:T(128)} %constant.124.clone.1..sunk, s32[]{:T(128)} %constant.124.clone.1..sunk, s32[]{:T(128)} %constant.124.clone.1..sunk, s32[]{:T(128)} %constant.124.clone.1..sunk) | dynamic-update-slice | bytes 786436 | tf_op jit(solution)/shard_map/transpose(jvp(vmap()))/while/body/jit(dynamic_update_index_in_dim)/dynamic_update_slice | solution.py:63
  265.0 7.6 %reduce-window.74 = f32[1,6,2,128]{3,2,1,0:T(2,128)S(1)} reduce-window(f32[1,6,2,128]{3,2,1,0:T(2,128)S(1)} %bitcast.560, f32[]{:T(128)} %constant.125.clone.1..sunk), window={size=1x1x1x128 pad=0_0x0_0x0_0x0_127}, to_apply=%region_18.18 | reduce-window | flops 195072 | bytes 12292 | tf_op jit(solution)/shard_map/reduce-window.32
  276.8 9.5 %dynamic_update_slice.73 = f32[4,1,256,6,64]{2,0,4,3,1:T(4,128)} dynamic-update-slice(f32[4,1,256,6,64]{2,0,4,3,1:T(4,128)} %get-tuple-element.1127, f32[1,1,256,6,64]{2,0,4,3,1:T(1,128)S(1)} %copy.325, s32[]{:T(128)S(6)} %sub.329, s32[]{:T(128)} %constant.124.clone.1..sunk, s32[]{:T(128)} %constant.124.clone.1..sunk, s32[]{:T(128)} %constant.124.clone.1..sunk, s32[]{:T(128)} %constant.124.clone.1..sunk) | dynamic-update-slice | bytes 786436 | tf_op jit(solution)/shard_map/transpose(jvp(vmap()))/while/body/jit(dynamic_update_index_in_dim)/dynamic_update_slice | solution.py:63
  306.9 7.6 %reduce-window.74 = f32[1,6,2,128]{3,2,1,0:T(2,128)S(1)} reduce-window(f32[1,6,2,128]{3,2,1,0:T(2,128)S(1)} %bitcast.560, f32[]{:T(128)} %constant.125.clone.1..sunk), window={size=1x1x1x128 pad=0_0x0_0x0_0x0_127}, to_apply=%region_18.18 | reduce-window | flops 195072 | bytes 12292 | tf_op jit(solution)/shard_map/reduce-window.32
  318.7 9.5 %dynamic_update_slice.73 = f32[4,1,256,6,64]{2,0,4,3,1:T(4,128)} dynamic-update-slice(f32[4,1,256,6,64]{2,0,4,3,1:T(4,128)} %get-tuple-element.1127, f32[1,1,256,6,64]{2,0,4,3,1:T(1,128)S(1)} %copy.325, s32[]{:T(128)S(6)} %sub.329, s32[]{:T(128)} %constant.124.clone.1..sunk, s32[]{:T(128)} %constant.124.clone.1..sunk, s32[]{:T(128)} %constant.124.clone.1..sunk, s32[]{:T(128)} %constant.124.clone.1..sunk) | dynamic-update-slice | bytes 786436 | tf_op jit(solution)/shard_map/transpose(jvp(vmap()))/while/body/jit(dynamic_update_index_in_dim)/dynamic_update_slice | solution.py:63
  332.2 3.1 copy.224
  335.3 4.1 multiply_reduce_fusion.6
  346.6 3.7 add_add_fusion
  351.7 4.8 convolution_convert_fusion
  356.8 5.9 fusion.161
  365.6 3.3 fusion.160
  368.9 74.4 %all-reduce.33.cloned.1.call-done = (f32[1024,1536]{1,0:T(8,128)}, f32[1,1024,256]{2,1,0:T(8,128)}) async-done(((f32[1024,1536]{1,0:T(8,128)}, f32[1,1024,256]{2,1,0:T(8,128)}), (f32[1024,1536]{1,0:T(8,128)}, f32[1,1024,256]{2,1,0:T(8,128)})) %all-reduce.33.cloned.1.call-update) | async-done | bytes 7340048 | tf_op jit(solution)/shard_map/psum | solution.py:190
  453.9 6.2 fusion.121
  460.1 61.7 %all-reduce.22 = (f32[1536]{0:T(1024)}, f32[1536,6]{0,1:T(8,128)}, f32[6]{0:T(128)}, f32[6]{0:T(128)}, f32[6]{0:T(128)}, /*index=5*/f32[4,384]{1,0:T(4,128)}, f3...) all-reduce(f32[1536]{0:T(1024)S(1)} %get-tuple-element.717, ...), channel_id=1, replica_groups=mesh['dp'=16,'tensor'=8] {'dp'}, use_global_device_ids=true, to_apply=%region_28.29 | all-reduce | flops 14354 | bytes 114832 | tf_op jit(solution)/shard_map/psum | solution.py:208
  521.8 8.6 %fusion.118 = (bf16[1024,1536]{1,0:T(8,128)(2,1)}, bf16[1024,1536]{1,0:T(8,128)(2,1)}) fusion(bf16[1024,1536]{1,0:T(8,128)(2,1)} %param.20, bf16[1024,1536]{1,0:T(8,128)(2,1)} %param.35, f32[1024,1536]{1,0:T(8,128)} %get-tuple-element.856, f32[1024]{0:T(1024)S(1)} %broadcast_multiply_fusion.9, f32[1024]{0:T(1024)S(1)} %copy-done.64, ...), kind=kLoop, calls=%fused_computation.168 | loop fusion | flops 18874368 | bytes 22038528 | tf_op jit(solution)/shard_map/convert_element_type | solution.py:192
  530.3 134.3 %all-reduce.31.cloned.1.call-done = (f32[1536,384]{1,0:T(8,128)}, f32[1536,384]{1,0:T(8,128)}, f32[1536,256]{1,0:T(8,128)}, f32[384,1536]{1,0:T(8,128)}) async-done(((f32[1536,384]{1,0:T(8,128)}, f32[1536,384]{1,0:T(8,128)}, f32[1536,256]{1,0:T(8,128)}, f32[384,1536]{1,0:T(8,128)}), (f32[1536,384]{1,0:T(8,128)}, f32[1536,384]{1,0:T(8,128)}, f32[1536,256]{1,0:T(8,128)}, ...) | async-done | bytes 8650768 | tf_op jit(solution)/shard_map/psum | solution.py:208
  664.7 3.4 copy.381
  (637 shorter events, 194.5 us)
Async XLA Ops:
  7.2 99.4 %copy-start = (bf16[1536,384]{1,0:T(8,128)(2,1)S(1)}, bf16[1536,384]{1,0:T(8,128)(2,1)}, u32[]{:S(2)}) copy-start(bf16[1536,384]{1,0:T(8,128)(2,1)} %param.22) | copy-start | bytes 3538948
  7.2 436.1 %all-reduce.33.cloned.1.call-start = ((), (), s32[]{:S(2)}) async-start(), calls=%async_computation.2 | async-start | bytes 14680064 | tf_op jit(solution)/shard_map/psum | solution.py:190
  106.6 41.5 %copy-start.60 = (f32[384]{0:T(512)}, f32[384]{0:T(512)S(1)}, u32[]{:S(2)}) copy-start(f32[384]{0:T(512)S(1)} %mul.798) | copy-start | bytes 4612
  106.6 20.5 %copy-start.88 = (f32[384]{0:T(512)S(1)}, f32[384]{0:T(512)}, u32[]{:S(2)}) copy-start(f32[384]{0:T(512)} %param.33) | copy-start | bytes 4612
  127.1 21.1 %copy-start.62 = (f32[1024]{0:T(1024)}, f32[1024]{0:T(1024)S(1)}, u32[]{:S(2)}) copy-start(f32[1024]{0:T(1024)S(1)} %get-tuple-element.845) | copy-start | bytes 12292
  178.4 12.0 %copy-start.35 = (f32[256,6]{0,1:T(8,128)S(1)}, f32[256,6]{0,1:T(8,128)}, u32[]{:S(2)}) copy-start(f32[256,6]{0,1:T(8,128)} %copy-done.34) | copy-start | bytes 18436 | tf_op jit(solution)/shard_map/transpose(jvp(vmap()))/while
  192.5 10.0 %copy-start.26 = (f32[256,6]{0,1:T(8,128)S(1)}, f32[256,6]{0,1:T(8,128)}, u32[]{:S(2)}) copy-start(f32[256,6]{0,1:T(8,128)} %copy-done.25) | copy-start | bytes 18436 | tf_op jit(solution)/shard_map/transpose(jvp(vmap()))/while
  192.5 10.4 %copy-start.65 = (f32[6]{0:T(128)S(1)}, f32[6]{0:T(128)}, u32[]{:S(2)}) copy-start(f32[6]{0:T(128)} %get-tuple-element.1125) | copy-start | bytes 76 | tf_op jit(solution)/shard_map/transpose(jvp(vmap()))/while
  192.5 11.0 %copy-start.33 = (f32[4,1,256,6]{2,3,1,0:T(8,128)S(1)}, f32[4,1,256,6]{2,3,1,0:T(8,128)}, u32[]{:S(2)}) copy-start(f32[4,1,256,6]{2,3,1,0:T(8,128)} %copy-done.32) | copy-start | bytes 73732 | tf_op jit(solution)/shard_map/transpose(jvp(vmap()))/while
  192.5 10.9 %copy-start.51 = (f32[6]{0:T(128)S(1)}, f32[6]{0:T(128)}, u32[]{:S(2)}) copy-start(f32[6]{0:T(128)} %copy-done.50) | copy-start | bytes 76 | tf_op jit(solution)/shard_map/transpose(jvp(vmap()))/while
  220.3 12.1 %copy-start.35 = (f32[256,6]{0,1:T(8,128)S(1)}, f32[256,6]{0,1:T(8,128)}, u32[]{:S(2)}) copy-start(f32[256,6]{0,1:T(8,128)} %copy-done.34) | copy-start | bytes 18436 | tf_op jit(solution)/shard_map/transpose(jvp(vmap()))/while
  234.4 10.0 %copy-start.26 = (f32[256,6]{0,1:T(8,128)S(1)}, f32[256,6]{0,1:T(8,128)}, u32[]{:S(2)}) copy-start(f32[256,6]{0,1:T(8,128)} %copy-done.25) | copy-start | bytes 18436 | tf_op jit(solution)/shard_map/transpose(jvp(vmap()))/while
  234.4 10.4 %copy-start.65 = (f32[6]{0:T(128)S(1)}, f32[6]{0:T(128)}, u32[]{:S(2)}) copy-start(f32[6]{0:T(128)} %get-tuple-element.1125) | copy-start | bytes 76 | tf_op jit(solution)/shard_map/transpose(jvp(vmap()))/while
  234.5 11.0 %copy-start.33 = (f32[4,1,256,6]{2,3,1,0:T(8,128)S(1)}, f32[4,1,256,6]{2,3,1,0:T(8,128)}, u32[]{:S(2)}) copy-start(f32[4,1,256,6]{2,3,1,0:T(8,128)} %copy-done.32) | copy-start | bytes 73732 | tf_op jit(solution)/shard_map/transpose(jvp(vmap()))/while
  234.5 10.9 %copy-start.51 = (f32[6]{0:T(128)S(1)}, f32[6]{0:T(128)}, u32[]{:S(2)}) copy-start(f32[6]{0:T(128)} %copy-done.50) | copy-start | bytes 76 | tf_op jit(solution)/shard_map/transpose(jvp(vmap()))/while
  262.2 12.1 %copy-start.35 = (f32[256,6]{0,1:T(8,128)S(1)}, f32[256,6]{0,1:T(8,128)}, u32[]{:S(2)}) copy-start(f32[256,6]{0,1:T(8,128)} %copy-done.34) | copy-start | bytes 18436 | tf_op jit(solution)/shard_map/transpose(jvp(vmap()))/while
  276.4 10.0 %copy-start.26 = (f32[256,6]{0,1:T(8,128)S(1)}, f32[256,6]{0,1:T(8,128)}, u32[]{:S(2)}) copy-start(f32[256,6]{0,1:T(8,128)} %copy-done.25) | copy-start | bytes 18436 | tf_op jit(solution)/shard_map/transpose(jvp(vmap()))/while
  276.4 10.4 %copy-start.65 = (f32[6]{0:T(128)S(1)}, f32[6]{0:T(128)}, u32[]{:S(2)}) copy-start(f32[6]{0:T(128)} %get-tuple-element.1125) | copy-start | bytes 76 | tf_op jit(solution)/shard_map/transpose(jvp(vmap()))/while
  276.4 11.0 %copy-start.33 = (f32[4,1,256,6]{2,3,1,0:T(8,128)S(1)}, f32[4,1,256,6]{2,3,1,0:T(8,128)}, u32[]{:S(2)}) copy-start(f32[4,1,256,6]{2,3,1,0:T(8,128)} %copy-done.32) | copy-start | bytes 73732 | tf_op jit(solution)/shard_map/transpose(jvp(vmap()))/while
  276.4 10.9 %copy-start.51 = (f32[6]{0:T(128)S(1)}, f32[6]{0:T(128)}, u32[]{:S(2)}) copy-start(f32[6]{0:T(128)} %copy-done.50) | copy-start | bytes 76 | tf_op jit(solution)/shard_map/transpose(jvp(vmap()))/while
  304.2 12.1 %copy-start.35 = (f32[256,6]{0,1:T(8,128)S(1)}, f32[256,6]{0,1:T(8,128)}, u32[]{:S(2)}) copy-start(f32[256,6]{0,1:T(8,128)} %copy-done.34) | copy-start | bytes 18436 | tf_op jit(solution)/shard_map/transpose(jvp(vmap()))/while
  318.3 10.0 %copy-start.26 = (f32[256,6]{0,1:T(8,128)S(1)}, f32[256,6]{0,1:T(8,128)}, u32[]{:S(2)}) copy-start(f32[256,6]{0,1:T(8,128)} %copy-done.25) | copy-start | bytes 18436 | tf_op jit(solution)/shard_map/transpose(jvp(vmap()))/while
  318.3 10.4 %copy-start.65 = (f32[6]{0:T(128)S(1)}, f32[6]{0:T(128)}, u32[]{:S(2)}) copy-start(f32[6]{0:T(128)} %get-tuple-element.1125) | copy-start | bytes 76 | tf_op jit(solution)/shard_map/transpose(jvp(vmap()))/while
  318.3 11.0 %copy-start.33 = (f32[4,1,256,6]{2,3,1,0:T(8,128)S(1)}, f32[4,1,256,6]{2,3,1,0:T(8,128)}, u32[]{:S(2)}) copy-start(f32[4,1,256,6]{2,3,1,0:T(8,128)} %copy-done.32) | copy-start | bytes 73732 | tf_op jit(solution)/shard_map/transpose(jvp(vmap()))/while
  318.3 10.9 %copy-start.51 = (f32[6]{0:T(128)S(1)}, f32[6]{0:T(128)}, u32[]{:S(2)}) copy-start(f32[6]{0:T(128)} %copy-done.50) | copy-start | bytes 76 | tf_op jit(solution)/shard_map/transpose(jvp(vmap()))/while
  350.3 171.5 %all-reduce.29.cloned.1.call-start = ((), (), s32[]{:S(2)}) async-start(), calls=%async_computation | async-start | bytes 6291456 | tf_op jit(solution)/shard_map/psum | solution.py:152
  356.5 308.2 %all-reduce.31.cloned.1.call-start = ((), (), s32[]{:S(2)}) async-start(), calls=%async_computation.1 | async-start | bytes 17301504 | tf_op jit(solution)/shard_map/psum | solution.py:208
  365.6 77.7 %copy-start.10 = (f32[1024,256]{1,0:T(8,128)S(1)}, f32[1024,256]{1,0:T(8,128)}, u32[]{:S(2)}) copy-start(f32[1024,256]{1,0:T(8,128)} %copy-done.9) | copy-start | bytes 3145732
  365.6 77.7 %copy-start.17 = (f32[1,1024,256]{2,1,0:T(8,128)S(1)}, f32[1,1024,256]{2,1,0:T(8,128)}, u32[]{:S(2)}) copy-start(f32[1,1024,256]{2,1,0:T(8,128)} %get-tuple-element.814) | copy-start | bytes 3145732
  453.8 6.2 copy-start.76
  453.8 6.2 copy-start.86
  453.9 67.9 %copy-start.64 = (f32[1024]{0:T(1024)S(1)}, f32[1024]{0:T(1024)}, u32[]{:S(2)}) copy-start(f32[1024]{0:T(1024)} %get-tuple-element.842) | copy-start | bytes 12292
  (113 other events, 283.4 us)
Sparse Core Ops, SparseCore 0:
  350.4 92.8 all-reduce.32
  446.3 68.0 all-reduce.28
  519.7 144.9 all-reduce.30
where the time goes:
time: 688 us; the launch traced here: 681 us
  waiting for transfers between devices  209 us (30%)
  local copies, waits for them, and re-layouts  158 us (23%)
  matrix products  106 us (15%)
  other arithmetic  100 us (15%)
  blocking collectives  90.8 us (13%)
  between operations  14.7 us (2%)
    psum x1, waiting for transfers between devices, on_device(): lax.psum((grad_norm_gain, grad_in_gate, grad_in_value, grad_in_state, gra...  134 us
    dynamic_update_slice x24, local copies, waits for them, and re-layouts, scan_sequence(): lax.scan(jax.checkpoint(advance), start_state, shaped)  82.5 us
    psum x1, waiting for transfers between devices, on_device(): lax.psum(partial_sum, 'tensor') + dot_transposed(round_state, in_state)  74.4 us
    psum x1, blocking collectives, on_device(): lax.psum((grad_norm_gain, grad_in_gate, grad_in_value, grad_in_state, gra...  61.7 us
    another operation x36, other arithmetic  54.3 us
    dot_general x12, matrix products, advance(): jnp.einsum('ijh,jhp->ihp', mixing, block_values, precision=scan_precision)  26.8 us
    unnamed x163, local copies, waits for them, and re-layouts  23.7 us
    dot_general x5, matrix products, dot_transposed(): lax.dot_general(left, right, (((1,), (1,)), ((), ())), preferred_element_...  19.9 us
  transfers between devices with their start and end apart: 3, of which 2 were waited for; matrix products, arithmetic and copies ran while one was open for 6% of the time, Pallas kernels for 0%

commit v1 on v0

v1 whole, which is shorter than its diff:
```python
from functools import partial

import jax
import jax.numpy as jnp
from jax import lax
from jax.experimental import pallas as pl
from jax.experimental.pallas import tpu as pltpu
from jax.sharding import PartitionSpec as P

STATE = 128
CONV = 4
LEN = 1024
HEAD = 64
Q = 128
ROWS = 256
LANES = 128
HALO = 8

epsilon = 1e-05
f32 = jnp.float32
bf16 = jnp.bfloat16
exact = lax.Precision.HIGHEST
VMEM = 56 * 1024 * 1024


def mm(a, b, precision=None):
    return lax.dot_general(
        a, b, (((1,), (0,)), ((), ())), precision=precision, preferred_element_type=f32
    )


def mm_nt(a, b):
    return lax.dot_general(a, b, (((1,), (1,)), ((), ())), preferred_element_type=f32)


def mm_tn(a, b):
    return lax.dot_general(a, b, (((0,), (0,)), ((), ())), preferred_element_type=f32)


def sigmoid(v):
    return 1.0 / (1.0 + jnp.exp(-v))


def softplus(v):
    return jnp.maximum(v, 0.0) + jnp.log1p(jnp.exp(-jnp.abs(v)))


def iota(shape, axis):
    return lax.broadcasted_iota(jnp.int32, shape, axis)


def column(m, at):
    return jnp.broadcast_to(m[:, at : at + 1], (m.shape[0], LANES))


def low_half(rows):
    return iota((rows, LANES), 1) < HEAD


def expand(m, heads):
    half = low_half(m.shape[0])
    return jnp.concatenate(
        [jnp.where(half, column(m, h), column(m, h + 1)) for h in range(0, heads, 2)], axis=1
    )


def split_heads(pair):
    half = low_half(pair.shape[0])
    zero = jnp.zeros_like(pair)
    return jnp.concatenate([jnp.where(half, pair, zero), jnp.where(half, zero, pair)], axis=0)


def head_sum(m, channels_to_heads):
    high = m.astype(bf16)
    low = (m - high.astype(f32)).astype(bf16)
    return mm(high, channels_to_heads) + mm(low, channels_to_heads)


def forward_kernel(
    heads,
    tokens,
    norm_gain,
    in_gate,
    in_value,
    in_state,
    in_step,
    step_bias,
    rate,
    skip,
    value_kernel,
    value_bias,
    state_kernel,
    state_bias,
    gate_gain,
    out_weight,
    cotangent,
    normed_out,
    gate_out,
    value_out,
    value_conv_out,
    state_out,
    state_conv_out,
    step_out,
    mixed_out,
    back_out,
    memory_out,
    stats_out,
    value_buf,
    state_buf,
    memory,
):
    @pl.when(pl.program_id(0) == 0)
    def _():
        value_buf[0:HALO, :] = jnp.zeros((HALO, value_buf.shape[1]), f32)
        state_buf[0:HALO, :] = jnp.zeros((HALO, state_buf.shape[1]), f32)
        memory[...] = jnp.zeros_like(memory)

    x = tokens[...].astype(f32)
    inverse = lax.rsqrt(jnp.mean(x * x, axis=1, keepdims=True) + epsilon)
    normed = (x * inverse * norm_gain[...]).astype(bf16)
    normed_out[...] = normed
    state_pre = mm(normed, in_state[...])
    value_pre = mm(normed, in_value[...])
    step_pre = mm(normed, in_step[...]) + step_bias[...]
    gate_pre = mm(normed, in_gate[...])
    gate_out[...] = gate_pre
    value_out[...] = value_pre
    state_out[...] = state_pre
    step_out[...] = step_pre

    def conv(buf, pre, kernel, bias):
        buf[HALO:, :] = pre
        result = bias[...] + buf[HALO - 3 : HALO - 3 + ROWS, :] * kernel[0:1, :]
        for k in range(1, CONV):
            result = result + buf[HALO - 3 + k : HALO - 3 + k + ROWS, :] * kernel[k : k + 1, :]
        buf[0:HALO, :] = buf[ROWS : ROWS + HALO, :]
        return result

    value_conv = conv(value_buf, value_pre, value_kernel, value_bias)
    value_conv_out[...] = value_conv
    values = (value_conv * sigmoid(value_conv)).astype(bf16)
    state_conv = conv(state_buf, state_pre, state_kernel, state_bias)
    state_conv_out[...] = state_conv
    states = (state_conv * sigmoid(state_conv)).astype(bf16)
    step = softplus(step_pre)
    log_step = step * rate[...]

    causal = iota((Q, Q), 0) >= iota((Q, Q), 1)
    tri = jnp.where(causal, 1.0, 0.0).astype(f32)
    mixed_parts = []
    for part in range(ROWS // Q):
        rows = slice(part * Q, (part + 1) * Q)
        b = states[rows, :STATE]
        c = states[rows, STATE:]
        v = values[rows, :].astype(f32)
        dt = step[rows, :]
        decay = mm(tri, log_step[rows, :], precision=exact)
        decay_t = decay.T
        wide = expand(decay, heads)
        dt_wide = expand(dt, heads)
        grown = jnp.exp(wide)
        scaled = v * dt_wide
        scaled_low = scaled.astype(bf16)
        cb = mm_nt(c, b)
        held = memory[...]
        held_low = held.astype(bf16)
        memory_out[part] = held_low
        y = mm(c, held_low) * grown + skip[...] * v
        inside = []
        for h in range(0, heads, 2):
            blocks = []
            for at in (h, h + 1):
                gap = column(decay, at) - decay_t[at : at + 1, :]
                blocks.append((cb * jnp.exp(jnp.where(causal, gap, -1e30))).astype(bf16))
            pair = scaled_low[:, h * HEAD : (h + 2) * HEAD]
            inside.append(mm(jnp.concatenate(blocks, axis=1), split_heads(pair)))
        mixed_parts.append(y + jnp.concatenate(inside, axis=1))
        ended = (scaled * jnp.exp(wide[Q - 1 : Q, :] - wide)).astype(bf16)
        memory[...] = held * grown[Q - 1 : Q, :] + mm_tn(b, ended)

    mixed = jnp.concatenate(mixed_parts, axis=0)
    mixed_out[...] = mixed
    gated = mixed * gate_pre * sigmoid(gate_pre)
    back = mm_nt(cotangent[...], out_weight[...])
    back_out[...] = back
    squares = jnp.sum(gated * gated, axis=1, keepdims=True)
    moment = jnp.sum(back * gate_gain[...] * gated, axis=1, keepdims=True)
    lane = iota((ROWS, LANES), 1)
    both = jnp.where(lane == 0, squares, jnp.where(lane == 1, moment, 0.0))
    stats_out[...] = both.T[0:8, :]


def stats_columns(stats, inner):
    padded = jnp.concatenate([stats, jnp.zeros((LANES - 8, stats.shape[1]), f32)], axis=0).T
    scale = lax.rsqrt(padded[:, 0:1] / inner + epsilon)
    return scale, padded[:, 1:2] / inner


def out_kernel(inner, stats, gate_pre, mixed, gate_gain, out_weight, outgoing_out, part_out):
    scale, _ = stats_columns(stats[...], inner)
    pre = gate_pre[...]
    gated = mixed[...] * pre * sigmoid(pre)
    outgoing = (gated * scale * gate_gain[...]).astype(bf16)
    outgoing_out[...] = outgoing
    part_out[...] = mm(outgoing, out_weight[...]).astype(bf16)


def backward_kernel(
    heads,
    inner,
    stats,
    tokens,
    gate,
    value,
    value_conv,
    state,
    state_conv,
    step_in,
    mixed_in,
    back_in,
    memory_in,
    rate,
    skip,
    value_kernel,
    state_kernel,
    gate_gain,
    in_gate,
    in_value,
    in_state,
    in_step,
    channels_to_heads,
    part_out,
    gate_out,
    value_out,
    state_out,
    step_out,
    norm_gain_out,
    gate_gain_out,
    value_taps_out,
    state_taps_out,
    skip_out,
    steps_out,
    value_buf,
    state_buf,
    adjoint,
):
    @pl.when(pl.program_id(0) == 0)
    def _():
        value_buf[ROWS:, :] = jnp.zeros((HALO, value_buf.shape[1]), f32)
        state_buf[ROWS:, :] = jnp.zeros((HALO, state_buf.shape[1]), f32)
        adjoint[...] = jnp.zeros_like(adjoint)
        for ref in (norm_gain_out, gate_gain_out, value_taps_out, state_taps_out, skip_out, steps_out):
            ref[...] = jnp.zeros_like(ref)

    def add_row(ref, at, rows):
        ref[at : at + 1, :] += jnp.sum(rows, axis=0, keepdims=True)

    scale, moment = stats_columns(stats[...], inner)
    mixed = mixed_in[...]
    back = back_in[...]
    pre = gate[...]
    bent = sigmoid(pre)
    silu = pre * bent
    gated = mixed * silu
    add_row(gate_gain_out, 0, back * gated * scale)
    grad_gated = scale * (back * gate_gain[...]) - gated * (scale * scale * scale * moment)
    grad_mixed = grad_gated * silu
    round_gate = (grad_gated * mixed * (bent * (1.0 + pre * (1.0 - bent)))).astype(bf16)
    gate_out[...] = round_gate

    value_at = value_conv[...]
    value_bent = sigmoid(value_at)
    values = (value_at * value_bent).astype(bf16)
    state_at = state_conv[...]
    state_bent = sigmoid(state_at)
    states = (state_at * state_bent).astype(bf16)
    step_pre = step_in[...]
    step = softplus(step_pre)
    log_step = step * rate[...]

    ahead = iota((Q, Q), 1) >= iota((Q, Q), 0)
    tri = jnp.where(iota((Q, Q), 0) >= iota((Q, Q), 1), 1.0, 0.0).astype(f32)
    tri_up = jnp.where(ahead, 1.0, 0.0).astype(f32)
    tri_strict = jnp.where(iota((Q, Q), 0) > iota((Q, Q), 1), 1.0, 0.0).astype(f32)
    lane = iota((Q, LANES), 1)
    row8 = iota((8, Q), 0)
    parts = ROWS // Q
    grad_value_parts = [None] * parts
    grad_state_parts = [None] * parts
    grad_step_parts = [None] * parts
    for part in reversed(range(parts)):
        rows = slice(part * Q, (part + 1) * Q)
        b = states[rows, :STATE]
        c = states[rows, STATE:]
        v_low = values[rows, :]
        v = v_low.astype(f32)
        dt = step[rows, :]
        dy = grad_mixed[rows, :]
        dy_low = dy.astype(bf16)
        decay = mm(tri, log_step[rows, :], precision=exact)
        decay_t = decay.T
        wide = expand(decay, heads)
        dt_wide = expand(dt, heads)
        grown = jnp.exp(wide)
        to_end = jnp.exp(wide[Q - 1 : Q, :] - wide)
        held = memory_in[part]
        later = adjoint[...]
        later_low = later.astype(bf16)
        bd = mm(b, later_low)
        cs = mm(c, held)
        bc = mm_nt(b, c)
        dy_grown = dy * grown
        dy_grown_low = dy_grown.astype(bf16)
        at_end = bd * to_end
        inside = []
        grad_bc = jnp.zeros((Q, Q), f32)
        direct = jnp.zeros((Q, LANES), f32)
        row_sums = jnp.zeros((8, Q), f32)
        for h in range(0, heads, 2):
            lanes = slice(h * HEAD, (h + 2) * HEAD)
            v_split = split_heads(v_low[:, lanes])
            grad_pair = mm_nt(v_split, dy_low[:, lanes])
            blocks = []
            for at in (h, h + 1):
                gap = decay_t[at : at + 1, :] - column(decay, at)
                fall = jnp.exp(jnp.where(ahead, gap, -1e30))
                grad_fall = grad_pair[(at - h) * Q : (at - h + 1) * Q, :] * fall
                direct += jnp.where(lane == at, jnp.sum(grad_fall * bc, axis=1, keepdims=True), 0.0)
                grad_one = grad_fall * column(dt, at)
                grad_bc += grad_one
                row_sums += jnp.where(
                    row8 == at, jnp.sum(grad_one * bc, axis=0, keepdims=True), 0.0
                )
                blocks.append((bc * fall).astype(bf16))
            inside.append(mm(jnp.concatenate(blocks, axis=1), split_heads(dy_low[:, lanes])))
        grad_value_parts[part] = (
            dt_wide * (jnp.concatenate(inside, axis=1) + at_end) + skip[...] * dy
        )
        add_row(skip_out, 0, dy * v)
        grown_sum = head_sum(dy_grown * cs, channels_to_heads[...])
        end_sum = head_sum(at_end * v, channels_to_heads[...])
        constant = head_sum(
            grown[Q - 1 : Q, :] * jnp.sum(held.astype(f32) * later, axis=0, keepdims=True),
            channels_to_heads[...],
        )
        row_t = jnp.concatenate([row_sums, jnp.zeros((LANES - 8, Q), f32)], axis=0).T
        grad_log = (
            mm(tri_up, row_t - direct * dt + grown_sum, precision=exact)
            + mm(tri_strict, end_sum * dt, precision=exact)
            + constant
        )
        grad_step = direct + end_sum + rate[...] * grad_log
        grad_step = grad_step * sigmoid(step_pre[rows, :])
        grad_step_parts[part] = grad_step
        add_row(steps_out, 0, grad_step)
        add_row(steps_out, 1, dt * grad_log * rate[...])
        grad_bc_low = grad_bc.astype(bf16)
        grad_b = mm(grad_bc_low, c) + mm_nt((v * dt_wide * to_end).astype(bf16), later_low)
        grad_c = mm_tn(grad_bc_low, b) + mm_nt(dy_grown_low, held)
        grad_state_parts[part] = jnp.concatenate([grad_b, grad_c], axis=1)
        adjoint[...] = later * grown[Q - 1 : Q, :] + mm_tn(c, dy_grown_low)

    def conv_back(buf, grad, at, bent, pre, kernel, taps_out):
        buf[0:ROWS, :] = grad * (bent * (1.0 + at * (1.0 - bent)))
        result = None
        for k in range(CONV):
            moved = buf[3 - k : 3 - k + ROWS, :]
            term = moved * kernel[k : k + 1, :]
            result = term if result is None else result + term
            add_row(taps_out, k, pre * moved)
        add_row(taps_out, CONV, buf[0:ROWS, :])
        buf[ROWS:, :] = buf[0:HALO, :]
        return result.astype(bf16)

    round_value = conv_back(
        value_buf,
        jnp.concatenate(grad_value_parts, axis=0),
        value_at,
        value_bent,
        value[...],
        value_kernel,
        value_taps_out,
    )
    round_state = conv_back(
        state_buf,
        jnp.concatenate(grad_state_parts, axis=0),
        state_at,
        state_bent,
        state[...],
        state_kernel,
        state_taps_out,
    )
    round_step = jnp.concatenate(grad_step_parts, axis=0).astype(bf16)
    value_out[...] = round_value
    state_out[...] = round_state
    step_out[...] = round_step
    total = (
        mm_nt(round_gate, in_gate[...])
        + mm_nt(round_value, in_value[...])
        + mm_nt(round_state, in_state[...])
        + mm_nt(round_step, in_step[...])
    )
    part_out[...] = total.astype(bf16)
    x = tokens[...].astype(f32)
    inverse = lax.rsqrt(jnp.mean(x * x, axis=1, keepdims=True) + epsilon)
    add_row(norm_gain_out, 0, total * (x * inverse))


def whole(array):
    zeros = (0,) * array.ndim
    return pl.BlockSpec(array.shape, lambda i: zeros)


def by_rows(width, steps=None, rows=ROWS):
    if steps is None:
        return pl.BlockSpec((rows, width), lambda i: (i, 0))
    return pl.BlockSpec((rows, width), lambda i: (steps - 1 - i, 0))


def swap_core(x):
    return lax.ppermute(x, "tensor", [(i, i ^ 1) for i in range(8)])


def move_z(x, k):
    return lax.ppermute(x, "tensor", [(i, (i + 2 * k) % 8) for i in range(8)])


def pick(x, at):
    return lax.dynamic_index_in_dim(x, at, 0, keepdims=False)


def add_over_tensor(x):
    for bit in (1, 2, 4):
        x = x + lax.ppermute(x, "tensor", [(i, i ^ bit) for i in range(8)])
    return x


def scatter_over_tensor(x):
    me = lax.axis_index("tensor")
    z, core = me // 2, me % 2
    blocks = x.reshape((4, 2) + (x.shape[0] // 8,) + x.shape[1:])
    mine = lax.dynamic_index_in_dim(blocks, core, 1, keepdims=False)
    other = lax.dynamic_index_in_dim(blocks, 1 - core, 1, keepdims=False)
    both = (mine.astype(f32) + swap_core(other).astype(f32)).astype(bf16)
    total = pick(both, z).astype(f32)
    for k in (1, 2, 3):
        total = total + move_z(pick(both, (z + k) % 4), k).astype(f32)
    return total


def scatter_over_dp(x):
    got = lax.all_to_all(x, "dp", 0, 0, tiled=True)
    return jnp.sum(got.astype(f32), axis=0)


def gather_over_dp(x):
    return lax.all_to_all(jnp.broadcast_to(x[None], (lax.axis_size("dp"),) + x.shape), "dp", 0, 0, tiled=True)


def two_parts(x):
    high = x.astype(bf16)
    return high, (x - high.astype(f32)).astype(bf16)


def on_device(
    tokens,
    norm_gain,
    in_gate,
    in_value,
    in_state,
    in_step,
    step_bias,
    decay_log,
    skip_gain,
    conv_value_kernel,
    conv_value_bias,
    conv_state_kernel,
    conv_state_bias,
    gate_gain,
    out_weight,
    cotangent,
):
    features = tokens.shape[1]
    channels = in_gate.shape[1]
    heads = step_bias.shape[0]
    inner = channels * lax.axis_size("tensor")
    steps = LEN // ROWS
    parts = ROWS // Q
    dp = lax.axis_size("dp")
    me = lax.axis_index("tensor")

    pad_heads = lambda a: jnp.pad(a[None, :], ((0, 0), (0, LANES - heads)))
    step_weight = jnp.pad(in_step, ((0, 0), (0, LANES - heads)))
    rate = pad_heads(-jnp.exp(decay_log))
    skip = jnp.repeat(skip_gain, HEAD)[None, :]
    gain_row = gate_gain[None, :]
    sds = jax.ShapeDtypeStruct
    params = pltpu.CompilerParams(
        dimension_semantics=("arbitrary",), vmem_limit_bytes=VMEM
    )

    operands = (
        tokens,
        norm_gain[None, :],
        in_gate,
        in_value,
        in_state,
        step_weight,
        pad_heads(step_bias),
        rate,
        skip,
        conv_value_kernel,
        conv_value_bias[None, :],
        conv_state_kernel,
        conv_state_bias[None, :],
        gain_row,
        out_weight,
        cotangent,
    )
    (
        normed,
        gate_pre,
        value_pre,
        value_conv,
        state_pre,
        state_conv,
        step_pre,
        mixed,
        back,
        memories,
        stats,
    ) = pl.pallas_call(
        partial(forward_kernel, heads),
        grid=(steps,),
        in_specs=[by_rows(features)]
        + [whole(a) for a in operands[1:-1]]
        + [by_rows(features)],
        out_specs=[
            by_rows(features),
            by_rows(channels),
            by_rows(channels),
            by_rows(channels),
            by_rows(2 * STATE),
            by_rows(2 * STATE),
            by_rows(LANES),
            by_rows(channels),
            by_rows(channels),
            pl.BlockSpec((parts, STATE, channels), lambda i: (i, 0, 0)),
            pl.BlockSpec((8, ROWS), lambda i: (0, i)),
        ],
        out_shape=[
            sds((LEN, features), bf16),
            sds((LEN, channels), f32),
            sds((LEN, channels), f32),
            sds((LEN, channels), f32),
            sds((LEN, 2 * STATE), f32),
            sds((LEN, 2 * STATE), f32),
            sds((LEN, LANES), f32),
            sds((LEN, channels), f32),
            sds((LEN, channels), f32),
            sds((LEN // Q, STATE, channels), bf16),
            sds((8, LEN), f32),
        ],
        scratch_shapes=[
            pltpu.VMEM((ROWS + HALO, channels), f32),
            pltpu.VMEM((ROWS + HALO, 2 * STATE), f32),
            pltpu.VMEM((STATE, channels), f32),
        ],
        compiler_params=params,
        cost_estimate=pl.CostEstimate(
            flops=5_000_000_000, bytes_accessed=30_000_000, transcendentals=4_000_000
        ),
    )(*operands)

    stats = add_over_tensor(stats)

    outgoing, part = pl.pallas_call(
        partial(out_kernel, inner),
        grid=(steps,),
        in_specs=[
            pl.BlockSpec((8, ROWS), lambda i: (0, i)),
            by_rows(channels),
            by_rows(channels),
            whole(gain_row),
            whole(out_weight),
        ],
        out_specs=[by_rows(channels), by_rows(features)],
        out_shape=[sds((LEN, channels), bf16), sds((LEN, features), bf16)],
        compiler_params=params,
        cost_estimate=pl.CostEstimate(
            flops=1_200_000_000, bytes_accessed=9_000_000, transcendentals=400_000
        ),
    )(stats, gate_pre, mixed, gain_row, out_weight)

    own = lambda a: lax.dynamic_slice_in_dim(a, me * (LEN // 8), LEN // 8, 0)
    own_tokens = own(tokens).astype(f32)
    own_output = (own_tokens + scatter_over_tensor(part)).astype(bf16)
    block_output = lax.all_gather(own_output, "tensor", tiled=True)
    grad_out_weight = mm_tn(outgoing, cotangent)

    channels_to_heads = (
        jnp.arange(channels)[:, None] // HEAD == jnp.arange(LANES)[None, :]
    ).astype(bf16)
    operands = (
        stats,
        tokens,
        gate_pre,
        value_pre,
        value_conv,
        state_pre,
        state_conv,
        step_pre,
        mixed,
        back,
        memories,
        rate,
        skip,
        conv_value_kernel,
        conv_state_kernel,
        gain_row,
        in_gate,
        in_value,
        in_state,
        step_weight,
        channels_to_heads,
    )
    back_rows = partial(by_rows, steps=steps)
    row_sum = lambda rows, width: pl.BlockSpec((rows, width), lambda i: (0, 0))
    (
        grad_part,
        round_gate,
        round_value,
        round_state,
        round_step,
        norm_gain_part,
        gate_gain_part,
        value_taps,
        state_taps,
        skip_part,
        step_parts,
    ) = pl.pallas_call(
        partial(backward_kernel, heads, inner),
        grid=(steps,),
        in_specs=[
            pl.BlockSpec((8, ROWS), lambda i: (0, steps - 1 - i)),
            back_rows(features),
            back_rows(channels),
            back_rows(channels),
            back_rows(channels),
            back_rows(2 * STATE),
            back_rows(2 * STATE),
            back_rows(LANES),
            back_rows(channels),
            back_rows(channels),
            pl.BlockSpec((parts, STATE, channels), lambda i: (steps - 1 - i, 0, 0)),
        ]
        + [whole(a) for a in operands[11:]],
        out_specs=[
            back_rows(features),
            back_rows(channels),
            back_rows(channels),
            back_rows(2 * STATE),
            back_rows(LANES),
            row_sum(8, features),
            row_sum(8, channels),
            row_sum(8, channels),
            row_sum(8, 2 * STATE),
            row_sum(8, channels),
            row_sum(8, LANES),
        ],
        out_shape=[
            sds((LEN, features), bf16),
            sds((LEN, channels), bf16),
            sds((LEN, channels), bf16),
            sds((LEN, 2 * STATE), bf16),
            sds((LEN, LANES), bf16),
            sds((8, features), f32),
            sds((8, channels), f32),
            sds((8, channels), f32),
            sds((8, 2 * STATE), f32),
            sds((8, channels), f32),
            sds((8, LANES), f32),
        ],
        scratch_shapes=[
            pltpu.VMEM((ROWS + HALO, channels), f32),
            pltpu.VMEM((ROWS + HALO, 2 * STATE), f32),
            pltpu.VMEM((STATE, channels), f32),
        ],
        compiler_params=params,
        cost_estimate=pl.CostEstimate(
            flops=6_000_000_000, bytes_accessed=30_000_000, transcendentals=4_000_000
        ),
    )(*operands)

    grad_normed = scatter_over_tensor(grad_part)
    inverse = lax.rsqrt(jnp.mean(own_tokens * own_tokens, axis=1, keepdims=True) + epsilon)
    scaled = grad_normed * norm_gain
    moment = jnp.mean(scaled * own_tokens, axis=1, keepdims=True)
    own_grad = own(cotangent).astype(f32) + inverse * scaled - own_tokens * inverse**3 * moment
    grad_tokens = lax.all_gather(own_grad.astype(bf16), "tensor", tiled=True)

    grad_in_gate = mm_tn(normed, round_gate)
    grad_in_value = mm_tn(normed, round_value)
    grad_in_state = mm_tn(normed, round_state)
    grad_in_step = mm_tn(normed, round_step)[:, :heads]

    first = scatter_over_dp(
        jnp.concatenate(
            [
                grad_out_weight.astype(bf16).reshape(dp, -1, channels),
                grad_in_gate.astype(bf16).reshape(dp, -1, channels),
            ],
            axis=1,
        )
    )
    first = gather_over_dp(first.astype(bf16)).astype(f32)
    grad_out_weight, grad_in_gate = jnp.split(first, 2, axis=1)
    grad_out_weight = grad_out_weight.reshape(channels, features)
    grad_in_gate = grad_in_gate.reshape(features, channels)

    state_share = scatter_over_tensor(grad_in_state.astype(bf16))
    state_share = state_share.reshape(dp, -1, channels).astype(bf16)

    def as_rows(*arrays):
        flat = jnp.concatenate([a.reshape(-1) for a in arrays])
        return jnp.pad(flat, (0, -flat.shape[0] % channels)).reshape(-1, channels)

    head_rows = as_rows(step_parts[0, :heads], step_parts[1, :heads], skip_part[0])
    small = jnp.concatenate(
        [
            as_rows(grad_in_step),
            head_rows,
            value_taps[: CONV + 1],
            gate_gain_part[:1],
            as_rows(norm_gain_part[0], state_taps[: CONV + 1]),
        ],
        axis=0,
    )
    step_rows = features * heads // channels
    small = jnp.pad(small, ((0, 64 - small.shape[0]), (0, 0)))
    small = small.reshape(dp, -1, channels)
    small_rows = small.shape[1]
    second = scatter_over_dp(
        jnp.concatenate(
            (grad_in_value.astype(bf16).reshape(dp, -1, channels),)
            + two_parts(small)
            + (state_share,),
            axis=1,
        )
    )
    value_rows = features // dp
    state_at = value_rows + 2 * small_rows
    small = second[value_rows : value_rows + small_rows] + second[value_rows + small_rows : state_at]
    second = gather_over_dp(
        jnp.concatenate(
            (second[:value_rows].astype(bf16),)
            + two_parts(small)
            + (second[state_at:].astype(bf16),),
            axis=0,
        )
    )
    grad_in_value = second[:, :value_rows].reshape(features, channels).astype(f32)
    small = second[:, value_rows : value_rows + small_rows].astype(f32)
    small = small + second[:, value_rows + small_rows : state_at].astype(f32)
    small = small.reshape(64, channels)
    state_share = second[:, state_at:].reshape(features // 8, 2 * STATE)
    grad_in_state = lax.all_gather(state_share, "tensor", tiled=True).astype(f32)

    grad_in_step = small[:step_rows].reshape(features, heads)
    at = step_rows
    head_flat = small[at : at + 2].reshape(-1)
    grad_step_bias = head_flat[:heads]
    grad_decay_log = head_flat[heads : 2 * heads]
    grad_skip_gain = head_flat[2 * heads : 2 * heads + channels].reshape(heads, HEAD).sum(axis=1)
    at += 2
    grad_conv_value_kernel = small[at : at + CONV]
    grad_conv_value_bias = small[at + CONV]
    grad_gate_gain = small[at + CONV + 1]
    at += CONV + 2
    shared = add_over_tensor(small[at : at + 8]).reshape(-1)
    grad_norm_gain = shared[:features]
    state_flat = shared[features : features + (CONV + 1) * 2 * STATE].reshape(CONV + 1, 2 * STATE)
    return (
        block_output,
        grad_tokens,
        grad_norm_gain,
        grad_in_gate,
        grad_in_value,
        grad_in_state,
        grad_in_step,
        grad_step_bias,
        grad_decay_log,
        grad_skip_gain,
        grad_conv_value_kernel,
        grad_conv_value_bias,
        state_flat[:CONV],
        state_flat[CONV],
        grad_gate_gain,
        grad_out_weight,
    )


def solution(mesh):
    placed = (
        P("dp", None),
        P(),
        P(None, "tensor"),
        P(None, "tensor"),
        P(),
        P(None, "tensor"),
        P("tensor"),
        P("tensor"),
        P("tensor"),
        P(None, "tensor"),
        P("tensor"),
        P(),
        P(),
        P("tensor"),
        P("tensor", None),
        P("dp", None),
    )
    return jax.shard_map(
        on_device,
        mesh=mesh,
        in_specs=placed,
        out_specs=(
            P("dp", None),
            P("dp", None),
            P(),
            P(None, "tensor"),
            P(None, "tensor"),
            P(),
            P(None, "tensor"),
            P("tensor"),
            P("tensor"),
            P("tensor"),
            P(None, "tensor"),
            P("tensor"),
            P(),
            P(),
            P("tensor"),
            P("tensor", None),
        ),
        check_vma=False,
    )
```

time: 688 us -> 306 us (0.44)
  local copies, waits for them, and re-layouts: 158 us -> 44.6 us
  waiting for transfers between devices: 209 us -> 95.7 us
  matrix products: 106 us -> 14.5 us
  other arithmetic: 100 us -> 21.8 us
  blocking collectives: 90.8 us -> 13.3 us
  starting transfers between devices: 0.29 us -> 53.1 us
  Pallas kernels: 0 us -> 45 us
    psum x3 -> x0, waiting for transfers between devices: 209 us -> none  [the longest x1 134 us: on_device(): lax.psum((grad_norm_gain, grad_in_gate, grad_in_value, grad_in_state, gra...]
    dot_general x63 -> x4, matrix products: 104 us -> 12.6 us  [mm_tn(): lax.dot_general(a, b, (((0,), (0,)), ((), ())), preferred_element_type=f32)]
    psum x3 -> x0, blocking collectives: 90.8 us -> none  [the longest x1 61.7 us: on_device(): lax.psum((grad_norm_gain, grad_in_gate, grad_in_value, grad_in_state, gra...]
    dynamic_update_slice x24 -> x0, local copies, waits for them, and re-layouts: 82.5 us -> none  [scan_sequence(): lax.scan(jax.checkpoint(advance), start_state, shaped)]
    all_to_all x0 -> x4, waiting for transfers between devices: none -> 55.9 us  [the longest x2 38.1 us: scatter_over_dp(): got = lax.all_to_all(x, 'dp', 0, 0, tiled=True)]
    another operation x40 -> x1, other arithmetic: 54.4 us -> 0.01 us
    pallas_call x0 -> x3, Pallas kernels: none -> 45 us  [the longest x1 20.8 us: on_device(): pl.pallas_call(partial(backward_kernel, heads, inner), grid=(steps,), in_...]
    ppermute x0 -> x18, waiting for transfers between devices: none -> 39 us  [the longest x9 33.9 us: move_z(): return lax.ppermute(x, 'tensor', [(i, (i + 2 * k) % 8) for i in range(8)])]
  transfers between devices with their start and end apart: 3 -> 24, of which waited for: 2 -> 12; matrix products, arithmetic and copies ran while one was open for 6% -> 20% of each run, Pallas kernels for 0% -> 2%
where the time goes in v1:
time: 306 us; the launch traced here: 302 us
  waiting for transfers between devices  95.7 us (31%)
  starting transfers between devices  53.1 us (17%)
  Pallas kernels  45 us (15%)
  local copies, waits for them, and re-layouts  44.6 us (15%)
  other arithmetic  21.8 us (7%)
  matrix products  14.5 us (5%)
  between operations  14.5 us (5%)
  blocking collectives  13.3 us (4%)
    all_to_all x2, waiting for transfers between devices, scatter_over_dp(): got = lax.all_to_all(x, 'dp', 0, 0, tiled=True)  38.1 us
    ppermute x9, waiting for transfers between devices, move_z(): return lax.ppermute(x, 'tensor', [(i, (i + 2 * k) % 8) for i in range(8)])  33.9 us
    pallas_call x1, Pallas kernels, on_device(): pl.pallas_call(partial(backward_kernel, heads, inner), grid=(steps,), in_...  20.8 us
    all_to_all x2, waiting for transfers between devices, gather_over_dp(): lax.all_to_all(jnp.broadcast_to(x[None], (lax.axis_size('dp'),) + x.shape...  17.8 us
    pallas_call x1, Pallas kernels, on_device(): pl.pallas_call(partial(forward_kernel, heads), grid=(steps,), in_specs=[b...  17.8 us
    ppermute x9, starting transfers between devices, move_z(): return lax.ppermute(x, 'tensor', [(i, (i + 2 * k) % 8) for i in range(8)])  15.2 us
    all_gather x1, blocking collectives, on_device(): lax.all_gather(state_share, 'tensor', tiled=True).astype(f32)  13.3 us
    dot_general x4, matrix products, mm_tn(): lax.dot_general(a, b, (((0,), (0,)), ((), ())), preferred_element_type=f32)  12.6 us
  transfers between devices with their start and end apart: 24, of which 12 were waited for; matrix products, arithmetic and copies ran while one was open for 20% of the time, Pallas kernels for 2%

profile of v1, /device:TPU:1, one launch (start us, length us, event | category | flops | bytes accessed | tf_op | source)
XLA Modules:
  0.0 302.4 jit_solution(4181509280437136157)
XLA Ops:
  16.6 17.8 %shard_map.279 = (bf16[1024,1536]{1,0:T(8,128)(2,1)}, f32[1024,384]{1,0:T(8,128)}, f32[1024,384]{1,0:T(8,128)}, f32[1024,384]{1,0:T(8,128)}, f32[1024,256]{1,0:T...) custom-call(bf16[1024,1536]{1,0:T(8,128)(2,1)} %tokens.3, ...), custom_call_target="tpu_custom_call" | custom-call | flops 5000000000 | bytes 30000000 | tf_op jit(solution)/shard_map/pallas_call | solution.py:532
  40.7 3.4 %collective-permute-start.2 = (f32[8,1024]{1,0:T(8,128)S(1)}, f32[8,1024]{1,0:T(8,128)S(1)}, u32[]{:S(2)}, u32[]{:S(2)}) collective-permute-start(f32[8,1024]{1,0:T(8,128)S(1)} %add.176), channel_id=1, source_target_pairs={{0,4},{1,5},{2,6},{3,7},{4,0},{5,1},{6,2},{7,3},{8,12},{9,13},{10,... | collective-permute-start | bytes 98312 | tf_op jit(solution)/shard_map/ppermute | solution.py:434
  46.1 20.8 %shard_map.281 = (bf16[1024,1536]{1,0:T(8,128)(2,1)}, bf16[1024,384]{1,0:T(8,128)(2,1)}, bf16[1024,384]{1,0:T(8,128)(2,1)}, bf16[1024,256]{1,0:T(8,128)(2,1)}, b...) custom-call(f32[8,1024]{1,0:T(8,128)} %add.177.stats, ...), custom_call_target="tpu_custom_call" | custom-call | flops 6000000000 | bytes 30000000 | tf_op jit(solution)/shard_map/pallas_call | solution.py:641
  66.8 2.7 dynamic-slice_bitcast_fusion
  69.5 2.4 collective-permute-start.7
  71.9 6.4 %shard_map.280 = (bf16[1024,384]{1,0:T(8,128)(2,1)}, bf16[1024,1536]{1,0:T(8,128)(2,1)}) custom-call(f32[8,1024]{1,0:T(8,128)} %add.177.stats, f32[1024,384]{1,0:T(8,128)} %get-tuple-element.41.gate_pre.gate, f32[1024,384]{1,0:T(8,128)} %get-tuple-element.42.mixed.mixed_in, f32[1,384]{1,0:T(1,128)} %broadcast_in_dim.44.gate_gain, bf16[384,1536]{1,0:T(8,128)(2,1)} %out_weight.3), custom_call_target="tpu_custom_call" | custom-call | flops 1200000000 | bytes 9000000 | tf_op jit(solution)/shard_map/pallas_call | solution.py:577
  78.3 2.8 dynamic-slice_bitcast_fusion.1
  83.2 3.5 %collective-permute-start.10 = (bf16[128,1536]{1,0:T(8,128)(2,1)S(1)}, bf16[128,1536]{1,0:T(8,128)(2,1)S(1)}, u32[]{:S(2)}, u32[]{:S(2)}) collective-permute-start(bf16[128,1536]{1,0:T(8,128)(2,1)S(1)} %get-tuple-element.109), channel_id=1, source_target_pairs={{0,6},{1,7},{2,0},{3,1},{4,2},{5,3},{6,4},{7,5},{8,14},{9,15},{10,... | collective-permute-start | bytes 1179656 | tf_op jit(solution)/shard_map/ppermute | solution.py:425
  92.5 18.8 %collective-permute-done.10 = bf16[128,1536]{1,0:T(8,128)(2,1)S(1)} collective-permute-done((bf16[128,1536]{1,0:T(8,128)(2,1)S(1)}, bf16[128,1536]{1,0:T(8,128)(2,1)S(1)}, u32[]{:S(2)}, u32[]{:S(2)}) %collective-permute-start.10) | collective-permute-done | bytes 393248 | tf_op jit(solution)/shard_map/ppermute | solution.py:425
  111.4 3.6 %collective-permute-start.6 = (bf16[128,1536]{1,0:T(8,128)(2,1)S(1)}, bf16[128,1536]{1,0:T(8,128)(2,1)S(1)}, u32[]{:S(2)}, u32[]{:S(2)}) collective-permute-start(bf16[128,1536]{1,0:T(8,128)(2,1)S(1)} %get-tuple-element.112), channel_id=1, source_target_pairs={{0,6},{1,7},{2,0},{3,1},{4,2},{5,3},{6,4},{7,5},{8,14},{9,15},{10,... | collective-permute-start | bytes 1179656 | tf_op jit(solution)/shard_map/ppermute | solution.py:425
  116.4 5.4 %collective-permute-done.5 = bf16[128,1536]{1,0:T(8,128)(2,1)S(1)} collective-permute-done((bf16[128,1536]{1,0:T(8,128)(2,1)S(1)}, bf16[128,1536]{1,0:T(8,128)(2,1)S(1)}, u32[]{:S(2)}, u32[]{:S(2)}) %collective-permute-start.5) | collective-permute-done | bytes 393248 | tf_op jit(solution)/shard_map/ppermute | solution.py:425
  122.0 2.8 fusion.6
  133.7 2.8 collective-permute-start.11
  136.5 2.9 convolution_convert_fusion.2
  139.6 4.1 %collective-permute-start.13 = (bf16[192,256]{1,0:T(8,128)(2,1)S(1)}, bf16[192,256]{1,0:T(8,128)(2,1)S(1)}, u32[]{:S(2)}, u32[]{:S(2)}) collective-permute-start(bf16[192,256]{1,0:T(8,128)(2,1)S(1)} %get-tuple-element.116), channel_id=1, source_target_pairs={{0,4},{1,5},{2,6},{3,7},{4,0},{5,1},{6,2},{7,3},{8,12},{9,13},{10,... | collective-permute-start | bytes 294920 | tf_op jit(solution)/shard_map/ppermute | solution.py:425
  143.7 4.0 %collective-permute-done.12 = bf16[192,256]{1,0:T(8,128)(2,1)S(1)} collective-permute-done((bf16[192,256]{1,0:T(8,128)(2,1)S(1)}, bf16[192,256]{1,0:T(8,128)(2,1)S(1)}, u32[]{:S(2)}, u32[]{:S(2)}) %collective-permute-start.12) | collective-permute-done | bytes 98336 | tf_op jit(solution)/shard_map/ppermute | solution.py:425
  147.7 5.4 %collective-permute-done.13 = bf16[192,256]{1,0:T(8,128)(2,1)S(1)} collective-permute-done((bf16[192,256]{1,0:T(8,128)(2,1)S(1)}, bf16[192,256]{1,0:T(8,128)(2,1)S(1)}, u32[]{:S(2)}, u32[]{:S(2)}) %collective-permute-start.13) | collective-permute-done | bytes 98336 | tf_op jit(solution)/shard_map/ppermute | solution.py:425
  153.3 2.5 pad_maximum_fusion.1
  155.8 6.8 %all-to-all-start = ((bf16[16,112,384]{2,1,0:T(8,128)(2,1)}), bf16[16,112,384]{2,1,0:T(8,128)(2,1)}, u32[]{:S(2)}, u32[]{:S(2)}) async-start(bf16[16,112,384]{2,1,0:T(8,128)(2,1)} %pad_maximum_fusion.1), calls=%async_computation | async-start | bytes 2752512 | tf_op jit(solution)/shard_map/all_to_all | solution.py:452
  162.6 4.6 %convolution_convert_fusion.1 = bf16[384,1536]{1,0:T(8,128)(2,1)} fusion(bf16[1024,384]{1,0:T(8,128)(2,1)} %get-tuple-element.62, bf16[1024,1536]{1,0:T(8,128)(2,1)} %cotangent.1), kind=kOutput, calls=%fused_computation.5 | convolution fusion | flops 1208549376 | bytes 5111808 | tf_op jit(solution)/shard_map/dot_general | solution.py:37
  167.2 3.1 %reshape.186 = bf16[16,96,384]{2,1,0:T(8,128)(2,1)} reshape(bf16[384,1536]{1,0:T(8,128)(2,1)} %convolution_convert_fusion.1) | data formatting | bytes 2359296 | tf_op jit(solution)/shard_map/reshape | solution.py:710
  170.3 3.1 %convolution_convert_fusion = bf16[1536,384]{1,0:T(8,128)(2,1)S(1)} fusion(bf16[1024,1536]{1,0:T(8,128)(2,1)S(1)} %copy-done, bf16[1024,384]{1,0:T(8,128)(2,1)} %get-tuple-element.63), kind=kOutput, calls=%fused_computation.4 | convolution fusion | flops 1208549376 | bytes 5111808 | tf_op jit(solution)/shard_map/dot_general | solution.py:37
  175.2 6.8 %all-to-all-done = bf16[16,112,384]{2,1,0:T(8,128)(2,1)} async-done(((bf16[16,112,384]{2,1,0:T(8,128)(2,1)}), bf16[16,112,384]{2,1,0:T(8,128)(2,1)}, u32[]{:S(2)}, u32[]{:S(2)}) %all-to-all-start) | async-done | bytes 1376288 | tf_op jit(solution)/shard_map/all_to_all | solution.py:452
  182.0 5.7 %all-to-all-start.2 = ((bf16[16,192,384]{2,1,0:T(8,128)(2,1)}), bf16[16,192,384]{2,1,0:T(8,128)(2,1)S(1)}, u32[]{:S(2)}, u32[]{:S(2)}) async-start(bf16[16,192,384]{2,1,0:T(8,128)(2,1)} %pad_maximum_fusion), calls=%async_computation.2 | async-start | bytes 4718592 | tf_op jit(solution)/shard_map/all_to_all | solution.py:452
  190.1 31.3 %all-to-all-done.2 = bf16[16,192,384]{2,1,0:T(8,128)(2,1)S(1)} async-done(((bf16[16,192,384]{2,1,0:T(8,128)(2,1)}), bf16[16,192,384]{2,1,0:T(8,128)(2,1)S(1)}, u32[]{:S(2)}, u32[]{:S(2)}) %all-to-all-start.2) | async-done | bytes 2359328 | tf_op jit(solution)/shard_map/all_to_all | solution.py:452
  222.6 4.4 %all-to-all-start.1 = ((bf16[16,112,384]{2,1,0:T(8,128)(2,1)}), bf16[16,112,384]{2,1,0:T(8,128)(2,1)}, u32[]{:S(2)}, u32[]{:S(2)}) async-start(bf16[16,112,384]{2,1,0:T(8,128)(2,1)} %broadcast_in_dim.45), calls=%async_computation.1 | async-start | bytes 2752512 | tf_op jit(solution)/shard_map/all_to_all | solution.py:457
  227.3 17.8 %all-to-all-done.1 = bf16[16,112,384]{2,1,0:T(8,128)(2,1)} async-done(((bf16[16,112,384]{2,1,0:T(8,128)(2,1)}), bf16[16,112,384]{2,1,0:T(8,128)(2,1)}, u32[]{:S(2)}, u32[]{:S(2)}) %all-to-all-start.1) | async-done | bytes 1376288 | tf_op jit(solution)/shard_map/all_to_all | solution.py:457
  246.8 5.6 %all-to-all-start.3 = ((bf16[16,192,384]{2,1,0:T(8,128)(2,1)}), bf16[16,192,384]{2,1,0:T(8,128)(2,1)S(1)}, u32[]{:S(2)}, u32[]{:S(2)}) async-start(bf16[16,192,384]{2,1,0:T(8,128)(2,1)} %broadcast_in_dim.46), calls=%async_computation.3 | async-start | bytes 4718592 | tf_op jit(solution)/shard_map/all_to_all | solution.py:457
  259.8 13.3 %all_gather.11 = bf16[1536,256]{1,0:T(8,128)(2,1)S(1)} all-gather(bf16[192,256]{1,0:T(8,128)(2,1)S(1)} %reshape.189), channel_id=1, replica_groups=mesh['dp'=16,'tensor'=8] {'tensor'}, dimensions={0}, use_global_device_ids=true | all-gather | bytes 884736 | tf_op jit(solution)/shard_map/all_gather | solution.py:767
  284.0 2.8 fusion.25
  286.7 3.3 %reshape.195 = f32[384,1536]{1,0:T(8,128)} reshape(f32[16,96,384]{2,1,0:T(8,128)} %get-tuple-element.106) | data formatting | bytes 4718592 | tf_op jit(solution)/shard_map/reshape | solution.py:718
  290.0 3.9 %copy.49 = bf16[1024,1536]{1,0:T(8,128)(2,1)} copy(bf16[1024,1536]{1,0:T(8,128)(2,1)} %all-gather.3.cloned.1.call-done) | data formatting | bytes 6291456
  (138 shorter events, 63.6 us)
Async XLA Ops:
  7.2 282.8 %all-gather.3.cloned.1.call-start = ((), (), s32[]{:S(2)}) async-start(), calls=%async_computation.4 | async-start | bytes 3538944 | tf_op jit(solution)/shard_map/all_gather | solution.py:598
  34.4 2.6 collective-permute-start
  37.7 3.0 %collective-permute-start.1 = (f32[8,1024]{1,0:T(8,128)S(1)}, f32[8,1024]{1,0:T(8,128)S(1)}, u32[]{:S(2)}, u32[]{:S(2)}) collective-permute-start(f32[8,1024]{1,0:T(8,128)S(1)} %add.175), channel_id=1, source_target_pairs={{0,2},{1,3},{2,0},{3,1},{4,6},{5,7},{6,4},{7,5},{8,10},{9,11},{10,... | collective-permute-start | bytes 98312 | tf_op jit(solution)/shard_map/ppermute | solution.py:434
  40.7 4.7 %collective-permute-start.2 = (f32[8,1024]{1,0:T(8,128)S(1)}, f32[8,1024]{1,0:T(8,128)S(1)}, u32[]{:S(2)}, u32[]{:S(2)}) collective-permute-start(f32[8,1024]{1,0:T(8,128)S(1)} %add.176), channel_id=1, source_target_pairs={{0,4},{1,5},{2,6},{3,7},{4,0},{5,1},{6,2},{7,3},{8,12},{9,13},{10,... | collective-permute-start | bytes 98312 | tf_op jit(solution)/shard_map/ppermute | solution.py:434
  69.5 11.6 %collective-permute-start.7 = (bf16[4,128,1536]{2,1,0:T(8,128)(2,1)}, bf16[4,128,1536]{2,1,0:T(8,128)(2,1)}, u32[]{:S(2)}, u32[]{:S(2)}) collective-permute-start(bf16[4,128,1536]{2,1,0:T(8,128)(2,1)} %dynamic-slice_bitcast_fusion), channel_id=1, source_target_pairs={{0,1},{1,0},{2,3},{3,2},{4,5},{5,4},{6,7},{7,6},{8,9},{9,8},{10,11... | collective-permute-start | bytes 4718600 | tf_op jit(solution)/shard_map/ppermute | solution.py:421
  81.1 6.9 %collective-permute-start.3 = (bf16[4,128,1536]{2,1,0:T(8,128)(2,1)}, bf16[4,128,1536]{2,1,0:T(8,128)(2,1)}, u32[]{:S(2)}, u32[]{:S(2)}) collective-permute-start(bf16[4,128,1536]{2,1,0:T(8,128)(2,1)} %dynamic-slice_bitcast_fusion.1), channel_id=1, source_target_pairs={{0,1},{1,0},{2,3},{3,2},{4,5},{5,4},{6,7},{7,6},{8,9},{9,8},{10,11... | collective-permute-start | bytes 4718600 | tf_op jit(solution)/shard_map/ppermute | solution.py:421
  81.1 6.9 %copy-start.3 = (bf16[1024,1536]{1,0:T(8,128)(2,1)S(1)}, bf16[1024,1536]{1,0:T(8,128)(2,1)}, u32[]{:S(2)}) copy-start(bf16[1024,1536]{1,0:T(8,128)(2,1)} %get-tuple-element.43) | copy-start | bytes 9437188
  83.2 28.2 %collective-permute-start.10 = (bf16[128,1536]{1,0:T(8,128)(2,1)S(1)}, bf16[128,1536]{1,0:T(8,128)(2,1)S(1)}, u32[]{:S(2)}, u32[]{:S(2)}) collective-permute-start(bf16[128,1536]{1,0:T(8,128)(2,1)S(1)} %get-tuple-element.109), channel_id=1, source_target_pairs={{0,6},{1,7},{2,0},{3,1},{4,2},{5,3},{6,4},{7,5},{8,14},{9,15},{10,... | collective-permute-start | bytes 1179656 | tf_op jit(solution)/shard_map/ppermute | solution.py:425
  86.7 28.3 %collective-permute-start.8 = (bf16[128,1536]{1,0:T(8,128)(2,1)S(1)}, bf16[128,1536]{1,0:T(8,128)(2,1)S(1)}, u32[]{:S(2)}, u32[]{:S(2)}) collective-permute-start(bf16[128,1536]{1,0:T(8,128)(2,1)S(1)} %get-tuple-element.108), channel_id=1, source_target_pairs={{0,2},{1,3},{2,4},{3,5},{4,6},{5,7},{6,0},{7,1},{8,10},{9,11},{10,... | collective-permute-start | bytes 1179656 | tf_op jit(solution)/shard_map/ppermute | solution.py:425
  86.7 28.3 %collective-permute-start.9 = (bf16[128,1536]{1,0:T(8,128)(2,1)S(1)}, bf16[128,1536]{1,0:T(8,128)(2,1)S(1)}, u32[]{:S(2)}, u32[]{:S(2)}) collective-permute-start(bf16[128,1536]{1,0:T(8,128)(2,1)S(1)} %get-tuple-element.110), channel_id=1, source_target_pairs={{0,4},{1,5},{2,6},{3,7},{4,0},{5,1},{6,2},{7,3},{8,12},{9,13},{10,... | collective-permute-start | bytes 1179656 | tf_op jit(solution)/shard_map/ppermute | solution.py:425
  89.8 25.1 %copy-start.7 = (f32[1536]{0:T(1024)S(1)}, f32[1536]{0:T(1024)}, u32[]{:S(2)}) copy-start(f32[1536]{0:T(1024)} %param.17) | copy-start | bytes 18436
  89.9 26.4 %collective-permute-start.4 = (bf16[128,1536]{1,0:T(8,128)(2,1)S(1)}, bf16[128,1536]{1,0:T(8,128)(2,1)S(1)}, u32[]{:S(2)}, u32[]{:S(2)}) collective-permute-start(bf16[128,1536]{1,0:T(8,128)(2,1)S(1)} %get-tuple-element.111), channel_id=1, source_target_pairs={{0,2},{1,3},{2,4},{3,5},{4,6},{5,7},{6,0},{7,1},{8,10},{9,11},{10,... | collective-permute-start | bytes 1179656 | tf_op jit(solution)/shard_map/ppermute | solution.py:425
  91.9 29.8 %collective-permute-start.5 = (bf16[128,1536]{1,0:T(8,128)(2,1)S(1)}, bf16[128,1536]{1,0:T(8,128)(2,1)S(1)}, u32[]{:S(2)}, u32[]{:S(2)}) collective-permute-start(bf16[128,1536]{1,0:T(8,128)(2,1)S(1)} %get-tuple-element.113), channel_id=1, source_target_pairs={{0,4},{1,5},{2,6},{3,7},{4,0},{5,1},{6,2},{7,3},{8,12},{9,13},{10,... | collective-permute-start | bytes 1179656 | tf_op jit(solution)/shard_map/ppermute | solution.py:425
  111.4 10.6 %collective-permute-start.6 = (bf16[128,1536]{1,0:T(8,128)(2,1)S(1)}, bf16[128,1536]{1,0:T(8,128)(2,1)S(1)}, u32[]{:S(2)}, u32[]{:S(2)}) collective-permute-start(bf16[128,1536]{1,0:T(8,128)(2,1)S(1)} %get-tuple-element.112), channel_id=1, source_target_pairs={{0,6},{1,7},{2,0},{3,1},{4,2},{5,3},{6,4},{7,5},{8,14},{9,15},{10,... | collective-permute-start | bytes 1179656 | tf_op jit(solution)/shard_map/ppermute | solution.py:425
  122.0 4.4 %copy-start.9 = (f32[8,256]{1,0:T(8,128)S(1)}, f32[8,256]{1,0:T(8,128)}, u32[]{:S(2)}) copy-start(f32[8,256]{1,0:T(8,128)} %get-tuple-element.60) | copy-start | bytes 24580
  122.0 5.3 %copy-start = (bf16[1024,1536]{1,0:T(8,128)(2,1)S(1)}, bf16[1024,1536]{1,0:T(8,128)(2,1)}, u32[]{:S(2)}) copy-start(bf16[1024,1536]{1,0:T(8,128)(2,1)} %get-tuple-element.52) | copy-start | bytes 9437188
  122.0 5.3 %copy-start.6 = (bf16[1024,128]{1,0:T(8,128)(2,1)S(1)}, bf16[1024,128]{1,0:T(8,128)(2,1)}, u32[]{:S(2)}) copy-start(bf16[1024,128]{1,0:T(8,128)(2,1)} %get-tuple-element.54) | copy-start | bytes 786436
  127.3 4.1 %copy-start.8 = (f32[8,384]{1,0:T(8,128)S(1)}, f32[8,384]{1,0:T(8,128)}, u32[]{:S(2)}) copy-start(f32[8,384]{1,0:T(8,128)} %get-tuple-element.57) | copy-start | bytes 36868
  131.5 5.0 %copy-start.10 = (bf16[1024,384]{1,0:T(8,128)(2,1)S(1)}, bf16[1024,384]{1,0:T(8,128)(2,1)}, u32[]{:S(2)}) copy-start(bf16[1024,384]{1,0:T(8,128)(2,1)} %get-tuple-element.53) | copy-start | bytes 2359300
  133.7 5.7 %collective-permute-start.11 = (bf16[4,192,256]{2,1,0:T(8,128)(2,1)S(1)}, bf16[4,192,256]{2,1,0:T(8,128)(2,1)S(1)}, u32[]{:S(2)}, u32[]{:S(2)}) collective-permute-start(bf16[4,192,256]{2,1,0:T(8,128)(2,1)S(1)} %dynamic-slice_bitcast_fusion.2), channel_id=1, source_target_pairs={{0,1},{1,0},{2,3},{3,2},{4,5},{5,4},{6,7},{7,6},{8,9},{9,8},{10,11... | collective-permute-start | bytes 1179656 | tf_op jit(solution)/shard_map/ppermute | solution.py:421
  139.5 8.2 %collective-permute-start.12 = (bf16[192,256]{1,0:T(8,128)(2,1)S(1)}, bf16[192,256]{1,0:T(8,128)(2,1)S(1)}, u32[]{:S(2)}, u32[]{:S(2)}) collective-permute-start(bf16[192,256]{1,0:T(8,128)(2,1)S(1)} %get-tuple-element.114), channel_id=1, source_target_pairs={{0,2},{1,3},{2,4},{3,5},{4,6},{5,7},{6,0},{7,1},{8,10},{9,11},{10,... | collective-permute-start | bytes 294920 | tf_op jit(solution)/shard_map/ppermute | solution.py:425
  139.6 13.6 %collective-permute-start.13 = (bf16[192,256]{1,0:T(8,128)(2,1)S(1)}, bf16[192,256]{1,0:T(8,128)(2,1)S(1)}, u32[]{:S(2)}, u32[]{:S(2)}) collective-permute-start(bf16[192,256]{1,0:T(8,128)(2,1)S(1)} %get-tuple-element.116), channel_id=1, source_target_pairs={{0,4},{1,5},{2,6},{3,7},{4,0},{5,1},{6,2},{7,3},{8,12},{9,13},{10,... | collective-permute-start | bytes 294920 | tf_op jit(solution)/shard_map/ppermute | solution.py:425
  143.7 9.5 %collective-permute-start.14 = (bf16[192,256]{1,0:T(8,128)(2,1)S(1)}, bf16[192,256]{1,0:T(8,128)(2,1)S(1)}, u32[]{:S(2)}, u32[]{:S(2)}) collective-permute-start(bf16[192,256]{1,0:T(8,128)(2,1)S(1)} %get-tuple-element.115), channel_id=1, source_target_pairs={{0,6},{1,7},{2,0},{3,1},{4,2},{5,3},{6,4},{7,5},{8,14},{9,15},{10,... | collective-permute-start | bytes 294920 | tf_op jit(solution)/shard_map/ppermute | solution.py:425
  155.8 26.1 %all-to-all-start = ((bf16[16,112,384]{2,1,0:T(8,128)(2,1)}), bf16[16,112,384]{2,1,0:T(8,128)(2,1)}, u32[]{:S(2)}, u32[]{:S(2)}) async-start(bf16[16,112,384]{2,1,0:T(8,128)(2,1)} %pad_maximum_fusion.1), calls=%async_computation | async-start | bytes 2752512 | tf_op jit(solution)/shard_map/all_to_all | solution.py:452
  182.0 39.4 %all-to-all-start.2 = ((bf16[16,192,384]{2,1,0:T(8,128)(2,1)}), bf16[16,192,384]{2,1,0:T(8,128)(2,1)S(1)}, u32[]{:S(2)}, u32[]{:S(2)}) async-start(bf16[16,192,384]{2,1,0:T(8,128)(2,1)} %pad_maximum_fusion), calls=%async_computation.2 | async-start | bytes 4718592 | tf_op jit(solution)/shard_map/all_to_all | solution.py:452
  187.7 102.3 %all-gather.5.cloned.1.call-start = ((), (), s32[]{:S(2)}) async-start(), calls=%async_computation.5 | async-start | bytes 3538944 | tf_op jit(solution)/shard_map/all_gather | solution.py:700
  222.6 22.5 %all-to-all-start.1 = ((bf16[16,112,384]{2,1,0:T(8,128)(2,1)}), bf16[16,112,384]{2,1,0:T(8,128)(2,1)}, u32[]{:S(2)}, u32[]{:S(2)}) async-start(bf16[16,112,384]{2,1,0:T(8,128)(2,1)} %broadcast_in_dim.45), calls=%async_computation.1 | async-start | bytes 2752512 | tf_op jit(solution)/shard_map/all_to_all | solution.py:457
  246.8 37.2 %all-to-all-start.3 = ((bf16[16,192,384]{2,1,0:T(8,128)(2,1)}), bf16[16,192,384]{2,1,0:T(8,128)(2,1)S(1)}, u32[]{:S(2)}, u32[]{:S(2)}) async-start(bf16[16,192,384]{2,1,0:T(8,128)(2,1)} %broadcast_in_dim.46), calls=%async_computation.3 | async-start | bytes 4718592 | tf_op jit(solution)/shard_map/all_to_all | solution.py:457
  254.4 23.5 %copy-start.5 = (f32[16,4,384]{2,1,0:T(4,128)}, f32[16,4,384]{2,1,0:T(4,128)S(1)}, u32[]{:S(2)}) copy-start(f32[16,4,384]{2,1,0:T(4,128)S(1)} %convert_add_fusion.7) | copy-start | bytes 294916
  254.4 18.7 %collective-permute-start.15 = (f32[8,384]{1,0:T(8,128)S(1)}, f32[8,384]{1,0:T(8,128)S(1)}, u32[]{:S(2)}, u32[]{:S(2)}) collective-permute-start(f32[8,384]{1,0:T(8,128)S(1)} %slice.117), channel_id=1, source_target_pairs={{0,1},{1,0},{2,3},{3,2},{4,5},{5,4},{6,7},{7,6},{8,9},{9,8},{10,11... | collective-permute-start | bytes 36872 | tf_op jit(solution)/shard_map/ppermute | solution.py:434
  273.2 2.9 collective-permute-start.16
  276.1 6.1 %collective-permute-start.17 = (f32[8,384]{1,0:T(8,128)S(1)}, f32[8,384]{1,0:T(8,128)S(1)}, u32[]{:S(2)}, u32[]{:S(2)}) collective-permute-start(f32[8,384]{1,0:T(8,128)S(1)} %add.210), channel_id=1, source_target_pairs={{0,4},{1,5},{2,6},{3,7},{4,0},{5,1},{6,2},{7,3},{8,12},{9,13},{10,... | collective-permute-start | bytes 36872 | tf_op jit(solution)/shard_map/ppermute | solution.py:434
  (4 other events, 11.7 us)
Sparse Core Ops, SparseCore 0:
  124.9 36.2 all-gather.2
  190.8 28.1 all-gather.4

commit v2 on v1

v2 whole, which is shorter than its diff:
```python
import math
from functools import partial

import jax
import jax.numpy as jnp
from jax import lax
from jax.experimental import pallas as pl
from jax.experimental.pallas import tpu as pltpu
from jax.sharding import PartitionSpec as P

STATE = 128
CONV = 4
LEN = 1024
HEAD = 64
Q = 128
ROWS = 256
LANES = 128
HALO = 8
LOCAL = 32
SHARED = 16

epsilon = 1e-05
f32 = jnp.float32
bf16 = jnp.bfloat16
exact = lax.Precision.HIGHEST
VMEM = 60 * 1024 * 1024


def mm(a, b, precision=None):
    return lax.dot_general(
        a, b, (((1,), (0,)), ((), ())), precision=precision, preferred_element_type=f32
    )


def mm_nt(a, b):
    return lax.dot_general(a, b, (((1,), (1,)), ((), ())), preferred_element_type=f32)


def mm_tn(a, b):
    return lax.dot_general(a, b, (((0,), (0,)), ((), ())), preferred_element_type=f32)


def sigmoid(v):
    return 1.0 / (1.0 + jnp.exp(-v))


def softplus(v):
    return jnp.maximum(v, 0.0) + jnp.log1p(jnp.exp(-jnp.abs(v)))


def iota(shape, axis):
    return lax.broadcasted_iota(jnp.int32, shape, axis)


def column(m, at):
    return jnp.broadcast_to(m[:, at : at + 1], (m.shape[0], LANES))


def low_half(rows):
    return iota((rows, LANES), 1) < HEAD


def expand(m, heads):
    half = low_half(m.shape[0])
    return jnp.concatenate(
        [jnp.where(half, column(m, h), column(m, h + 1)) for h in range(0, heads, 2)], axis=1
    )


def split_heads(pair):
    half = low_half(pair.shape[0])
    zero = jnp.zeros_like(pair)
    return jnp.concatenate([jnp.where(half, pair, zero), jnp.where(half, zero, pair)], axis=0)


def head_sum(m, channels_to_heads):
    high = m.astype(bf16)
    low = (m - high.astype(f32)).astype(bf16)
    return mm(high, channels_to_heads) + mm(low, channels_to_heads)


def head_row(scalars, heads):
    lane = iota((1, LANES), 1)
    row = jnp.zeros((1, LANES), f32)
    for h in range(heads):
        row = jnp.where(lane == h, scalars[h], row)
    return row


def rate_row(decay_log, heads):
    return jnp.where(iota((1, LANES), 1) < heads, -jnp.exp(head_row(decay_log, heads)), 0.0)


def channel_row(scalars, heads):
    half = low_half(1)
    return jnp.concatenate(
        [jnp.where(half, scalars[h], scalars[h + 1]) for h in range(0, heads, 2)], axis=1
    )


def all_lanes(rows):
    below = jnp.zeros((LANES - rows.shape[0], rows.shape[1]), rows.dtype)
    return jnp.concatenate([rows, below], axis=0)


def row_of(ref):
    return ref[...].reshape(1, ref.shape[0])


def forward_kernel(
    heads,
    tokens,
    norm_gain,
    in_gate,
    in_value,
    in_state,
    in_step,
    step_bias,
    decay_log,
    skip_gain,
    value_kernel,
    value_bias,
    state_kernel,
    state_bias,
    gate_gain,
    out_weight,
    cotangent,
    normed_out,
    gate_out,
    value_out,
    value_conv_out,
    state_out,
    state_conv_out,
    step_out,
    mixed_out,
    back_out,
    part_out,
    memory_out,
    stats_out,
    value_buf,
    state_buf,
    memory,
):
    @pl.when(pl.program_id(0) == 0)
    def _():
        value_buf[0:HALO, :] = jnp.zeros((HALO, value_buf.shape[1]), f32)
        state_buf[0:HALO, :] = jnp.zeros((HALO, state_buf.shape[1]), f32)
        memory[...] = jnp.zeros_like(memory)

    x = tokens[...].astype(f32)
    inverse = lax.rsqrt(jnp.mean(x * x, axis=1, keepdims=True) + epsilon)
    normed = (x * inverse * row_of(norm_gain)).astype(bf16)
    normed_out[...] = normed
    state_pre = mm(normed, in_state[...])
    value_pre = mm(normed, in_value[...])
    step_pre = mm_nt(normed, all_lanes(in_step[...])) + head_row(step_bias, heads)
    gate_pre = mm(normed, in_gate[...])
    gate_out[...] = gate_pre
    value_out[...] = value_pre
    state_out[...] = state_pre
    step_out[...] = step_pre

    def conv(buf, pre, kernel, bias):
        buf[HALO:, :] = pre
        result = row_of(bias) + buf[HALO - 3 : HALO - 3 + ROWS, :] * kernel[0:1, :]
        for k in range(1, CONV):
            result = result + buf[HALO - 3 + k : HALO - 3 + k + ROWS, :] * kernel[k : k + 1, :]
        buf[0:HALO, :] = buf[ROWS : ROWS + HALO, :]
        return result

    value_conv = conv(value_buf, value_pre, value_kernel, value_bias)
    value_conv_out[...] = value_conv
    values = (value_conv * sigmoid(value_conv)).astype(bf16)
    state_conv = conv(state_buf, state_pre, state_kernel, state_bias)
    state_conv_out[...] = state_conv
    states = (state_conv * sigmoid(state_conv)).astype(bf16)
    step = softplus(step_pre)
    log_step = step * rate_row(decay_log, heads)
    skip = channel_row(skip_gain, heads)

    causal = iota((Q, Q), 0) >= iota((Q, Q), 1)
    tri = jnp.where(causal, 1.0, 0.0).astype(f32)
    mixed_parts = []
    for part in range(ROWS // Q):
        rows = slice(part * Q, (part + 1) * Q)
        b = states[rows, :STATE]
        c = states[rows, STATE:]
        v = values[rows, :].astype(f32)
        dt = step[rows, :]
        decay = mm(tri, log_step[rows, :], precision=exact)
        decay_t = decay.T
        wide = expand(decay, heads)
        dt_wide = expand(dt, heads)
        grown = jnp.exp(wide)
        scaled = v * dt_wide
        scaled_low = scaled.astype(bf16)
        cb = mm_nt(c, b)
        held = memory[...]
        held_low = held.astype(bf16)
        memory_out[part] = held_low
        y = mm(c, held_low) * grown + skip * v
        inside = []
        for h in range(0, heads, 2):
            blocks = []
            for at in (h, h + 1):
                gap = column(decay, at) - decay_t[at : at + 1, :]
                blocks.append((cb * jnp.exp(jnp.where(causal, gap, -1e30))).astype(bf16))
            pair = scaled_low[:, h * HEAD : (h + 2) * HEAD]
            inside.append(mm(jnp.concatenate(blocks, axis=1), split_heads(pair)))
        mixed_parts.append(y + jnp.concatenate(inside, axis=1))
        ended = (scaled * jnp.exp(wide[Q - 1 : Q, :] - wide)).astype(bf16)
        memory[...] = held * grown[Q - 1 : Q, :] + mm_tn(b, ended)

    mixed = jnp.concatenate(mixed_parts, axis=0)
    mixed_out[...] = mixed
    gated = mixed * gate_pre * sigmoid(gate_pre)
    back = mm_nt(cotangent[...], out_weight[...])
    back_out[...] = back
    gained = gated * row_of(gate_gain)
    part_out[...] = mm(gained.astype(bf16), out_weight[...]).astype(bf16)
    squares = jnp.sum(gated * gated, axis=1, keepdims=True)
    moment = jnp.sum(back * gained, axis=1, keepdims=True)
    lane = iota((ROWS, LANES), 1)
    both = jnp.where(lane == 0, squares, jnp.where(lane == 1, moment, 0.0))
    stats_out[...] = both.T[0:8, :]


def stats_columns(stats, inner):
    padded = jnp.concatenate([stats, jnp.zeros((LANES - 8, stats.shape[1]), f32)], axis=0).T
    scale = lax.rsqrt(padded[:, 0:1] / inner + epsilon)
    return scale, padded[:, 1:2] / inner


def add_row(ref, at, rows):
    ref[at : at + 1, :] += jnp.sum(rows, axis=0, keepdims=True)


def backward_kernel(
    heads,
    inner,
    steps,
    side,
    place,
    stats,
    normed,
    cotangent,
    gate,
    mixed_in,
    back_in,
    value,
    value_conv,
    state,
    state_conv,
    step_in,
    memory_in,
    gate_gain,
    decay_log,
    skip_gain,
    value_kernel,
    state_kernel,
    gate_out,
    value_out,
    state_out,
    step_out,
    *refs,
):
    pieces_out = refs[:side]
    (
        value_buf,
        state_buf,
        adjoint,
        weight_total,
        out_total,
        step_total,
        gate_gain_out,
        value_taps_out,
        state_taps_out,
        skip_out,
        steps_out,
        local_rows,
        shared_rows,
        slabs,
    ) = refs[side:]

    @pl.when(pl.program_id(0) == 0)
    def _():
        value_buf[ROWS:, :] = jnp.zeros((HALO, value_buf.shape[1]), f32)
        state_buf[ROWS:, :] = jnp.zeros((HALO, state_buf.shape[1]), f32)
        adjoint[...] = jnp.zeros_like(adjoint)
        for ref in (
            weight_total,
            out_total,
            step_total,
            gate_gain_out,
            value_taps_out,
            state_taps_out,
            skip_out,
            steps_out,
        ):
            ref[...] = jnp.zeros_like(ref)

    scale, moment = stats_columns(stats[...], inner)
    mixed = mixed_in[...]
    back = back_in[...]
    pre = gate[...]
    bent = sigmoid(pre)
    silu = pre * bent
    gated = mixed * silu
    scaled = gated * scale
    gain = row_of(gate_gain)
    add_row(gate_gain_out, 0, back * scaled)
    grad_gated = scale * (back * gain) - scaled * (scale * scale * moment)
    grad_mixed = grad_gated * silu
    round_gate = (grad_gated * mixed * (bent * (1.0 + pre * (1.0 - bent)))).astype(bf16)
    gate_out[...] = round_gate
    outgoing = (scaled * gain).astype(bf16)
    width = out_total.shape[2]
    for x in range(side):
        out_total[x] += mm_tn(outgoing, cotangent[:, x * width : (x + 1) * width])

    value_at = value_conv[...]
    value_bent = sigmoid(value_at)
    values = (value_at * value_bent).astype(bf16)
    state_at = state_conv[...]
    state_bent = sigmoid(state_at)
    states = (state_at * state_bent).astype(bf16)
    step_pre = step_in[...]
    step = softplus(step_pre)
    rate = rate_row(decay_log, heads)
    skip = channel_row(skip_gain, heads)
    log_step = step * rate

    ahead = iota((Q, Q), 1) >= iota((Q, Q), 0)
    tri = jnp.where(iota((Q, Q), 0) >= iota((Q, Q), 1), 1.0, 0.0).astype(f32)
    tri_up = jnp.where(ahead, 1.0, 0.0).astype(f32)
    tri_strict = jnp.where(iota((Q, Q), 0) > iota((Q, Q), 1), 1.0, 0.0).astype(f32)
    lane = iota((Q, LANES), 1)
    row8 = iota((8, Q), 0)
    channels = heads * HEAD
    to_heads = jnp.where(
        lax.shift_right_logical(iota((channels, LANES), 0), 6) == iota((channels, LANES), 1), 1.0, 0.0
    ).astype(bf16)
    parts = ROWS // Q
    grad_value_parts = [None] * parts
    grad_state_parts = [None] * parts
    grad_step_parts = [None] * parts
    for part in reversed(range(parts)):
        rows = slice(part * Q, (part + 1) * Q)
        b = states[rows, :STATE]
        c = states[rows, STATE:]
        v_low = values[rows, :]
        v = v_low.astype(f32)
        dt = step[rows, :]
        dy = grad_mixed[rows, :]
        dy_low = dy.astype(bf16)
        decay = mm(tri, log_step[rows, :], precision=exact)
        decay_t = decay.T
        wide = expand(decay, heads)
        dt_wide = expand(dt, heads)
        grown = jnp.exp(wide)
        to_end = jnp.exp(wide[Q - 1 : Q, :] - wide)
        held = memory_in[part]
        later = adjoint[...]
        later_low = later.astype(bf16)
        bd = mm(b, later_low)
        cs = mm(c, held)
        bc = mm_nt(b, c)
        dy_grown = dy * grown
        dy_grown_low = dy_grown.astype(bf16)
        at_end = bd * to_end
        inside = []
        grad_bc = jnp.zeros((Q, Q), f32)
        direct = jnp.zeros((Q, LANES), f32)
        row_sums = jnp.zeros((8, Q), f32)
        for h in range(0, heads, 2):
            lanes = slice(h * HEAD, (h + 2) * HEAD)
            v_split = split_heads(v_low[:, lanes])
            grad_pair = mm_nt(v_split, dy_low[:, lanes])
            blocks = []
            for at in (h, h + 1):
                gap = decay_t[at : at + 1, :] - column(decay, at)
                fall = jnp.exp(jnp.where(ahead, gap, -1e30))
                grad_fall = grad_pair[(at - h) * Q : (at - h + 1) * Q, :] * fall
                direct += jnp.where(lane == at, jnp.sum(grad_fall * bc, axis=1, keepdims=True), 0.0)
                grad_one = grad_fall * column(dt, at)
                grad_bc += grad_one
                row_sums += jnp.where(
                    row8 == at, jnp.sum(grad_one * bc, axis=0, keepdims=True), 0.0
                )
                blocks.append((bc * fall).astype(bf16))
            inside.append(mm(jnp.concatenate(blocks, axis=1), split_heads(dy_low[:, lanes])))
        grad_value_parts[part] = dt_wide * (jnp.concatenate(inside, axis=1) + at_end) + skip * dy
        add_row(skip_out, 0, dy * v)
        grown_sum = head_sum(dy_grown * cs, to_heads)
        end_sum = head_sum(at_end * v, to_heads)
        constant = head_sum(
            grown[Q - 1 : Q, :] * jnp.sum(held.astype(f32) * later, axis=0, keepdims=True), to_heads
        )
        row_t = jnp.concatenate([row_sums, jnp.zeros((LANES - 8, Q), f32)], axis=0).T
        grad_log = (
            mm(tri_up, row_t - direct * dt + grown_sum, precision=exact)
            + mm(tri_strict, end_sum * dt, precision=exact)
            + constant
        )
        grad_step = direct + end_sum + rate * grad_log
        grad_step = grad_step * sigmoid(step_pre[rows, :])
        grad_step_parts[part] = grad_step
        add_row(steps_out, 0, grad_step)
        add_row(steps_out, 1, dt * grad_log * rate)
        grad_bc_low = grad_bc.astype(bf16)
        grad_b = mm(grad_bc_low, c) + mm_nt((v * dt_wide * to_end).astype(bf16), later_low)
        grad_c = mm_tn(grad_bc_low, b) + mm_nt(dy_grown_low, held)
        grad_state_parts[part] = jnp.concatenate([grad_b, grad_c], axis=1)
        adjoint[...] = later * grown[Q - 1 : Q, :] + mm_tn(c, dy_grown_low)

    def conv_back(buf, grad, at, bent, pre, kernel, taps_out):
        buf[0:ROWS, :] = grad * (bent * (1.0 + at * (1.0 - bent)))
        result = None
        for k in range(CONV):
            moved = buf[3 - k : 3 - k + ROWS, :]
            term = moved * kernel[k : k + 1, :]
            result = term if result is None else result + term
            add_row(taps_out, k, pre * moved)
        add_row(taps_out, CONV, buf[0:ROWS, :])
        buf[ROWS:, :] = buf[0:HALO, :]
        return result.astype(bf16)

    round_value = conv_back(
        value_buf,
        jnp.concatenate(grad_value_parts, axis=0),
        value_at,
        value_bent,
        value[...],
        value_kernel,
        value_taps_out,
    )
    round_state = conv_back(
        state_buf,
        jnp.concatenate(grad_state_parts, axis=0),
        state_at,
        state_bent,
        state[...],
        state_kernel,
        state_taps_out,
    )
    round_step = jnp.concatenate(grad_step_parts, axis=0).astype(bf16)
    value_out[...] = round_value
    state_out[...] = round_state
    step_out[...] = round_step
    weight_total[...] += mm_tn(
        normed[...], jnp.concatenate([round_value, round_gate, round_state], axis=1)
    )
    step_total[...] += mm_tn(round_step, normed[...])

    @pl.when(pl.program_id(0) == steps - 1)
    def _():
        fold = step_total.shape[1] // channels
        local_rows[...] = jnp.zeros_like(local_rows)
        for h in range(heads):
            for q in range(fold):
                local_rows[h * fold + q : h * fold + q + 1, :] = step_total[
                    h : h + 1, q * channels : (q + 1) * channels
                ]
        at = heads * fold
        local_rows[at : at + CONV + 1, :] = value_taps_out[0 : CONV + 1, :]
        at += CONV + 1
        local_rows[at : at + 1, :] = gate_gain_out[0:1, :]
        local_rows[at + 1 : at + 2, :] = jnp.concatenate(
            [steps_out[0:1, :], steps_out[1:2, :], head_sum(skip_out[...], to_heads)[0:1, :]],
            axis=1,
        )
        shared_rows[...] = jnp.zeros_like(shared_rows)
        shared_rows[0 : CONV + 1, :] = state_taps_out[0 : CONV + 1, :]

        _, tall, _ = pieces_out[0].shape
        count = small_rows(side**2, channels)
        slabs[...] = jnp.zeros_like(slabs)
        for d in range(side**2):
            at = 0
            for ref in (local_rows, shared_rows):
                each = ref.shape[0] // side**2
                for j in range(d * each, (d + 1) * each):
                    for lanes in range(0, ref.shape[1], LANES):
                        mine = ref[j : j + 1, lanes : lanes + LANES]
                        high = mine.astype(bf16).astype(f32)
                        slabs[d, at : at + 1, :] = high
                        slabs[d, count + at : count + at + 1, :] = mine - high
                        at += 1
        rows = channels // side
        for k, piece in enumerate(pieces_out):
            for j in range(side):
                y, x = block_of(place, lax.rem(place[3 + place[1]] + k, side), j)
                here = pl.ds(pl.multiple_of((y * side + x) * tall, tall), tall)
                piece[j, :, 0 : 2 * channels] = weight_total[here, 0 : 2 * channels].astype(bf16)
                for c in range(width // channels):
                    piece[j, c * rows : (c + 1) * rows, 2 * channels : 3 * channels] = out_total[
                        x,
                        pl.ds(pl.multiple_of(y * rows, rows), rows),
                        c * channels : (c + 1) * channels,
                    ].astype(bf16)
                at = 3 * channels
                piece[j, :, at : at + 2 * STATE] = weight_total[here, 2 * channels :].astype(bf16)
                piece[j, :, at + 2 * STATE :] = slabs[y * side + x].astype(bf16)


def block_of(place, first, second):
    core = place[1]
    return first + core * (second - first), second + core * (first - second)


def small_rows(pieces, channels):
    return (LOCAL * channels + SHARED * 2 * STATE) // LANES // pieces


def input_kernel(
    tokens,
    round_gate,
    round_value,
    round_state,
    round_step,
    in_gate,
    in_value,
    in_state,
    in_step,
    part_out,
    norm_gain_out,
):
    @pl.when(pl.program_id(0) == 0)
    def _():
        norm_gain_out[...] = jnp.zeros_like(norm_gain_out)

    total = (
        mm_nt(round_gate[...], in_gate[...])
        + mm_nt(round_value[...], in_value[...])
        + mm_nt(round_state[...], in_state[...])
        + mm(round_step[...], all_lanes(in_step[...]))
    )
    part_out[...] = total.astype(bf16)
    x = tokens[...].astype(f32)
    x = x * lax.rsqrt(jnp.mean(x * x, axis=1, keepdims=True) + epsilon)
    add_row(norm_gain_out, 0, total * x)


def gather_kernel(index, place, *refs):
    *pieces, out, sems = refs
    copies = [
        pltpu.make_async_copy(piece, out.at[index(place, k)], sems.at[k])
        for k, piece in enumerate(pieces)
    ]
    for copy in copies:
        copy.start()
    for copy in copies:
        copy.wait()


def total_of(pieces):
    total = pieces[0][...].astype(f32)
    for piece in pieces[1:]:
        total = total + piece[...].astype(f32)
    return total


def line_sum_kernel(place, *refs):
    side = len(refs) // 2
    for k, out in enumerate(refs[side:]):
        at = lax.rem(place[4 - place[1]] + k, side)
        out[...] = total_of([ref.at[at] for ref in refs[:side]]).astype(bf16)


def block_sum_kernel(plain, count, gain_rows, *refs):
    *pieces, norm_gain, weights_out, rest_out = refs
    total = total_of(pieces)
    weights_out[...] = total[:, :plain].astype(bf16)
    rest_out[:, 0 : 2 * STATE] = total[:, plain : plain + 2 * STATE]
    small = total[:, plain + 2 * STATE :]
    rest_out[:, 2 * STATE :] = jnp.zeros_like(small)
    rest_out[0:count, 2 * STATE :] = small[:count, :] + small[count : 2 * count, :]
    for j in range(norm_gain.shape[1] // LANES):
        at = gain_rows + j
        rest_out[at : at + 1, 2 * STATE :] = norm_gain[0:1, j * LANES : (j + 1) * LANES]


def block_pack_kernel(local, count, gain_rows, gains, weights, before, own, one, two, three, out):
    total = (own[...] + two[...]) + (one[...] + three[...])
    plain = weights.shape[1]
    out[:, :plain] = weights[...]
    out[:, plain : plain + 2 * STATE] = total[:, : 2 * STATE].astype(bf16)
    small = total[:, 2 * STATE :]
    small = jnp.where(iota(small.shape, 0) < local, before[:, 2 * STATE :], small)
    high = small.astype(bf16).astype(f32)
    low = small - high
    packed = jnp.concatenate(
        [
            high[:count, :],
            low[:count, :],
            high[gain_rows : gain_rows + gains, :],
            low[gain_rows : gain_rows + gains, :],
            jnp.zeros((small.shape[0] - 2 * count - 2 * gains, LANES), f32),
        ],
        axis=0,
    )
    out[:, plain + 2 * STATE :] = packed.astype(bf16)


def unpack_kernel(heads, side, count, gains, place, *refs):
    pieces = refs[:side]
    value_out, gate_out, out_out, state_out, *small_outs = refs[side:-5]
    wide, states, small_rows_at, gain_parts, sems = refs[-5:]
    _, _, tall, channels = wide.shape
    rows, width = out_out.shape[0] // side, out_out.shape[1] // side
    copies = []

    def send(source, target):
        copies.append(pltpu.make_async_copy(source, target, sems.at[len(copies)]))
        copies[-1].start()

    for k, piece in enumerate(pieces):
        first = lax.rem(place[3 + place[1]] + side - k, side)
        for j in range(side):
            y, x = block_of(place, first, j)
            at = k * side + j
            d = y * side + x
            here = pl.ds(pl.multiple_of(d * tall, tall), tall)
            for c in range(3):
                wide[at, c] = piece[j, :, c * channels : (c + 1) * channels].astype(f32)
            send(wide.at[at, 0], value_out.at[here])
            send(wide.at[at, 1], gate_out.at[here])
            for c in range(width // channels):
                send(
                    wide.at[at, 2, pl.ds(c * rows, rows)],
                    out_out.at[
                        pl.ds(pl.multiple_of(y * rows, rows), rows),
                        pl.ds(pl.multiple_of(x * width + c * channels, channels), channels),
                    ],
                )
            plain = 3 * channels
            states[at] = piece[j, :, plain : plain + 2 * STATE].astype(f32)
            send(states.at[at], state_out.at[here])
            small = piece[j, :, plain + 2 * STATE :].astype(f32)
            small_rows_at[d] = small[:count, :] + small[count : 2 * count, :]
            low = 2 * count + gains
            gain_parts[d] = small[2 * count : low, :] + small[low : low + gains, :]
    (
        step_out,
        step_bias_out,
        decay_out,
        skip_out,
        value_taps_out,
        value_bias_out,
        gate_gain_out,
        norm_gain_out,
        state_taps_out,
        state_bias_out,
    ) = small_outs
    fold, across = step_out.shape[1] // channels, channels // LANES
    own, ours = LOCAL // side**2, SHARED // side**2

    def local(row, tile):
        at = row % own * across + tile
        return small_rows_at[row // own, at : at + 1, :]

    def shared(row, tile):
        at = own * across + row % ours * (2 * STATE // LANES) + tile
        return small_rows_at[row // ours, at : at + 1, :]

    total = gain_parts[0]
    for d in range(1, side**2):
        total = total + gain_parts[d]
    for t in range(gains):
        norm_gain_out[t * LANES : (t + 1) * LANES] = total[t, :]
    for h in range(heads):
        for q in range(fold):
            for t in range(across):
                at = q * channels + t * LANES
                step_out[h : h + 1, at : at + LANES] = local(h * fold + q, t)
    row = heads * fold
    for t in range(across):
        lanes = slice(t * LANES, (t + 1) * LANES)
        for k in range(CONV):
            value_taps_out[k : k + 1, lanes] = local(row + k, t)
        value_bias_out[lanes] = local(row + CONV, t)[0]
        gate_gain_out[lanes] = local(row + CONV + 1, t)[0]
    for t, out in enumerate((step_bias_out, decay_out, skip_out)):
        out[...] = local(row + CONV + 2, t)[:, :heads]
    for t in range(2 * STATE // LANES):
        lanes = slice(t * LANES, (t + 1) * LANES)
        for k in range(CONV):
            state_taps_out[k : k + 1, lanes] = shared(k, t)
        state_bias_out[lanes] = shared(CONV, t)[0]
    for copy in copies:
        copy.wait()


def output_kernel(inner, total, tokens, stats, out):
    scale, _ = stats_columns(stats[...], inner)
    out[...] = (tokens[...].astype(f32) + scale * total[...].astype(f32)).astype(bf16)


def grad_kernel(total, tokens, cotangent, norm_gain, out):
    x = tokens[...].astype(f32)
    inverse = lax.rsqrt(jnp.mean(x * x, axis=1, keepdims=True) + epsilon)
    scaled = total[...].astype(f32) * row_of(norm_gain)
    moment = jnp.mean(scaled * x, axis=1, keepdims=True)
    grad = inverse * scaled - x * (inverse * inverse * inverse * moment)
    out[...] = (cotangent[...].astype(f32) + grad).astype(bf16)


def whole(array):
    zeros = (0,) * array.ndim
    return pl.BlockSpec(array.shape, lambda i: zeros)


def in_scalars():
    return pl.BlockSpec(memory_space=pltpu.SMEM)


def by_rows(width, steps=None, rows=ROWS):
    if steps is None:
        return pl.BlockSpec((rows, width), lambda i: (i, 0))
    return pl.BlockSpec((rows, width), lambda i: (steps - 1 - i, 0))


def swap_core(x):
    return lax.ppermute(x, "tensor", [(i, i ^ 1) for i in range(8)])


def move_z(x, k):
    return lax.ppermute(x, "tensor", [(i, (i + 2 * k) % 8) for i in range(8)])


def move_dp(x, k, side, stage):
    pairs = []
    for y in range(side):
        for x_at in range(side):
            for t in range(8):
                if (t + stage) % 2 == 0:
                    to = (y + k) % side * side + x_at
                else:
                    to = y * side + (x_at + k) % side
                pairs.append(((y * side + x_at) * 8 + t, to * 8 + t))
    return lax.ppermute(x, ("dp", "tensor"), pairs)


def after(x, *others):
    return lax.optimization_barrier((x,) + others)[0]


free = pl.CostEstimate(flops=0, bytes_accessed=0, transcendentals=0)


def at_place(kernel, place, operands, grid, in_specs, out_specs, out_shape, scratch=()):
    return pl.pallas_call(
        kernel,
        grid_spec=pltpu.PrefetchScalarGridSpec(
            num_scalar_prefetch=1,
            grid=grid,
            in_specs=in_specs,
            out_specs=out_specs,
            scratch_shapes=scratch,
        ),
        out_shape=out_shape,
        compiler_params=pltpu.CompilerParams(
            dimension_semantics=("arbitrary",) * len(grid), vmem_limit_bytes=VMEM
        ),
        cost_estimate=free,
    )(place, *operands)


def fixed(*shape):
    return pl.BlockSpec(shape, lambda *_: (0,) * len(shape))


def gather_pieces(place, pieces, index):
    return at_place(
        partial(gather_kernel, index),
        place,
        pieces,
        (1,),
        [fixed(*pieces[0].shape)] * len(pieces),
        pl.BlockSpec(memory_space=pl.ANY),
        jax.ShapeDtypeStruct((len(pieces),) + pieces[0].shape, pieces[0].dtype),
        [pltpu.SemaphoreType.DMA((len(pieces),))],
    )


def along_second(place, pieces):
    side = len(pieces)
    return gather_pieces(
        place, pieces, lambda at, k: lax.rem(at[4 - at[1]] + side - k, side)
    )


def on_device(
    tokens,
    norm_gain,
    in_gate,
    in_value,
    in_state,
    in_step,
    step_bias,
    decay_log,
    skip_gain,
    conv_value_kernel,
    conv_value_bias,
    conv_state_kernel,
    conv_state_bias,
    gate_gain,
    out_weight,
    cotangent,
):
    features = tokens.shape[1]
    channels = in_gate.shape[1]
    heads = step_bias.shape[0]
    inner = channels * lax.axis_size("tensor")
    steps = LEN // ROWS
    parts = ROWS // Q
    dp = lax.axis_size("dp")
    side = math.isqrt(dp)
    me = lax.axis_index("tensor")
    row = lax.axis_index("dp")
    place = jnp.stack([me // 2, me % 2, me, row // side, row % side]).astype(jnp.int32)

    step_weight = in_step.T
    sds = jax.ShapeDtypeStruct
    params = pltpu.CompilerParams(
        dimension_semantics=("arbitrary",), vmem_limit_bytes=VMEM
    )
    stats_rows = pl.BlockSpec((8, ROWS), lambda i: (0, i))
    memory_rows = lambda at: pl.BlockSpec((parts, STATE, channels), lambda i: (at(i), 0, 0))

    (
        normed,
        gate_pre,
        value_pre,
        value_conv,
        state_pre,
        state_conv,
        step_pre,
        mixed,
        back,
        part,
        memories,
        stats,
    ) = pl.pallas_call(
        partial(forward_kernel, heads),
        grid=(steps,),
        in_specs=[
            by_rows(features),
            whole(norm_gain),
            whole(in_gate),
            whole(in_value),
            whole(in_state),
            whole(step_weight),
            in_scalars(),
            in_scalars(),
            in_scalars(),
            whole(conv_value_kernel),
            whole(conv_value_bias),
            whole(conv_state_kernel),
            whole(conv_state_bias),
            whole(gate_gain),
            whole(out_weight),
            by_rows(features),
        ],
        out_specs=[
            by_rows(features),
            by_rows(channels),
            by_rows(channels),
            by_rows(channels),
            by_rows(2 * STATE),
            by_rows(2 * STATE),
            by_rows(LANES),
            by_rows(channels),
            by_rows(channels),
            by_rows(features),
            memory_rows(lambda i: i),
            stats_rows,
        ],
        out_shape=[
            sds((LEN, features), bf16),
            sds((LEN, channels), f32),
            sds((LEN, channels), f32),
            sds((LEN, channels), f32),
            sds((LEN, 2 * STATE), f32),
            sds((LEN, 2 * STATE), f32),
            sds((LEN, LANES), f32),
            sds((LEN, channels), f32),
            sds((LEN, channels), f32),
            sds((LEN, features), bf16),
            sds((LEN // Q, STATE, channels), bf16),
            sds((8, LEN), f32),
        ],
        scratch_shapes=[
            pltpu.VMEM((ROWS + HALO, channels), f32),
            pltpu.VMEM((ROWS + HALO, 2 * STATE), f32),
            pltpu.VMEM((STATE, channels), f32),
        ],
        compiler_params=params,
        cost_estimate=free,
    )(
        tokens,
        norm_gain,
        in_gate,
        in_value,
        in_state,
        step_weight,
        step_bias,
        decay_log,
        skip_gain,
        conv_value_kernel,
        conv_value_bias,
        conv_state_kernel,
        conv_state_bias,
        gate_gain,
        out_weight,
        cotangent,
    )

    out_sum = lax.psum_scatter(part, "tensor", scatter_dimension=0, tiled=True)
    stats = stats + swap_core(stats)
    moved = [move_z(stats, k) for k in (1, 2, 3)]
    stats = (stats + moved[1]) + (moved[0] + moved[2])

    back_rows = partial(by_rows, steps=steps)
    lanes = 3 * channels + 2 * STATE + LANES
    tall = features // dp
    round_gate, round_value, round_state, round_step, *weights = pl.pallas_call(
        partial(backward_kernel, heads, inner, steps, side),
        grid=(steps,),
        in_specs=[
            in_scalars(),
            pl.BlockSpec((8, ROWS), lambda i: (0, steps - 1 - i)),
            back_rows(features),
            back_rows(features),
            back_rows(channels),
            back_rows(channels),
            back_rows(channels),
            back_rows(channels),
            back_rows(channels),
            back_rows(2 * STATE),
            back_rows(2 * STATE),
            back_rows(LANES),
            memory_rows(lambda i: steps - 1 - i),
            whole(gate_gain),
            in_scalars(),
            in_scalars(),
            whole(conv_value_kernel),
            whole(conv_state_kernel),
        ],
        out_specs=[
            back_rows(channels),
            back_rows(channels),
            back_rows(2 * STATE),
            back_rows(LANES),
        ]
        + [fixed(side, tall, lanes)] * side,
        out_shape=[
            sds((LEN, channels), bf16),
            sds((LEN, channels), bf16),
            sds((LEN, 2 * STATE), bf16),
            sds((LEN, LANES), bf16),
        ]
        + [sds((side, tall, lanes), bf16)] * side,
        scratch_shapes=[
            pltpu.VMEM((ROWS + HALO, channels), f32),
            pltpu.VMEM((ROWS + HALO, 2 * STATE), f32),
            pltpu.VMEM((STATE, channels), f32),
            pltpu.VMEM((features, 2 * channels + 2 * STATE), f32),
            pltpu.VMEM((side, channels, features // side), f32),
            pltpu.VMEM((LANES, features), f32),
            pltpu.VMEM((8, channels), f32),
            pltpu.VMEM((8, channels), f32),
            pltpu.VMEM((8, 2 * STATE), f32),
            pltpu.VMEM((8, channels), f32),
            pltpu.VMEM((8, LANES), f32),
            pltpu.VMEM((LOCAL, channels), f32),
            pltpu.VMEM((SHARED, 2 * STATE), f32),
            pltpu.VMEM((dp, tall, LANES), f32),
        ],
        compiler_params=params,
        cost_estimate=free,
    )(
        place,
        stats,
        normed,
        cotangent,
        gate_pre,
        mixed,
        back,
        value_pre,
        value_conv,
        state_pre,
        state_conv,
        step_pre,
        memories,
        gate_gain,
        decay_log,
        skip_gain,
        conv_value_kernel,
        conv_state_kernel,
    )
    out_sum = after(out_sum, round_gate)
    weights[0] = after(weights[0], out_sum)
    out_sum = lax.all_gather(out_sum, "tensor", tiled=True)

    weights = [weights[0]] + [
        move_dp(after(weights[k], weights[0]), k, side, 0) for k in range(1, side)
    ]

    part, norm_gain_part = pl.pallas_call(
        input_kernel,
        grid=(steps,),
        in_specs=[
            by_rows(features),
            by_rows(channels),
            by_rows(channels),
            by_rows(2 * STATE),
            by_rows(LANES),
            whole(in_gate),
            whole(in_value),
            whole(in_state),
            whole(step_weight),
        ],
        out_specs=[
            by_rows(features),
            fixed(8, features),
        ],
        out_shape=[
            sds((LEN, features), bf16),
            sds((8, features), f32),
        ],
        compiler_params=params,
        cost_estimate=free,
    )(
        tokens,
        round_gate,
        round_value,
        round_state,
        round_step,
        in_gate,
        in_value,
        in_state,
        step_weight,
    )
    weights[0] = after(weights[0], norm_gain_part)
    weights = at_place(
        line_sum_kernel,
        place,
        weights,
        (1,),
        [fixed(side, tall, lanes)] * side,
        [fixed(tall, lanes)] * side,
        [sds((tall, lanes), bf16)] * side,
    )
    grad_sum = lax.psum_scatter(
        after(part, weights[0]), "tensor", scatter_dimension=0, tiled=True
    )
    weights = [weights[0]] + [move_dp(weights[k], k, side, 1) for k in range(1, side)]

    block_output = pl.pallas_call(
        partial(output_kernel, inner),
        grid=(steps,),
        in_specs=[by_rows(features), by_rows(features), stats_rows],
        out_specs=by_rows(features),
        out_shape=sds((LEN, features), bf16),
        compiler_params=params,
        cost_estimate=free,
    )(after(out_sum, weights[0]), tokens, stats)

    weights[0] = after(weights[0], block_output)

    count = small_rows(dp, channels)
    local = LOCAL * channels // LANES // dp
    gains = features // LANES
    gain_rows = -(-count // 8) * 8
    plain = 3 * channels
    vmem = pltpu.CompilerParams(vmem_limit_bytes=VMEM)
    weights, rest = pl.pallas_call(
        partial(block_sum_kernel, plain, count, gain_rows),
        out_shape=[sds((tall, plain), bf16), sds((tall, lanes - plain), f32)],
        compiler_params=vmem,
        cost_estimate=free,
    )(*weights, norm_gain_part)
    both = rest + swap_core(rest)
    weights = pl.pallas_call(
        partial(block_pack_kernel, local, count, gain_rows, gains),
        out_shape=sds((tall, lanes), bf16),
        compiler_params=vmem,
        cost_estimate=free,
    )(weights, rest, both, *[move_z(both, k) for k in (1, 2, 3)])
    weights = [weights] + [move_dp(weights, k, side, 1) for k in range(1, side)]
    weights = along_second(place, weights)
    weights = [weights] + [move_dp(weights, k, side, 0) for k in range(1, side)]
    grad_sum = lax.all_gather(after(grad_sum, weights[0]), "tensor", tiled=True)
    grad_tokens = pl.pallas_call(
        grad_kernel,
        grid=(steps,),
        in_specs=[by_rows(features)] * 3 + [whole(norm_gain)],
        out_specs=by_rows(features),
        out_shape=sds((LEN, features), bf16),
        compiler_params=params,
        cost_estimate=free,
    )(grad_sum, tokens, cotangent, norm_gain)
    weights[0] = after(weights[0], grad_tokens)

    anywhere = pl.BlockSpec(memory_space=pl.ANY)
    smalls = [
        (heads, features),
        (1, heads),
        (1, heads),
        (1, heads),
        (CONV, channels),
        (channels,),
        (channels,),
        (features,),
        (CONV, 2 * STATE),
        (2 * STATE,),
    ]
    across = features // side // channels
    grad_in_value, grad_in_gate, grad_out_weight, grad_in_state, *smalls = at_place(
        partial(unpack_kernel, heads, side, count, gains),
        place,
        weights,
        (1,),
        [fixed(side, tall, lanes)] * side,
        [anywhere] * 4 + [fixed(*shape) for shape in smalls],
        [
            sds((features, channels), f32),
            sds((features, channels), f32),
            sds((channels, features), f32),
            sds((features, 2 * STATE), f32),
        ]
        + [sds(shape, f32) for shape in smalls],
        [
            pltpu.VMEM((dp, 3, tall, channels), f32),
            pltpu.VMEM((dp, tall, 2 * STATE), f32),
            pltpu.VMEM((dp, count, LANES), f32),
            pltpu.VMEM((dp, gains, LANES), f32),
            pltpu.SemaphoreType.DMA((dp * (3 + across),)),
        ],
    )
    grad_in_step = smalls[0].T
    (
        grad_step_bias,
        grad_decay_log,
        grad_skip_gain,
        grad_conv_value_kernel,
        grad_conv_value_bias,
        grad_gate_gain,
        grad_norm_gain,
        grad_conv_state_kernel,
        grad_conv_state_bias,
    ) = (a[0] if a.shape[0] == 1 else a for a in smalls[1:])
    return (
        block_output,
        grad_tokens,
        grad_norm_gain,
        grad_in_gate,
        grad_in_value,
        grad_in_state,
        grad_in_step,
        grad_step_bias,
        grad_decay_log,
        grad_skip_gain,
        grad_conv_value_kernel,
        grad_conv_value_bias,
        grad_conv_state_kernel,
        grad_conv_state_bias,
        grad_gate_gain,
        grad_out_weight,
    )


def solution(mesh):
    placed = (
        P("dp", None),
        P(),
        P(None, "tensor"),
        P(None, "tensor"),
        P(),
        P(None, "tensor"),
        P("tensor"),
        P("tensor"),
        P("tensor"),
        P(None, "tensor"),
        P("tensor"),
        P(),
        P(),
        P("tensor"),
        P("tensor", None),
        P("dp", None),
    )
    return jax.shard_map(
        on_device,
        mesh=mesh,
        in_specs=placed,
        out_specs=(
            P("dp", None),
            P("dp", None),
            P(),
            P(None, "tensor"),
            P(None, "tensor"),
            P(),
            P(None, "tensor"),
            P("tensor"),
            P("tensor"),
            P("tensor"),
            P(None, "tensor"),
            P("tensor"),
            P(),
            P(),
            P("tensor"),
            P("tensor", None),
        ),
        check_vma=False,
    )
```

time: 306 us -> 207 us (0.68); the launches traced: 302 us -> 207 us
  Pallas kernels: 45 us -> 86 us
  local copies, waits for them, and re-layouts: 44.6 us -> 9.53 us
  waiting for transfers between devices: 95.7 us -> 67.1 us
  starting transfers between devices: 53.1 us -> 28.8 us
  other arithmetic: 21.8 us -> 1.55 us
  matrix products: 14.5 us -> 0 us
  blocking collectives: 13.3 us -> 0 us
    all_to_all x4 -> x0, waiting for transfers between devices: 55.9 us -> none  [the longest x2 38.1 us: scatter_over_dp(): got = lax.all_to_all(x, 'dp', 0, 0, tiled=True)]
    pallas_call x2 -> x9, Pallas kernels: 27.2 us -> 67.2 us  [the longest x1 25.8 us: on_device(): pl.pallas_call(partial(backward_kernel, heads, inner, steps, side), grid=...]
    all_gather x2, waiting for transfers between devices: 0.01 us -> 26.1 us  [the longest x1 26.1 us: on_device(): grad_sum = lax.all_gather(after(grad_sum, weights[0]), 'tensor', tiled=True)]
    all_to_all x4 -> x0, starting transfers between devices: 22.5 us -> none  [the longest x2 12.5 us: scatter_over_dp(): got = lax.all_to_all(x, 'dp', 0, 0, tiled=True)]
    ppermute x9 -> x6, waiting for transfers between devices: 33.9 us -> 13.1 us  [move_z(): return lax.ppermute(x, 'tensor', [(i, (i + 2 * k) % 8) for i in range(8)])]
    ppermute x6 -> x12, waiting for transfers between devices: 5.15 us -> 25.7 us  [move_dp(): return lax.ppermute(x, ('dp', 'tensor'), pairs)]
    all_gather x1 -> x0, blocking collectives: 13.3 us -> none  [on_device(): lax.all_gather(state_share, 'tensor', tiled=True).astype(f32)]
    dot_general x4 -> x0, matrix products: 12.6 us -> none  [mm_tn(): lax.dot_general(a, b, (((0,), (0,)), ((), ())), preferred_element_type=f32)]
  transfers between devices with their start and end apart: 24 -> 24, of which waited for: 12 -> 14; matrix products, arithmetic and copies ran while one was open for 20% -> 1% of each run, Pallas kernels for 2% -> 29%
where the time goes in v2:
time: 207 us
  Pallas kernels  86 us (42%)
  waiting for transfers between devices  67.1 us (32%)
  starting transfers between devices  28.8 us (14%)
  between operations  13.9 us (7%)
  local copies, waits for them, and re-layouts  9.53 us (5%)
    all_gather x1, waiting for transfers between devices, on_device(): grad_sum = lax.all_gather(after(grad_sum, weights[0]), 'tensor', tiled=True)  26.1 us
    pallas_call x1, Pallas kernels, on_device(): pl.pallas_call(partial(backward_kernel, heads, inner, steps, side), grid=...  25.8 us
    ppermute x12, waiting for transfers between devices, move_dp(): return lax.ppermute(x, ('dp', 'tensor'), pairs)  25.7 us
    pallas_call x1, Pallas kernels, on_device(): pl.pallas_call(partial(forward_kernel, heads), grid=(steps,), in_specs=[b...  18.8 us
    pallas_call x3, Pallas kernels, at_place(): pl.pallas_call(kernel, grid_spec=pltpu.PrefetchScalarGridSpec(num_scalar_...  15 us
    ppermute x12, starting transfers between devices, move_dp(): return lax.ppermute(x, ('dp', 'tensor'), pairs)  14.4 us
    ppermute x6, waiting for transfers between devices, move_z(): return lax.ppermute(x, 'tensor', [(i, (i + 2 * k) % 8) for i in range(8)])  13.1 us
    pallas_call x1, Pallas kernels, on_device(): pl.pallas_call(input_kernel, grid=(steps,), in_specs=[by_rows(features),...  9.33 us
  transfers between devices with their start and end apart: 24, of which 14 were waited for; matrix products, arithmetic and copies ran while one was open for 1% of the time, Pallas kernels for 29%

profile of v2, /device:TPU:1, one launch (start us, length us, event | category | flops | bytes accessed | tf_op | source)
XLA Modules:
  0.0 206.9 jit_solution(9414331864687162590)
XLA Ops:
  7.2 18.8 %shard_map.279 = (bf16[1024,1536]{1,0:T(8,128)(2,1)}, f32[1024,384]{1,0:T(8,128)}, f32[1024,384]{1,0:T(8,128)}, f32[1024,384]{1,0:T(8,128)}, f32[1024,256]{1,0:T...) custom-call(bf16[1024,1536]{1,0:T(8,128)(2,1)} %tokens.7, ...), custom_call_target="tpu_custom_call" | custom-call | tf_op jit(solution)/shard_map/pallas_call | solution.py:844
  26.8 1.4 collective-permute-start
  29.1 3.8 %collective-permute-start.3 = (f32[8,1024]{1,0:T(8,128)S(1)}, f32[8,1024]{1,0:T(8,128)S(1)}, u32[]{:S(2)}, u32[]{:S(2)}) collective-permute-start(f32[8,1024]{1,0:T(8,128)S(1)} %add.30), channel_id=1, source_target_pairs={{0,6},{1,7},{2,0},{3,1},{4,2},{5,3},{6,4},{7,5},{8,14},{9,15},{10,... | collective-permute-start | bytes 98312 | tf_op jit(solution)/shard_map/ppermute | solution.py:728
  32.9 1.3 collective-permute-start.1
  34.9 2.0 collective-permute-done.2
  37.9 25.8 %shard_map.280 = (bf16[1024,384]{1,0:T(8,128)(2,1)}, bf16[1024,384]{1,0:T(8,128)(2,1)}, bf16[1024,256]{1,0:T(8,128)(2,1)}, bf16[1024,128]{1,0:T(8,128)(2,1)}, bf...) custom-call(s32[5]{0:T(128)} %stack.23.place, ...), custom_call_target="tpu_custom_call" | custom-call | tf_op jit(solution)/shard_map/pallas_call | solution.py:927
  63.8 1.4 collective-permute-start.4
  65.2 2.4 %collective-permute-start.5 = (bf16[4,96,1536]{2,1,0:T(8,128)(2,1)}, bf16[4,96,1536]{2,1,0:T(8,128)(2,1)S(1)}, u32[]{:S(2)}, u32[]{:S(2)}) collective-permute-start(bf16[4,96,1536]{2,1,0:T(8,128)(2,1)} %get-tuple-element.93), channel_id=1, source_target_pairs={{0,64},{1,17},{2,66},{3,19},{4,68},{5,21},{6,70},{7,23},{8,72},{9,... | collective-permute-start | bytes 3538952 | tf_op jit(solution)/shard_map/ppermute | solution.py:741
  67.6 1.1 collective-permute-start.6
  68.8 9.3 %shard_map.281 = (bf16[1024,1536]{1,0:T(8,128)(2,1)}, f32[8,1536]{1,0:T(8,128)}) custom-call(bf16[1024,1536]{1,0:T(8,128)(2,1)} %tokens.7, bf16[1024,384]{1,0:T(8,128)(2,1)} %get-tuple-element.81.round_gate, bf16[1024,384]{1,0:T(8,128)(2,1)} %get-tuple-element.85.round_value, bf16[1024,256]{1,0:T(8,128)(2,1)} %get-tuple-element.86.round_state, ...), custom_call_target="tpu_custom_call" | custom-call | tf_op jit(solution)/shard_map/pallas_call | solution.py:1010
  78.1 2.6 %collective-permute-done.4.refs_1_ = bf16[4,96,1536]{2,1,0:T(8,128)(2,1)S(1)} collective-permute-done((bf16[4,96,1536]{2,1,0:T(8,128)(2,1)}, bf16[4,96,1536]{2,1,0:T(8,128)(2,1)S(1)}, u32[]{:S(2)}, u32[]{:S(2)}) %collective-permute-start.4) | collective-permute-done | bytes 1179680 | tf_op jit(solution)/shard_map/ppermute | solution.py:741
  80.7 13.7 %collective-permute-done.5.refs_2_ = bf16[4,96,1536]{2,1,0:T(8,128)(2,1)S(1)} collective-permute-done((bf16[4,96,1536]{2,1,0:T(8,128)(2,1)}, bf16[4,96,1536]{2,1,0:T(8,128)(2,1)S(1)}, u32[]{:S(2)}, u32[]{:S(2)}) %collective-permute-start.5) | collective-permute-done | bytes 1179680 | tf_op jit(solution)/shard_map/ppermute | solution.py:741
  96.4 4.5 %shard_map.282 = (bf16[96,1536]{1,0:T(8,128)(2,1)}, bf16[96,1536]{1,0:T(8,128)(2,1)}, bf16[96,1536]{1,0:T(8,128)(2,1)}, bf16[96,1536]{1,0:T(8,128)(2,1)}) custom-call(s32[5]{0:T(128)} %stack.23.place, bf16[4,96,1536]{2,1,0:T(8,128)(2,1)} %get-tuple-element.89.refs_0_, bf16[4,96,1536]{2,1,0:T(8,128)(2,1)} %copy-done.2, bf16[4,96,1536]{2,1,0:T(8,128)(2,1)} %copy-done.4, ...), custom_call_target="tpu_custom_call" | custom-call | tf_op jit(solution)/shard_map/pallas_call | solution.py:752
  102.8 2.6 %collective-permute-start.8 = (bf16[96,1536]{1,0:T(8,128)(2,1)S(1)}, bf16[96,1536]{1,0:T(8,128)(2,1)S(1)}, u32[]{:S(2)}, u32[]{:S(2)}) collective-permute-start(bf16[96,1536]{1,0:T(8,128)(2,1)S(1)} %copy-done.18), channel_id=1, source_target_pairs={{0,16},{1,65},{2,18},{3,67},{4,20},{5,69},{6,22},{7,71},{8,24},{9,... | collective-permute-start | bytes 884744 | tf_op jit(solution)/shard_map/ppermute | solution.py:741
  106.5 5.6 %shard_map.283 = bf16[1024,1536]{1,0:T(8,128)(2,1)} custom-call(bf16[1024,1536]{1,0:T(8,128)(2,1)} %all-gather.3.cloned.1.call-done.total, bf16[1024,1536]{1,0:T(8,128)(2,1)} %tokens.7, f32[8,1024]{1,0:T(8,128)} %add_add_fusion.stats), custom_call_target="tpu_custom_call" | custom-call | tf_op jit(solution)/shard_map/pallas_call | solution.py:1060
  114.1 2.1 %shard_map.284 = (bf16[96,1152]{1,0:T(8,128)(2,1)}, f32[96,384]{1,0:T(8,128)}) custom-call(bf16[96,1536]{1,0:T(8,128)(2,1)} %get-tuple-element.100.refs_0_, bf16[96,1536]{1,0:T(8,128)(2,1)} %copy-done.10, bf16[96,1536]{1,0:T(8,128)(2,1)} %copy-done.11, bf16[96,1536]{1,0:T(8,128)(2,1)} %copy-done.12, f32[8,1536]{1,0:T(8,128)} %get-tuple-element.88.refs_4_), custom_call_target="tpu_custom_call" | custom-call | tf_op jit(solution)/shard_map/pallas_call | solution.py:1078
  116.2 4.4 %collective-permute-start.10 = (f32[96,384]{1,0:T(8,128)}, f32[96,384]{1,0:T(8,128)S(1)}, u32[]{:S(2)}, u32[]{:S(2)}) collective-permute-start(f32[96,384]{1,0:T(8,128)} %get-tuple-element.105.before), channel_id=1, source_target_pairs={{0,1},{1,0},{2,3},{3,2},{4,5},{5,4},{6,7},{7,6},{8,9},{9,8},{10,11... | collective-permute-start | bytes 442376 | tf_op jit(solution)/shard_map/ppermute | solution.py:724
  120.5 1.2 collective-permute-done.10
  122.7 2.7 %collective-permute-start.13 = (f32[96,384]{1,0:T(8,128)S(1)}, f32[96,384]{1,0:T(8,128)S(1)}, u32[]{:S(2)}, u32[]{:S(2)}) collective-permute-start(f32[96,384]{1,0:T(8,128)S(1)} %add.34.own), channel_id=1, source_target_pairs={{0,6},{1,7},{2,0},{3,1},{4,2},{5,3},{6,4},{7,5},{8,14},{9,15},{10,... | collective-permute-start | bytes 442376 | tf_op jit(solution)/shard_map/ppermute | solution.py:728
  126.1 5.2 %collective-permute-done.13.three = f32[96,384]{1,0:T(8,128)S(1)} collective-permute-done((f32[96,384]{1,0:T(8,128)S(1)}, f32[96,384]{1,0:T(8,128)S(1)}, u32[]{:S(2)}, u32[]{:S(2)}) %collective-permute-start.13) | collective-permute-done | bytes 147488 | tf_op jit(solution)/shard_map/ppermute | solution.py:728
  131.3 1.6 collective-permute-done.12.two
  132.9 4.0 %collective-permute-done.11.one = f32[96,384]{1,0:T(8,128)S(1)} collective-permute-done((f32[96,384]{1,0:T(8,128)S(1)}, f32[96,384]{1,0:T(8,128)S(1)}, u32[]{:S(2)}, u32[]{:S(2)}) %collective-permute-start.11) | collective-permute-done | bytes 147488 | tf_op jit(solution)/shard_map/ppermute | solution.py:728
  137.5 2.1 shard_map.285.refs_0_
  139.6 1.4 collective-permute-start.15
  141.5 4.1 %collective-permute-done.16.refs_3_ = bf16[96,1536]{1,0:T(8,128)(2,1)S(1)} collective-permute-done((bf16[96,1536]{1,0:T(8,128)(2,1)}, bf16[96,1536]{1,0:T(8,128)(2,1)S(1)}, u32[]{:S(2)}, u32[]{:S(2)}) %collective-permute-start.16) | collective-permute-done | bytes 294944 | tf_op jit(solution)/shard_map/ppermute | solution.py:741
  145.6 1.6 collective-permute-done.15.refs_2_
  147.3 3.1 %collective-permute-done.14.refs_1_ = bf16[96,1536]{1,0:T(8,128)(2,1)S(1)} collective-permute-done((bf16[96,1536]{1,0:T(8,128)(2,1)}, bf16[96,1536]{1,0:T(8,128)(2,1)S(1)}, u32[]{:S(2)}, u32[]{:S(2)}) %collective-permute-start.14) | collective-permute-done | bytes 294944 | tf_op jit(solution)/shard_map/ppermute | solution.py:741
  151.1 3.0 %shard_map.286.refs_0_ = bf16[4,96,1536]{2,1,0:T(8,128)(2,1)} custom-call(s32[5]{0:T(128)} %stack.23.place, bf16[96,1536]{1,0:T(8,128)(2,1)} %shard_map.285.refs_0_, bf16[96,1536]{1,0:T(8,128)(2,1)} %copy-done.9, bf16[96,1536]{1,0:T(8,128)(2,1)} %copy-done.8, bf16[96,1536]{1,0:T(8,128)(2,1)} %copy-done.7), custom_call_target="tpu_custom_call" | custom-call | tf_op jit(solution)/shard_map/pallas_call | solution.py:752
  154.1 1.8 collective-permute-start.19
  157.0 26.1 %all-gather.5.cloned.1.call-done.total = bf16[1024,1536]{1,0:T(8,128)(2,1)} async-done(((bf16[128,1536]{1,0:T(8,128)(2,1)}), bf16[1024,1536]{1,0:T(8,128)(2,1)}) %all-gather.5.cloned.1.call-update) | async-done | bytes 3145744 | tf_op jit(solution)/shard_map/all_gather | solution.py:1094
  183.1 7.2 %shard_map.287 = bf16[1024,1536]{1,0:T(8,128)(2,1)} custom-call(bf16[1024,1536]{1,0:T(8,128)(2,1)} %all-gather.5.cloned.1.call-done.total, bf16[1024,1536]{1,0:T(8,128)(2,1)} %tokens.7, bf16[1024,1536]{1,0:T(8,128)(2,1)} %cotangent.5, f32[1536]{0:T(1024)} %norm_gain.3), custom_call_target="tpu_custom_call" | custom-call | tf_op jit(solution)/shard_map/pallas_call | solution.py:1095
  192.8 7.6 %shard_map.288 = (f32[1536,384]{1,0:T(8,128)}, f32[1536,384]{1,0:T(8,128)}, f32[384,1536]{1,0:T(8,128)}, f32[1536,256]{1,0:T(8,128)}, f32[6,1536]{1,0:T(8,128)},...) custom-call(s32[5]{0:T(128)} %stack.23.place, ...), custom_call_target="tpu_custom_call" | custom-call | tf_op jit(solution)/shard_map/pallas_call | solution.py:752
  (74 shorter events, 17.5 us)
Async XLA Ops:
  7.2 56.6 %reduce-scatter.3.cloned.1.call-start = ((), (), s32[]{:S(2)}) async-start(), calls=%async_computation.2 | async-start | bytes 3538944 | tf_op jit(solution)/shard_map/reduce_scatter | solution.py:919
  26.1 80.4 %all-gather.3.cloned.1.call-start = ((), (), s32[]{:S(2)}) async-start(), calls=%async_computation.3 | async-start | bytes 3538944 | tf_op jit(solution)/shard_map/all_gather | solution.py:1004
  26.8 2.3 %collective-permute-start = (f32[8,1024]{1,0:T(8,128)S(1)}, f32[8,1024]{1,0:T(8,128)S(1)}, u32[]{:S(2)}, u32[]{:S(2)}) collective-permute-start(f32[8,1024]{1,0:T(8,128)S(1)} %copy-done.16), channel_id=1, source_target_pairs={{0,1},{1,0},{2,3},{3,2},{4,5},{5,4},{6,7},{7,6},{8,9},{9,8},{10,11... | collective-permute-start | bytes 98312 | tf_op jit(solution)/shard_map/ppermute | solution.py:724
  29.1 5.8 %collective-permute-start.3 = (f32[8,1024]{1,0:T(8,128)S(1)}, f32[8,1024]{1,0:T(8,128)S(1)}, u32[]{:S(2)}, u32[]{:S(2)}) collective-permute-start(f32[8,1024]{1,0:T(8,128)S(1)} %add.30), channel_id=1, source_target_pairs={{0,6},{1,7},{2,0},{3,1},{4,2},{5,3},{6,4},{7,5},{8,14},{9,15},{10,... | collective-permute-start | bytes 98312 | tf_op jit(solution)/shard_map/ppermute | solution.py:728
  32.9 4.0 %collective-permute-start.2 = (f32[8,1024]{1,0:T(8,128)S(1)}, f32[8,1024]{1,0:T(8,128)S(1)}, u32[]{:S(2)}, u32[]{:S(2)}) collective-permute-start(f32[8,1024]{1,0:T(8,128)S(1)} %add.30), channel_id=1, source_target_pairs={{0,2},{1,3},{2,4},{3,5},{4,6},{5,7},{6,0},{7,1},{8,10},{9,11},{10,... | collective-permute-start | bytes 98312 | tf_op jit(solution)/shard_map/ppermute | solution.py:728
  32.9 4.3 %collective-permute-start.1 = (f32[8,1024]{1,0:T(8,128)S(1)}, f32[8,1024]{1,0:T(8,128)S(1)}, u32[]{:S(2)}, u32[]{:S(2)}) collective-permute-start(f32[8,1024]{1,0:T(8,128)S(1)} %add.30), channel_id=1, source_target_pairs={{0,4},{1,5},{2,6},{3,7},{4,0},{5,1},{6,2},{7,3},{8,12},{9,13},{10,... | collective-permute-start | bytes 98312 | tf_op jit(solution)/shard_map/ppermute | solution.py:728
  63.8 90.3 %reduce-scatter.5.cloned.1.call-start = ((), (), s32[]{:S(2)}) async-start(), calls=%async_computation.4 | async-start | bytes 3538944 | tf_op jit(solution)/shard_map/reduce_scatter | solution.py:1055
  63.8 16.8 %collective-permute-start.4 = (bf16[4,96,1536]{2,1,0:T(8,128)(2,1)}, bf16[4,96,1536]{2,1,0:T(8,128)(2,1)S(1)}, u32[]{:S(2)}, u32[]{:S(2)}) collective-permute-start(bf16[4,96,1536]{2,1,0:T(8,128)(2,1)} %get-tuple-element.91), channel_id=1, source_target_pairs={{0,32},{1,9},{2,34},{3,11},{4,36},{5,13},{6,38},{7,15},{8,40},{9,1... | collective-permute-start | bytes 3538952 | tf_op jit(solution)/shard_map/ppermute | solution.py:741
  65.2 29.2 %collective-permute-start.5 = (bf16[4,96,1536]{2,1,0:T(8,128)(2,1)}, bf16[4,96,1536]{2,1,0:T(8,128)(2,1)S(1)}, u32[]{:S(2)}, u32[]{:S(2)}) collective-permute-start(bf16[4,96,1536]{2,1,0:T(8,128)(2,1)} %get-tuple-element.93), channel_id=1, source_target_pairs={{0,64},{1,17},{2,66},{3,19},{4,68},{5,21},{6,70},{7,23},{8,72},{9,... | collective-permute-start | bytes 3538952 | tf_op jit(solution)/shard_map/ppermute | solution.py:741
  67.6 26.7 %collective-permute-start.6 = (bf16[4,96,1536]{2,1,0:T(8,128)(2,1)}, bf16[4,96,1536]{2,1,0:T(8,128)(2,1)S(1)}, u32[]{:S(2)}, u32[]{:S(2)}) collective-permute-start(bf16[4,96,1536]{2,1,0:T(8,128)(2,1)} %get-tuple-element.95), channel_id=1, source_target_pairs={{0,96},{1,25},{2,98},{3,27},{4,100},{5,29},{6,102},{7,31},{8,104},... | collective-permute-start | bytes 3538952 | tf_op jit(solution)/shard_map/ppermute | solution.py:741
  80.7 13.7 %copy-start.2 = (bf16[4,96,1536]{2,1,0:T(8,128)(2,1)}, bf16[4,96,1536]{2,1,0:T(8,128)(2,1)S(1)}, u32[]{:S(2)}) copy-start(bf16[4,96,1536]{2,1,0:T(8,128)(2,1)S(1)} %collective-permute-done.4.refs_1_) | copy-start | bytes 3538948
  100.9 1.9 copy-start.18
  100.9 4.5 %copy-start.17 = (bf16[96,1536]{1,0:T(8,128)(2,1)S(1)}, bf16[96,1536]{1,0:T(8,128)(2,1)}, u32[]{:S(2)}) copy-start(bf16[96,1536]{1,0:T(8,128)(2,1)} %get-tuple-element.103) | copy-start | bytes 884740
  100.9 82.2 %all-gather.5.cloned.1.call-start = ((), (), s32[]{:S(2)}) async-start(), calls=%async_computation.5 | async-start | bytes 3538944 | tf_op jit(solution)/shard_map/all_gather | solution.py:1094
  101.8 10.2 %collective-permute-start.7 = (bf16[96,1536]{1,0:T(8,128)(2,1)S(1)}, bf16[96,1536]{1,0:T(8,128)(2,1)S(1)}, u32[]{:S(2)}, u32[]{:S(2)}) collective-permute-start(bf16[96,1536]{1,0:T(8,128)(2,1)S(1)} %copy-done.19), channel_id=1, source_target_pairs={{0,8},{1,33},{2,10},{3,35},{4,12},{5,37},{6,14},{7,39},{8,16},{9,4... | collective-permute-start | bytes 884744 | tf_op jit(solution)/shard_map/ppermute | solution.py:741
  102.8 9.8 %collective-permute-start.8 = (bf16[96,1536]{1,0:T(8,128)(2,1)S(1)}, bf16[96,1536]{1,0:T(8,128)(2,1)S(1)}, u32[]{:S(2)}, u32[]{:S(2)}) collective-permute-start(bf16[96,1536]{1,0:T(8,128)(2,1)S(1)} %copy-done.18), channel_id=1, source_target_pairs={{0,16},{1,65},{2,18},{3,67},{4,20},{5,69},{6,22},{7,71},{8,24},{9,... | collective-permute-start | bytes 884744 | tf_op jit(solution)/shard_map/ppermute | solution.py:741
  105.4 7.3 %collective-permute-start.9 = (bf16[96,1536]{1,0:T(8,128)(2,1)S(1)}, bf16[96,1536]{1,0:T(8,128)(2,1)S(1)}, u32[]{:S(2)}, u32[]{:S(2)}) collective-permute-start(bf16[96,1536]{1,0:T(8,128)(2,1)S(1)} %copy-done.17), channel_id=1, source_target_pairs={{0,24},{1,97},{2,26},{3,99},{4,28},{5,101},{6,30},{7,103},{8,0},{9... | collective-permute-start | bytes 884744 | tf_op jit(solution)/shard_map/ppermute | solution.py:741
  116.2 5.6 %collective-permute-start.10 = (f32[96,384]{1,0:T(8,128)}, f32[96,384]{1,0:T(8,128)S(1)}, u32[]{:S(2)}, u32[]{:S(2)}) collective-permute-start(f32[96,384]{1,0:T(8,128)} %get-tuple-element.105.before), channel_id=1, source_target_pairs={{0,1},{1,0},{2,3},{3,2},{4,5},{5,4},{6,7},{7,6},{8,9},{9,8},{10,11... | collective-permute-start | bytes 442376 | tf_op jit(solution)/shard_map/ppermute | solution.py:724
  122.7 14.1 %copy-start.6 = (f32[96,384]{1,0:T(8,128)}, f32[96,384]{1,0:T(8,128)S(1)}, u32[]{:S(2)}) copy-start(f32[96,384]{1,0:T(8,128)S(1)} %add.34.own) | copy-start | bytes 442372
  122.7 8.6 %collective-permute-start.13 = (f32[96,384]{1,0:T(8,128)S(1)}, f32[96,384]{1,0:T(8,128)S(1)}, u32[]{:S(2)}, u32[]{:S(2)}) collective-permute-start(f32[96,384]{1,0:T(8,128)S(1)} %add.34.own), channel_id=1, source_target_pairs={{0,6},{1,7},{2,0},{3,1},{4,2},{5,3},{6,4},{7,5},{8,14},{9,15},{10,... | collective-permute-start | bytes 442376 | tf_op jit(solution)/shard_map/ppermute | solution.py:728
  125.4 7.5 %collective-permute-start.12 = (f32[96,384]{1,0:T(8,128)S(1)}, f32[96,384]{1,0:T(8,128)S(1)}, u32[]{:S(2)}, u32[]{:S(2)}) collective-permute-start(f32[96,384]{1,0:T(8,128)S(1)} %add.34.own), channel_id=1, source_target_pairs={{0,4},{1,5},{2,6},{3,7},{4,0},{5,1},{6,2},{7,3},{8,12},{9,13},{10,... | collective-permute-start | bytes 442376 | tf_op jit(solution)/shard_map/ppermute | solution.py:728
  125.4 11.5 %collective-permute-start.11 = (f32[96,384]{1,0:T(8,128)S(1)}, f32[96,384]{1,0:T(8,128)S(1)}, u32[]{:S(2)}, u32[]{:S(2)}) collective-permute-start(f32[96,384]{1,0:T(8,128)S(1)} %add.34.own), channel_id=1, source_target_pairs={{0,2},{1,3},{2,4},{3,5},{4,6},{5,7},{6,0},{7,1},{8,10},{9,11},{10,... | collective-permute-start | bytes 442376 | tf_op jit(solution)/shard_map/ppermute | solution.py:728
  131.3 5.6 %copy-start.13 = (f32[96,384]{1,0:T(8,128)}, f32[96,384]{1,0:T(8,128)S(1)}, u32[]{:S(2)}) copy-start(f32[96,384]{1,0:T(8,128)S(1)} %collective-permute-done.13.three) | copy-start | bytes 442372
  132.9 4.0 %copy-start.14 = (f32[96,384]{1,0:T(8,128)}, f32[96,384]{1,0:T(8,128)S(1)}, u32[]{:S(2)}) copy-start(f32[96,384]{1,0:T(8,128)S(1)} %collective-permute-done.12.two) | copy-start | bytes 442372
  139.6 6.1 %collective-permute-start.16 = (bf16[96,1536]{1,0:T(8,128)(2,1)}, bf16[96,1536]{1,0:T(8,128)(2,1)S(1)}, u32[]{:S(2)}, u32[]{:S(2)}) collective-permute-start(bf16[96,1536]{1,0:T(8,128)(2,1)} %shard_map.285.refs_0_), channel_id=1, source_target_pairs={{0,24},{1,97},{2,26},{3,99},{4,28},{5,101},{6,30},{7,103},{8,0},{9... | collective-permute-start | bytes 884744 | tf_op jit(solution)/shard_map/ppermute | solution.py:741
  139.6 7.6 %collective-permute-start.15 = (bf16[96,1536]{1,0:T(8,128)(2,1)}, bf16[96,1536]{1,0:T(8,128)(2,1)S(1)}, u32[]{:S(2)}, u32[]{:S(2)}) collective-permute-start(bf16[96,1536]{1,0:T(8,128)(2,1)} %shard_map.285.refs_0_), channel_id=1, source_target_pairs={{0,16},{1,65},{2,18},{3,67},{4,20},{5,69},{6,22},{7,71},{8,24},{9,... | collective-permute-start | bytes 884744 | tf_op jit(solution)/shard_map/ppermute | solution.py:741
  141.0 9.4 %collective-permute-start.14 = (bf16[96,1536]{1,0:T(8,128)(2,1)}, bf16[96,1536]{1,0:T(8,128)(2,1)S(1)}, u32[]{:S(2)}, u32[]{:S(2)}) collective-permute-start(bf16[96,1536]{1,0:T(8,128)(2,1)} %shard_map.285.refs_0_), channel_id=1, source_target_pairs={{0,8},{1,33},{2,10},{3,35},{4,12},{5,37},{6,14},{7,39},{8,16},{9,4... | collective-permute-start | bytes 884744 | tf_op jit(solution)/shard_map/ppermute | solution.py:741
  145.6 4.7 %copy-start.7 = (bf16[96,1536]{1,0:T(8,128)(2,1)}, bf16[96,1536]{1,0:T(8,128)(2,1)S(1)}, u32[]{:S(2)}) copy-start(bf16[96,1536]{1,0:T(8,128)(2,1)S(1)} %collective-permute-done.16.refs_3_) | copy-start | bytes 884740
  147.3 3.1 %copy-start.8 = (bf16[96,1536]{1,0:T(8,128)(2,1)}, bf16[96,1536]{1,0:T(8,128)(2,1)S(1)}, u32[]{:S(2)}) copy-start(bf16[96,1536]{1,0:T(8,128)(2,1)S(1)} %collective-permute-done.15.refs_2_) | copy-start | bytes 884740
  154.1 36.2 %collective-permute-start.19 = (bf16[4,96,1536]{2,1,0:T(8,128)(2,1)}, bf16[4,96,1536]{2,1,0:T(8,128)(2,1)S(1)}, u32[]{:S(2)}, u32[]{:S(2)}) collective-permute-start(bf16[4,96,1536]{2,1,0:T(8,128)(2,1)} %shard_map.286.refs_0_), channel_id=1, source_target_pairs={{0,96},{1,25},{2,98},{3,27},{4,100},{5,29},{6,102},{7,31},{8,104},... | collective-permute-start | bytes 3538952 | tf_op jit(solution)/shard_map/ppermute | solution.py:741
  155.9 34.4 %collective-permute-start.18 = (bf16[4,96,1536]{2,1,0:T(8,128)(2,1)}, bf16[4,96,1536]{2,1,0:T(8,128)(2,1)S(1)}, u32[]{:S(2)}, u32[]{:S(2)}) collective-permute-start(bf16[4,96,1536]{2,1,0:T(8,128)(2,1)} %shard_map.286.refs_0_), channel_id=1, source_target_pairs={{0,64},{1,17},{2,66},{3,19},{4,68},{5,21},{6,70},{7,23},{8,72},{9,... | collective-permute-start | bytes 3538952 | tf_op jit(solution)/shard_map/ppermute | solution.py:741
  157.0 33.4 %collective-permute-start.17 = (bf16[4,96,1536]{2,1,0:T(8,128)(2,1)}, bf16[4,96,1536]{2,1,0:T(8,128)(2,1)S(1)}, u32[]{:S(2)}, u32[]{:S(2)}) collective-permute-start(bf16[4,96,1536]{2,1,0:T(8,128)(2,1)} %shard_map.286.refs_0_), channel_id=1, source_target_pairs={{0,32},{1,9},{2,34},{3,11},{4,36},{5,13},{6,38},{7,15},{8,40},{9,1... | collective-permute-start | bytes 3538952 | tf_op jit(solution)/shard_map/ppermute | solution.py:741
  (12 other events, 10.8 us)
Sparse Core Ops, SparseCore 0:
  26.2 35.9 reduce-scatter.2
  63.9 30.9 all-gather.2
  101.0 41.2 reduce-scatter.4
  154.2 28.7 all-gather.4

commit v3 on v2

--- a/solution.py
+++ b/solution.py
@@ -22,14 +22,25 @@
 epsilon = 1e-05
 f32 = jnp.float32
 bf16 = jnp.bfloat16
-exact = lax.Precision.HIGHEST
 VMEM = 60 * 1024 * 1024
-
-
-def mm(a, b, precision=None):
-    return lax.dot_general(
-        a, b, (((1,), (0,)), ((), ())), precision=precision, preferred_element_type=f32
-    )
+SMALL_VMEM = 40 * 1024 * 1024
+
+
+def mm(a, b):
+    return lax.dot_general(a, b, (((1,), (0,)), ((), ())), preferred_element_type=f32)
+
+
+def parts_of(x):
+    high = x.astype(bf16)
+    rest = x - high.astype(f32)
+    middle = rest.astype(bf16)
+    return [high, middle, (rest - middle.astype(f32)).astype(bf16)]
+
+
+def sum_rows(triangle, x):
+    width = x.shape[1]
+    total = mm(triangle, jnp.concatenate(parts_of(x), axis=1))
+    return total[:, :width] + total[:, width : 2 * width] + total[:, 2 * width :]
 
 
 def mm_nt(a, b):
@@ -179,7 +190,7 @@
     skip = channel_row(skip_gain, heads)
 
     causal = iota((Q, Q), 0) >= iota((Q, Q), 1)
-    tri = jnp.where(causal, 1.0, 0.0).astype(f32)
+    tri = jnp.where(causal, 1.0, 0.0).astype(bf16)
     mixed_parts = []
     for part in range(ROWS // Q):
         rows = slice(part * Q, (part + 1) * Q)
@@ -187,7 +198,7 @@
         c = states[rows, STATE:]
         v = values[rows, :].astype(f32)
         dt = step[rows, :]
-        decay = mm(tri, log_step[rows, :], precision=exact)
+        decay = sum_rows(tri, log_step[rows, :])
         decay_t = decay.T
         wide = expand(decay, heads)
         dt_wide = expand(dt, heads)
@@ -258,10 +269,15 @@
     skip_gain,
     value_kernel,
     state_kernel,
-    gate_out,
-    value_out,
-    state_out,
-    step_out,
+    norm_gain,
+    in_gate_at,
+    in_value_at,
+    in_state_at,
+    in_step,
+    part_out,
+    norm_gain_out,
+    keep_out,
+    send_out,
     *refs,
 ):
     pieces_out = refs[:side]
@@ -280,10 +296,23 @@
         local_rows,
         shared_rows,
         slabs,
+        in_gate,
+        in_value,
+        in_state,
+        sems,
     ) = refs[side:]
+    weights = [
+        pltpu.make_async_copy(source, target, sems.at[i])
+        for i, (source, target) in enumerate(
+            ((in_gate_at, in_gate), (in_value_at, in_value), (in_state_at, in_state))
+        )
+    ]
 
     @pl.when(pl.program_id(0) == 0)
     def _():
+        for copy in weights:
+            copy.start()
+        norm_gain_out[...] = jnp.zeros_like(norm_gain_out)
         value_buf[ROWS:, :] = jnp.zeros((HALO, value_buf.shape[1]), f32)
         state_buf[ROWS:, :] = jnp.zeros((HALO, state_buf.shape[1]), f32)
         adjoint[...] = jnp.zeros_like(adjoint)
@@ -312,7 +341,6 @@
     grad_gated = scale * (back * gain) - scaled * (scale * scale * moment)
     grad_mixed = grad_gated * silu
     round_gate = (grad_gated * mixed * (bent * (1.0 + pre * (1.0 - bent)))).astype(bf16)
-    gate_out[...] = round_gate
     outgoing = (scaled * gain).astype(bf16)
     width = out_total.shape[2]
     for x in range(side):
@@ -331,9 +359,14 @@
     log_step = step * rate
 
     ahead = iota((Q, Q), 1) >= iota((Q, Q), 0)
-    tri = jnp.where(iota((Q, Q), 0) >= iota((Q, Q), 1), 1.0, 0.0).astype(f32)
-    tri_up = jnp.where(ahead, 1.0, 0.0).astype(f32)
-    tri_strict = jnp.where(iota((Q, Q), 0) > iota((Q, Q), 1), 1.0, 0.0).astype(f32)
+    tri = jnp.where(iota((Q, Q), 0) >= iota((Q, Q), 1), 1.0, 0.0).astype(bf16)
+    tri_both = jnp.concatenate(
+        [
+            jnp.where(ahead, 1.0, 0.0),
+            jnp.where(iota((Q, Q), 0) > iota((Q, Q), 1), 1.0, 0.0),
+        ],
+        axis=1,
+    ).astype(bf16)
     lane = iota((Q, LANES), 1)
     row8 = iota((8, Q), 0)
     channels = heads * HEAD
@@ -353,7 +386,7 @@
         dt = step[rows, :]
         dy = grad_mixed[rows, :]
         dy_low = dy.astype(bf16)
-        decay = mm(tri, log_step[rows, :], precision=exact)
+        decay = sum_rows(tri, log_step[rows, :])
         decay_t = decay.T
         wide = expand(decay, heads)
         dt_wide = expand(dt, heads)
@@ -398,8 +431,10 @@
         )
         row_t = jnp.concatenate([row_sums, jnp.zeros((LANES - 8, Q), f32)], axis=0).T
         grad_log = (
-            mm(tri_up, row_t - direct * dt + grown_sum, precision=exact)
-            + mm(tri_strict, end_sum * dt, precision=exact)
+            sum_rows(
+                tri_both,
+                jnp.concatenate([row_t - direct * dt + grown_sum, end_sum * dt], axis=0),
+            )
             + constant
         )
         grad_step = direct + end_sum + rate * grad_log
@@ -444,9 +479,20 @@
         state_taps_out,
     )
     round_step = jnp.concatenate(grad_step_parts, axis=0).astype(bf16)
-    value_out[...] = round_value
-    state_out[...] = round_state
-    step_out[...] = round_step
+
+    @pl.when(pl.program_id(0) == 0)
+    def _():
+        for copy in weights:
+            copy.wait()
+
+    total = (
+        mm_nt(round_gate, in_gate[...])
+        + mm_nt(round_value, in_value[...])
+        + mm_nt(round_state, in_state[...])
+        + mm(round_step, all_lanes(in_step[...]))
+    )
+    part_out[...] = total.astype(bf16)
+    add_row(norm_gain_out, 0, total * normed[...].astype(f32))
     weight_total[...] += mm_tn(
         normed[...], jnp.concatenate([round_value, round_gate, round_state], axis=1)
     )
@@ -454,6 +500,7 @@
 
     @pl.when(pl.program_id(0) == steps - 1)
     def _():
+        norm_gain_out[...] = norm_gain_out[...] / row_of(norm_gain)
         fold = step_total.shape[1] // channels
         local_rows[...] = jnp.zeros_like(local_rows)
         for h in range(heads):
@@ -498,9 +545,17 @@
                         pl.ds(pl.multiple_of(y * rows, rows), rows),
                         c * channels : (c + 1) * channels,
                     ].astype(bf16)
-                at = 3 * channels
-                piece[j, :, at : at + 2 * STATE] = weight_total[here, 2 * channels :].astype(bf16)
-                piece[j, :, at + 2 * STATE :] = slabs[y * side + x].astype(bf16)
+                piece[j, :, 3 * channels :] = slabs[y * side + x].astype(bf16)
+
+        upper = place[1] == 0
+        tall = keep_out.shape[1]
+        for z in range(4):
+            even = weight_total[2 * z * tall : (2 * z + 1) * tall, 2 * channels :].astype(bf16)
+            odd = weight_total[(2 * z + 1) * tall : (2 * z + 2) * tall, 2 * channels :].astype(
+                bf16
+            )
+            keep_out[z] = jnp.where(upper, even, odd)
+            send_out[z] = jnp.where(upper, odd, even)
 
 
 def block_of(place, first, second):
@@ -512,45 +567,37 @@
     return (LOCAL * channels + SHARED * 2 * STATE) // LANES // pieces
 
 
-def input_kernel(
-    tokens,
-    round_gate,
-    round_value,
-    round_state,
-    round_step,
-    in_gate,
-    in_value,
-    in_state,
-    in_step,
-    part_out,
-    norm_gain_out,
-):
-    @pl.when(pl.program_id(0) == 0)
-    def _():
-        norm_gain_out[...] = jnp.zeros_like(norm_gain_out)
-
-    total = (
-        mm_nt(round_gate[...], in_gate[...])
-        + mm_nt(round_value[...], in_value[...])
-        + mm_nt(round_state[...], in_state[...])
-        + mm(round_step[...], all_lanes(in_step[...]))
-    )
-    part_out[...] = total.astype(bf16)
-    x = tokens[...].astype(f32)
-    x = x * lax.rsqrt(jnp.mean(x * x, axis=1, keepdims=True) + epsilon)
-    add_row(norm_gain_out, 0, total * x)
-
-
-def gather_kernel(index, place, *refs):
-    *pieces, out, sems = refs
-    copies = [
-        pltpu.make_async_copy(piece, out.at[index(place, k)], sems.at[k])
-        for k, piece in enumerate(pieces)
-    ]
-    for copy in copies:
-        copy.start()
-    for copy in copies:
-        copy.wait()
+def line_kernel(place, *refs):
+    *pieces, out = refs
+    side = len(pieces)
+    for k, piece in enumerate(pieces):
+        out[lax.rem(place[4 - place[1]] + side - k, side)] = piece[...]
+
+
+def chip_kernel(place, keep, got, *outs):
+    for k, out in enumerate(outs):
+        z = lax.rem(place[0] + k, 4)
+        out[...] = (keep[z].astype(f32) + got[z].astype(f32)).astype(bf16)
+
+
+def tile_at(t):
+    rows, lanes = 8 * (t // 2), LANES * (t % 2)
+    return slice(rows, rows + 8), slice(lanes, lanes + LANES)
+
+
+def share_kernel(side, place, own, one, two, three, *refs):
+    outs, tiles = refs[:-1], refs[-1]
+    total = total_of((own, one, two, three))
+    count = tiles.shape[0]
+    for t in range(count):
+        tiles[t] = total[tile_at(t)]
+    each = count // side**2
+    for k, out in enumerate(outs):
+        for j in range(side):
+            y, x = block_of(place, lax.rem(place[3 + place[1]] + k, side), j)
+            slab = [tiles[(y * side + x) * each + i] for i in range(each)]
+            below = out.shape[1] - 8 * each
+            out[j] = jnp.concatenate(slab + [jnp.zeros((below, LANES), f32)], axis=0).astype(bf16)
 
 
 def total_of(pieces):
@@ -560,52 +607,42 @@
     return total
 
 
-def line_sum_kernel(place, *refs):
-    side = len(refs) // 2
-    for k, out in enumerate(refs[side:]):
-        at = lax.rem(place[4 - place[1]] + k, side)
-        out[...] = total_of([ref.at[at] for ref in refs[:side]]).astype(bf16)
-
-
-def block_sum_kernel(plain, count, gain_rows, *refs):
-    *pieces, norm_gain, weights_out, rest_out = refs
+def line_sum_kernel(plain, at, place, *refs):
+    side = len(refs) // 3
+    pieces, shares, outs = refs[:side], refs[side : 2 * side], refs[2 * side :]
+    tall = shares[0].shape[1]
+    for k, out in enumerate(outs):
+        j = lax.rem(place[4 - place[1]] + k, side)
+        total = total_of([ref.at[j] for ref in pieces])
+        share = total_of([ref.at[j] for ref in shares])
+        out[:, :plain] = total[:, :plain].astype(bf16)
+        out[:, plain:] = jnp.concatenate(
+            [total[:at, plain:], share, total[at + tall :, plain:]], axis=0
+        ).astype(bf16)
+
+
+def block_sum_kernel(plain, count, gains, *refs):
+    *pieces, norm_gain, out = refs
     total = total_of(pieces)
-    weights_out[...] = total[:, :plain].astype(bf16)
-    rest_out[:, 0 : 2 * STATE] = total[:, plain : plain + 2 * STATE]
-    small = total[:, plain + 2 * STATE :]
-    rest_out[:, 2 * STATE :] = jnp.zeros_like(small)
-    rest_out[0:count, 2 * STATE :] = small[:count, :] + small[count : 2 * count, :]
-    for j in range(norm_gain.shape[1] // LANES):
-        at = gain_rows + j
-        rest_out[at : at + 1, 2 * STATE :] = norm_gain[0:1, j * LANES : (j + 1) * LANES]
-
-
-def block_pack_kernel(local, count, gain_rows, gains, weights, before, own, one, two, three, out):
-    total = (own[...] + two[...]) + (one[...] + three[...])
-    plain = weights.shape[1]
-    out[:, :plain] = weights[...]
-    out[:, plain : plain + 2 * STATE] = total[:, : 2 * STATE].astype(bf16)
-    small = total[:, 2 * STATE :]
-    small = jnp.where(iota(small.shape, 0) < local, before[:, 2 * STATE :], small)
-    high = small.astype(bf16).astype(f32)
-    low = small - high
-    packed = jnp.concatenate(
-        [
-            high[:count, :],
-            low[:count, :],
-            high[gain_rows : gain_rows + gains, :],
-            low[gain_rows : gain_rows + gains, :],
-            jnp.zeros((small.shape[0] - 2 * count - 2 * gains, LANES), f32),
-        ],
-        axis=0,
-    )
-    out[:, plain + 2 * STATE :] = packed.astype(bf16)
-
-
-def unpack_kernel(heads, side, count, gains, place, *refs):
+    out[:, :plain] = total[:, :plain].astype(bf16)
+    small = total[:count, plain:] + total[count : 2 * count, plain:]
+    gain = jnp.concatenate(
+        [norm_gain[0:1, j * LANES : (j + 1) * LANES] for j in range(gains)], axis=0
+    )
+    at = 2 * (count + gains)
+    out[:, plain:] = jnp.concatenate(
+        high_and_low(small) + high_and_low(gain) + [total[at:, plain:]], axis=0
+    ).astype(bf16)
+
+
+def high_and_low(rows):
+    high = rows.astype(bf16).astype(f32)
+    return [high, rows - high]
+
+
+def unpack_kernel(side, place, *refs):
     pieces = refs[:side]
-    value_out, gate_out, out_out, state_out, *small_outs = refs[side:-5]
-    wide, states, small_rows_at, gain_parts, sems = refs[-5:]
+    value_out, gate_out, out_out, wide, sems = refs[side:]
     _, _, tall, channels = wide.shape
     rows, width = out_out.shape[0] // side, out_out.shape[1] // side
     copies = []
@@ -619,8 +656,7 @@
         for j in range(side):
             y, x = block_of(place, first, j)
             at = k * side + j
-            d = y * side + x
-            here = pl.ds(pl.multiple_of(d * tall, tall), tall)
+            here = pl.ds(pl.multiple_of((y * side + x) * tall, tall), tall)
             for c in range(3):
                 wide[at, c] = piece[j, :, c * channels : (c + 1) * channels].astype(f32)
             send(wide.at[at, 0], value_out.at[here])
@@ -633,13 +669,12 @@
                         pl.ds(pl.multiple_of(x * width + c * channels, channels), channels),
                     ],
                 )
-            plain = 3 * channels
-            states[at] = piece[j, :, plain : plain + 2 * STATE].astype(f32)
-            send(states.at[at], state_out.at[here])
-            small = piece[j, :, plain + 2 * STATE :].astype(f32)
-            small_rows_at[d] = small[:count, :] + small[count : 2 * count, :]
-            low = 2 * count + gains
-            gain_parts[d] = small[2 * count : low, :] + small[low : low + gains, :]
+    for copy in copies:
+        copy.wait()
+
+
+def small_kernel(heads, side, count, gains, channels, place, *refs):
+    pieces = refs[:side]
     (
         step_out,
         step_bias_out,
@@ -648,26 +683,35 @@
         value_taps_out,
         value_bias_out,
         gate_gain_out,
-        norm_gain_out,
-        state_taps_out,
-        state_bias_out,
-    ) = small_outs
+        share_out,
+        small_at,
+        gain_at,
+        tiles,
+    ) = refs[side:]
+    each = tiles.shape[0] // side**2
+    for k, piece in enumerate(pieces):
+        first = lax.rem(place[3 + place[1]] + side - k, side)
+        for j in range(side):
+            y, x = block_of(place, first, j)
+            d = y * side + x
+            tile = piece[j, :, piece.shape[2] - LANES :].astype(f32)
+            small_at[d] = tile[:count, :] + tile[count : 2 * count, :]
+            at = 2 * count
+            gain_at[d] = tile[at : at + gains, :] + tile[at + gains : at + 2 * gains, :]
+            at += 2 * gains
+            for i in range(each):
+                tiles[d * each + i] = tile[at + 8 * i : at + 8 * (i + 1), :]
     fold, across = step_out.shape[1] // channels, channels // LANES
     own, ours = LOCAL // side**2, SHARED // side**2
 
     def local(row, tile):
         at = row % own * across + tile
-        return small_rows_at[row // own, at : at + 1, :]
+        return small_at[row // own, at : at + 1, :]
 
     def shared(row, tile):
         at = own * across + row % ours * (2 * STATE // LANES) + tile
-        return small_rows_at[row // ours, at : at + 1, :]
-
-    total = gain_parts[0]
-    for d in range(1, side**2):
-        total = total + gain_parts[d]
-    for t in range(gains):
-        norm_gain_out[t * LANES : (t + 1) * LANES] = total[t, :]
+        return small_at[row // ours, at : at + 1, :]
+
     for h in range(heads):
         for q in range(fold):
             for t in range(across):
@@ -682,13 +726,49 @@
         gate_gain_out[lanes] = local(row + CONV + 1, t)[0]
     for t, out in enumerate((step_bias_out, decay_out, skip_out)):
         out[...] = local(row + CONV + 2, t)[:, :heads]
-    for t in range(2 * STATE // LANES):
-        lanes = slice(t * LANES, (t + 1) * LANES)
-        for k in range(CONV):
-            state_taps_out[k : k + 1, lanes] = shared(k, t)
-        state_bias_out[lanes] = shared(CONV, t)[0]
-    for copy in copies:
-        copy.wait()
+
+    gain = gain_at[0]
+    for d in range(1, side**2):
+        gain = gain + gain_at[d]
+    rows = [gain[t : t + 1, :] for t in range(gains)]
+    rows += [shared(k, t) for k in range(CONV + 1) for t in range(2 * STATE // LANES)]
+    pairs = jnp.concatenate(
+        [jnp.concatenate(rows[i : i + 2], axis=1) for i in range(0, len(rows), 2)], axis=0
+    )
+    below = jnp.zeros((SHARED - pairs.shape[0], 2 * STATE), f32)
+    share = jnp.concatenate(
+        [
+            jnp.concatenate([tiles[t], tiles[t + 1]], axis=1)
+            for t in range(0, tiles.shape[0], 2)
+        ]
+        + [jnp.concatenate([part, below], axis=0) for part in high_and_low(pairs)],
+        axis=0,
+    )
+    share_out[...] = share.astype(bf16)
+
+
+def join_kernel(gains, place, *refs):
+    mine, other = refs[:4], refs[4:8]
+    state_out, norm_gain_out, taps_out, bias_out = refs[8:]
+    tall = state_out.shape[0] // 8
+    sums = []
+    for k in range(4):
+        z = lax.rem(place[0] + 4 - k, 4)
+        small = []
+        for piece, core in ((mine[k], place[1]), (other[k], 1 - place[1])):
+            here = pl.ds(pl.multiple_of((2 * z + core) * tall, tall), tall)
+            state_out[here, :] = piece[:tall, :].astype(f32)
+            small.append(
+                piece[tall : tall + SHARED, :].astype(f32) + piece[tall + SHARED :, :].astype(f32)
+            )
+        sums.append(small[0] + small[1])
+    total = (sums[0] + sums[2]) + (sums[1] + sums[3])
+    wide = total.shape[1]
+    for t in range(gains * LANES // wide):
+        norm_gain_out[t * wide : (t + 1) * wide] = total[t]
+    at = gains * LANES // wide
+    taps_out[...] = total[at : at + CONV, :]
+    bias_out[...] = total[at + CONV]
 
 
 def output_kernel(inner, total, tokens, stats, out):
@@ -760,34 +840,17 @@
         ),
         out_shape=out_shape,
         compiler_params=pltpu.CompilerParams(
-            dimension_semantics=("arbitrary",) * len(grid), vmem_limit_bytes=VMEM
+            dimension_semantics=("arbitrary",) * len(grid), vmem_limit_bytes=SMALL_VMEM
         ),
         cost_estimate=free,
     )(place, *operands)
 
 
+in_vmem = pl.BlockSpec(memory_space=pltpu.VMEM)
+
+
 def fixed(*shape):
     return pl.BlockSpec(shape, lambda *_: (0,) * len(shape))
-
-
-def gather_pieces(place, pieces, index):
-    return at_place(
-        partial(gather_kernel, index),
-        place,
-        pieces,
-        (1,),
-        [fixed(*pieces[0].shape)] * len(pieces),
-        pl.BlockSpec(memory_space=pl.ANY),
-        jax.ShapeDtypeStruct((len(pieces),) + pieces[0].shape, pieces[0].dtype),
-        [pltpu.SemaphoreType.DMA((len(pieces),))],
-    )
-
-
-def along_second(place, pieces):
-    side = len(pieces)
-    return gather_pieces(
-        place, pieces, lambda at, k: lax.rem(at[4 - at[1]] + side - k, side)
-    )
 
 
 def on_device(
@@ -922,9 +985,11 @@
     stats = (stats + moved[1]) + (moved[0] + moved[2])
 
     back_rows = partial(by_rows, steps=steps)
-    lanes = 3 * channels + 2 * STATE + LANES
+    anywhere = pl.BlockSpec(memory_space=pl.ANY)
+    lanes = 3 * channels + LANES
+    share = features // 8
     tall = features // dp
-    round_gate, round_value, round_state, round_step, *weights = pl.pallas_call(
+    part, norm_gain_part, keep, send, *weights = pl.pallas_call(
         partial(backward_kernel, heads, inner, steps, side),
         grid=(steps,),
         in_specs=[
@@ -946,19 +1011,24 @@
             in_scalars(),
             whole(conv_value_kernel),
             whole(conv_state_kernel),
+            whole(norm_gain),
+            anywhere,
+            anywhere,
+            anywhere,
+            whole(step_weight),
         ],
         out_specs=[
-            back_rows(channels),
-            back_rows(channels),
-            back_rows(2 * STATE),
-            back_rows(LANES),
+            back_rows(features),
+            fixed(8, features),
+            fixed(4, share, 2 * STATE),
+            fixed(4, share, 2 * STATE),
         ]
         + [fixed(side, tall, lanes)] * side,
         out_shape=[
-            sds((LEN, channels), bf16),
-            sds((LEN, channels), bf16),
-            sds((LEN, 2 * STATE), bf16),
-            sds((LEN, LANES), bf16),
+            sds((LEN, features), bf16),
+            sds((8, features), f32),
+            sds((4, share, 2 * STATE), bf16),
+            sds((4, share, 2 * STATE), bf16),
         ]
         + [sds((side, tall, lanes), bf16)] * side,
         scratch_shapes=[
@@ -976,6 +1046,10 @@
             pltpu.VMEM((LOCAL, channels), f32),
             pltpu.VMEM((SHARED, 2 * STATE), f32),
             pltpu.VMEM((dp, tall, LANES), f32),
+            pltpu.VMEM((features, channels), bf16),
+            pltpu.VMEM((features, channels), bf16),
+            pltpu.VMEM((features, 2 * STATE), bf16),
+            pltpu.SemaphoreType.DMA((3,)),
         ],
         compiler_params=params,
         cost_estimate=free,
@@ -998,112 +1072,102 @@
         skip_gain,
         conv_value_kernel,
         conv_state_kernel,
-    )
-    out_sum = after(out_sum, round_gate)
-    weights[0] = after(weights[0], out_sum)
-    out_sum = lax.all_gather(out_sum, "tensor", tiled=True)
-
-    weights = [weights[0]] + [
-        move_dp(after(weights[k], weights[0]), k, side, 0) for k in range(1, side)
-    ]
-
-    part, norm_gain_part = pl.pallas_call(
-        input_kernel,
-        grid=(steps,),
-        in_specs=[
-            by_rows(features),
-            by_rows(channels),
-            by_rows(channels),
-            by_rows(2 * STATE),
-            by_rows(LANES),
-            whole(in_gate),
-            whole(in_value),
-            whole(in_state),
-            whole(step_weight),
-        ],
-        out_specs=[
-            by_rows(features),
-            fixed(8, features),
-        ],
-        out_shape=[
-            sds((LEN, features), bf16),
-            sds((8, features), f32),
-        ],
-        compiler_params=params,
-        cost_estimate=free,
-    )(
-        tokens,
-        round_gate,
-        round_value,
-        round_state,
-        round_step,
+        norm_gain,
         in_gate,
         in_value,
         in_state,
         step_weight,
     )
-    weights[0] = after(weights[0], norm_gain_part)
+    out_sum = after(out_sum, part)
+    weights[0] = after(weights[0], out_sum)
+    weights = [weights[0]] + [
+        move_dp(after(weights[k], weights[0]), k, side, 0) for k in range(1, side)
+    ]
+
+    grad_sum = lax.psum_scatter(part, "tensor", scatter_dimension=0, tiled=True)
+
+    got = swap_core(send)
+    shares = at_place(
+        chip_kernel,
+        place,
+        (keep, got),
+        (1,),
+        [in_vmem] * 2,
+        [fixed(share, 2 * STATE)] * 4,
+        [sds((share, 2 * STATE), bf16)] * 4,
+    )
+    tiles = share * 2 * STATE // (8 * LANES)
+    share_tall = -(-tiles * 8 // dp // 16) * 16
+    shares = at_place(
+        partial(share_kernel, side),
+        place,
+        [shares[0]] + [move_z(shares[k], k) for k in (1, 2, 3)],
+        (1,),
+        [in_vmem] * 4,
+        [fixed(side, share_tall, LANES)] * side,
+        [sds((side, share_tall, LANES), bf16)] * side,
+        [pltpu.VMEM((tiles, 8, LANES), f32)],
+    )
+    shares = [shares[0]] + [move_dp(shares[k], k, side, 0) for k in range(1, side)]
+
+    count = small_rows(dp, channels)
+    gains = features // LANES
+    plain = 3 * channels
     weights = at_place(
-        line_sum_kernel,
+        partial(line_sum_kernel, plain, 2 * (count + gains)),
+        place,
+        weights + shares,
+        (1,),
+        [in_vmem] * (2 * side),
+        [fixed(tall, lanes)] * side,
+        [sds((tall, lanes), bf16)] * side,
+    )
+    weights = [weights[0]] + [move_dp(weights[k], k, side, 1) for k in range(1, side)]
+    grad_sum = lax.all_gather(after(grad_sum, weights[1]), "tensor", tiled=True)
+
+
+    vmem = pltpu.CompilerParams(vmem_limit_bytes=SMALL_VMEM)
+    weights = pl.pallas_call(
+        partial(block_sum_kernel, plain, count, gains),
+        in_specs=[in_vmem] * (side + 1),
+        out_shape=sds((tall, lanes), bf16),
+        compiler_params=vmem,
+        cost_estimate=free,
+    )(*weights, norm_gain_part)
+    out_sum = lax.all_gather(after(out_sum, weights), "tensor", tiled=True)
+    weights = [weights] + [move_dp(weights, k, side, 1) for k in range(1, side)]
+    weights = at_place(
+        line_kernel,
         place,
         weights,
         (1,),
-        [fixed(side, tall, lanes)] * side,
-        [fixed(tall, lanes)] * side,
-        [sds((tall, lanes), bf16)] * side,
-    )
-    grad_sum = lax.psum_scatter(
-        after(part, weights[0]), "tensor", scatter_dimension=0, tiled=True
-    )
-    weights = [weights[0]] + [move_dp(weights[k], k, side, 1) for k in range(1, side)]
-
-    block_output = pl.pallas_call(
-        partial(output_kernel, inner),
-        grid=(steps,),
-        in_specs=[by_rows(features), by_rows(features), stats_rows],
-        out_specs=by_rows(features),
-        out_shape=sds((LEN, features), bf16),
-        compiler_params=params,
-        cost_estimate=free,
-    )(after(out_sum, weights[0]), tokens, stats)
-
-    weights[0] = after(weights[0], block_output)
-
-    count = small_rows(dp, channels)
-    local = LOCAL * channels // LANES // dp
-    gains = features // LANES
-    gain_rows = -(-count // 8) * 8
-    plain = 3 * channels
-    vmem = pltpu.CompilerParams(vmem_limit_bytes=VMEM)
-    weights, rest = pl.pallas_call(
-        partial(block_sum_kernel, plain, count, gain_rows),
-        out_shape=[sds((tall, plain), bf16), sds((tall, lanes - plain), f32)],
-        compiler_params=vmem,
-        cost_estimate=free,
-    )(*weights, norm_gain_part)
-    both = rest + swap_core(rest)
-    weights = pl.pallas_call(
-        partial(block_pack_kernel, local, count, gain_rows, gains),
-        out_shape=sds((tall, lanes), bf16),
-        compiler_params=vmem,
-        cost_estimate=free,
-    )(weights, rest, both, *[move_z(both, k) for k in (1, 2, 3)])
-    weights = [weights] + [move_dp(weights, k, side, 1) for k in range(1, side)]
-    weights = along_second(place, weights)
+        [in_vmem] * side,
+        fixed(side, tall, lanes),
+        sds((side, tall, lanes), bf16),
+    )
     weights = [weights] + [move_dp(weights, k, side, 0) for k in range(1, side)]
-    grad_sum = lax.all_gather(after(grad_sum, weights[0]), "tensor", tiled=True)
+    wide = LEN // 2
+    wide_rows = by_rows(features, rows=wide)
     grad_tokens = pl.pallas_call(
         grad_kernel,
-        grid=(steps,),
-        in_specs=[by_rows(features)] * 3 + [whole(norm_gain)],
-        out_specs=by_rows(features),
+        grid=(LEN // wide,),
+        in_specs=[wide_rows] * 3 + [whole(norm_gain)],
+        out_specs=wide_rows,
         out_shape=sds((LEN, features), bf16),
         compiler_params=params,
         cost_estimate=free,
     )(grad_sum, tokens, cotangent, norm_gain)
+    block_output = pl.pallas_call(
+        partial(output_kernel, inner),
+        grid=(LEN // wide,),
+        in_specs=[wide_rows, wide_rows, pl.BlockSpec((8, wide), lambda i: (0, i))],
+        out_specs=wide_rows,
+        out_shape=sds((LEN, features), bf16),
+        compiler_params=params,
+        cost_estimate=free,
+    )(after(out_sum, grad_tokens), tokens, stats)
     weights[0] = after(weights[0], grad_tokens)
 
-    anywhere = pl.BlockSpec(memory_space=pl.ANY)
     smalls = [
         (heads, features),
         (1, heads),
@@ -1112,31 +1176,20 @@
         (CONV, channels),
         (channels,),
         (channels,),
-        (features,),
-        (CONV, 2 * STATE),
-        (2 * STATE,),
     ]
-    across = features // side // channels
-    grad_in_value, grad_in_gate, grad_out_weight, grad_in_state, *smalls = at_place(
-        partial(unpack_kernel, heads, side, count, gains),
+    share_rows = share + 2 * SHARED
+    *smalls, state = at_place(
+        partial(small_kernel, heads, side, count, gains, channels),
         place,
         weights,
         (1,),
-        [fixed(side, tall, lanes)] * side,
-        [anywhere] * 4 + [fixed(*shape) for shape in smalls],
+        [in_vmem] * side,
+        [fixed(*shape) for shape in smalls] + [fixed(share_rows, 2 * STATE)],
+        [sds(shape, f32) for shape in smalls] + [sds((share_rows, 2 * STATE), bf16)],
         [
-            sds((features, channels), f32),
-            sds((features, channels), f32),
-            sds((channels, features), f32),
-            sds((features, 2 * STATE), f32),
-        ]
-        + [sds(shape, f32) for shape in smalls],
-        [
-            pltpu.VMEM((dp, 3, tall, channels), f32),
-            pltpu.VMEM((dp, tall, 2 * STATE), f32),
             pltpu.VMEM((dp, count, LANES), f32),
             pltpu.VMEM((dp, gains, LANES), f32),
-            pltpu.SemaphoreType.DMA((dp * (3 + across),)),
+            pltpu.VMEM((tiles, 8, LANES), f32),
         ],
     )
     grad_in_step = smalls[0].T
@@ -1147,10 +1200,47 @@
         grad_conv_value_kernel,
         grad_conv_value_bias,
         grad_gate_gain,
-        grad_norm_gain,
-        grad_conv_state_kernel,
-        grad_conv_state_bias,
     ) = (a[0] if a.shape[0] == 1 else a for a in smalls[1:])
+    state = [state] + [move_z(state, k) for k in (1, 2, 3)]
+    across = features // side // channels
+    weights[0] = after(weights[0], state[0])
+    grad_in_value, grad_in_gate, grad_out_weight = at_place(
+        partial(unpack_kernel, side),
+        place,
+        weights,
+        (1,),
+        [in_vmem] * side,
+        [anywhere] * 3,
+        [
+            sds((features, channels), f32),
+            sds((features, channels), f32),
+            sds((channels, features), f32),
+        ],
+        [
+            pltpu.VMEM((dp, 3, tall, channels), f32),
+            pltpu.SemaphoreType.DMA((dp * (2 + across),)),
+        ],
+    )
+    state[0] = after(state[0], grad_in_value, block_output)
+    grad_in_state, grad_norm_gain, grad_conv_state_kernel, grad_conv_state_bias = at_place(
+        partial(join_kernel, gains),
+        place,
+        state + [swap_core(piece) for piece in state],
+        (1,),
+        [in_vmem] * 8,
+        [
+            fixed(features, 2 * STATE),
+            fixed(features),
+            fixed(CONV, 2 * STATE),
+            fixed(2 * STATE),
+        ],
+        [
+            sds((features, 2 * STATE), f32),
+            sds((features,), f32),
+            sds((CONV, 2 * STATE), f32),
+            sds((2 * STATE,), f32),
+        ],
+    )
     return (
         block_output,
         grad_tokens,

time: 207 us -> 191 us (0.923); the launches traced: 207 us -> 189 us
  starting transfers between devices: 28.8 us -> 42.5 us
  Pallas kernels: 86 us -> 73.5 us
  waiting for transfers between devices: 67.1 us -> 56.8 us
  local copies, waits for them, and re-layouts: 9.53 us -> 1.31 us
    all_gather x2, waiting for transfers between devices: 26.1 us -> 9.17 us  [the longest x1 5.3 us: on_device(): grad_sum = lax.all_gather(after(grad_sum, weights[1]), 'tensor', tiled=True)]
    pallas_call x5 -> x3, Pallas kernels: 26.3 us -> 11.6 us  [the longest x1 6.86 us: on_device(): pl.pallas_call(grad_kernel, grid=(LEN // wide,), in_specs=[wide_rows] * 3...]
    unnamed x40 -> x14, local copies, waits for them, and re-layouts: 8.85 us -> 0.71 us
    ppermute x6 -> x9, starting transfers between devices: 8.46 us -> 16 us  [move_z(): return lax.ppermute(x, 'tensor', [(i, (i + 2 * k) % 8) for i in range(8)])]
    reduce_scatter x1, waiting for transfers between devices: 0.02 us -> 6.48 us  [on_device(): grad_sum = lax.psum_scatter(part, 'tensor', scatter_dimension=0, tiled=True)]
    ppermute x12 -> x15, starting transfers between devices: 14.4 us -> 20.4 us  [move_dp(): return lax.ppermute(x, ('dp', 'tensor'), pairs)]
    ppermute x6 -> x9, waiting for transfers between devices: 13.1 us -> 7.16 us  [move_z(): return lax.ppermute(x, 'tensor', [(i, (i + 2 * k) % 8) for i in range(8)])]
    pallas_call x1, Pallas kernels: 25.8 us -> 30.9 us  [on_device(): pl.pallas_call(partial(backward_kernel, heads, inner, steps, side), grid=...]
  transfers between devices with their start and end apart: 24 -> 34, of which waited for: 14 -> 23; matrix products, arithmetic and copies ran while one was open for 1% -> 1% of each run, Pallas kernels for 29% -> 28%
where the time goes in v3:
time: 191 us; the launch traced here: 189 us
  Pallas kernels  73.5 us (38%)
  waiting for transfers between devices  56.8 us (30%)
  starting transfers between devices  42.5 us (22%)
  between operations  13.9 us (7%)
    pallas_call x1, Pallas kernels, on_device(): pl.pallas_call(partial(backward_kernel, heads, inner, steps, side), grid=...  30.9 us
    ppermute x15, waiting for transfers between devices, move_dp(): return lax.ppermute(x, ('dp', 'tensor'), pairs)  30.5 us
    ppermute x15, starting transfers between devices, move_dp(): return lax.ppermute(x, ('dp', 'tensor'), pairs)  20.4 us
    pallas_call x1, Pallas kernels, on_device(): pl.pallas_call(partial(forward_kernel, heads), grid=(steps,), in_specs=[b...  18.7 us
    ppermute x9, starting transfers between devices, move_z(): return lax.ppermute(x, 'tensor', [(i, (i + 2 * k) % 8) for i in range(8)])  16 us
    pallas_call x7, Pallas kernels, at_place(): pl.pallas_call(kernel, grid_spec=pltpu.PrefetchScalarGridSpec(num_scalar_...  12.3 us
    ppermute x9, waiting for transfers between devices, move_z(): return lax.ppermute(x, 'tensor', [(i, (i + 2 * k) % 8) for i in range(8)])  7.16 us
    pallas_call x1, Pallas kernels, on_device(): pl.pallas_call(grad_kernel, grid=(LEN // wide,), in_specs=[wide_rows] * 3...  6.86 us
  transfers between devices with their start and end apart: 34, of which 23 were waited for; matrix products, arithmetic and copies ran while one was open for 1% of the time, Pallas kernels for 28%

profile of v3, /device:TPU:1, one launch (start us, length us, event | category | flops | bytes accessed | tf_op | source)
XLA Modules:
  0.0 188.6 jit_solution(7991220969227882258)
XLA Ops:
  7.2 18.7 %shard_map.279 = (bf16[1024,1536]{1,0:T(8,128)(2,1)}, f32[1024,384]{1,0:T(8,128)}, f32[1024,384]{1,0:T(8,128)}, f32[1024,384]{1,0:T(8,128)}, f32[1024,256]{1,0:T...) custom-call(bf16[1024,1536]{1,0:T(8,128)(2,1)} %tokens.5, ...), custom_call_target="tpu_custom_call" | custom-call | tf_op jit(solution)/shard_map/pallas_call | solution.py:907
  26.7 1.4 collective-permute-start
  29.0 3.8 %collective-permute-start.3 = (f32[8,1024]{1,0:T(8,128)S(1)}, f32[8,1024]{1,0:T(8,128)S(1)}, u32[]{:S(2)}, u32[]{:S(2)}) collective-permute-start(f32[8,1024]{1,0:T(8,128)S(1)} %add.27), channel_id=1, source_target_pairs={{0,6},{1,7},{2,0},{3,1},{4,2},{5,3},{6,4},{7,5},{8,14},{9,15},{10,... | collective-permute-start | bytes 98312 | tf_op jit(solution)/shard_map/ppermute | solution.py:808
  34.8 2.1 %collective-permute-done.2 = f32[8,1024]{1,0:T(8,128)S(1)} collective-permute-done((f32[8,1024]{1,0:T(8,128)S(1)}, f32[8,1024]{1,0:T(8,128)S(1)}, u32[]{:S(2)}, u32[]{:S(2)}) %collective-permute-start.2) | collective-permute-done | bytes 32800 | tf_op jit(solution)/shard_map/ppermute | solution.py:808
  37.8 30.9 %shard_map.280 = (bf16[1024,1536]{1,0:T(8,128)(2,1)}, f32[8,1536]{1,0:T(8,128)}, bf16[4,192,256]{2,1,0:T(8,128)(2,1)}, bf16[4,192,256]{2,1,0:T(8,128)(2,1)}, bf1...) custom-call(s32[5]{0:T(128)} %stack.23.place, ...), custom_call_target="tpu_custom_call" | custom-call | tf_op jit(solution)/shard_map/pallas_call | solution.py:992
  70.1 2.4 %collective-permute-start.5 = (bf16[4,96,1280]{2,1,0:T(8,128)(2,1)}, bf16[4,96,1280]{2,1,0:T(8,128)(2,1)S(1)}, u32[]{:S(2)}, u32[]{:S(2)}) collective-permute-start(bf16[4,96,1280]{2,1,0:T(8,128)(2,1)} %get-tuple-element.93), channel_id=1, source_target_pairs={{0,64},{1,17},{2,66},{3,19},{4,68},{5,21},{6,70},{7,23},{8,72},{9,... | collective-permute-start | bytes 2949128 | tf_op jit(solution)/shard_map/ppermute | solution.py:821
  73.7 2.8 %collective-permute-start.7 = (bf16[4,192,256]{2,1,0:T(8,128)(2,1)S(1)}, bf16[4,192,256]{2,1,0:T(8,128)(2,1)S(1)}, u32[]{:S(2)}, u32[]{:S(2)}) collective-permute-start(bf16[4,192,256]{2,1,0:T(8,128)(2,1)S(1)} %copy-done.6), channel_id=1, source_target_pairs={{0,1},{1,0},{2,3},{3,2},{4,5},{5,4},{6,7},{7,6},{8,9},{9,8},{10,11... | collective-permute-start | bytes 1179656 | tf_op jit(solution)/shard_map/ppermute | solution.py:804
  78.8 3.9 %collective-permute-start.9 = (bf16[192,256]{1,0:T(8,128)(2,1)S(1)}, bf16[192,256]{1,0:T(8,128)(2,1)S(1)}, u32[]{:S(2)}, u32[]{:S(2)}) collective-permute-start(bf16[192,256]{1,0:T(8,128)(2,1)S(1)} %get-tuple-element.100), channel_id=1, source_target_pairs={{0,4},{1,5},{2,6},{3,7},{4,0},{5,1},{6,2},{7,3},{8,12},{9,13},{10,... | collective-permute-start | bytes 294920 | tf_op jit(solution)/shard_map/ppermute | solution.py:808
  82.7 2.0 %collective-permute-done.8.one = bf16[192,256]{1,0:T(8,128)(2,1)S(1)} collective-permute-done((bf16[192,256]{1,0:T(8,128)(2,1)S(1)}, bf16[192,256]{1,0:T(8,128)(2,1)S(1)}, u32[]{:S(2)}, u32[]{:S(2)}) %collective-permute-start.8) | collective-permute-done | bytes 98336 | tf_op jit(solution)/shard_map/ppermute | solution.py:808
  84.6 2.4 %collective-permute-start.10 = (bf16[192,256]{1,0:T(8,128)(2,1)S(1)}, bf16[192,256]{1,0:T(8,128)(2,1)S(1)}, u32[]{:S(2)}, u32[]{:S(2)}) collective-permute-start(bf16[192,256]{1,0:T(8,128)(2,1)S(1)} %get-tuple-element.101), channel_id=1, source_target_pairs={{0,6},{1,7},{2,0},{3,1},{4,2},{5,3},{6,4},{7,5},{8,14},{9,15},{10,... | collective-permute-start | bytes 294920 | tf_op jit(solution)/shard_map/ppermute | solution.py:808
  87.1 2.8 %collective-permute-done.9.two = bf16[192,256]{1,0:T(8,128)(2,1)S(1)} collective-permute-done((bf16[192,256]{1,0:T(8,128)(2,1)S(1)}, bf16[192,256]{1,0:T(8,128)(2,1)S(1)}, u32[]{:S(2)}, u32[]{:S(2)}) %collective-permute-start.9) | collective-permute-done | bytes 98336 | tf_op jit(solution)/shard_map/ppermute | solution.py:808
  91.8 2.5 %collective-permute-start.12 = (bf16[4,32,128]{2,1,0:T(8,128)(2,1)S(1)}, bf16[4,32,128]{2,1,0:T(8,128)(2,1)S(1)}, u32[]{:S(2)}, u32[]{:S(2)}) collective-permute-start(bf16[4,32,128]{2,1,0:T(8,128)(2,1)S(1)} %get-tuple-element.104), channel_id=1, source_target_pairs={{0,64},{1,17},{2,66},{3,19},{4,68},{5,21},{6,70},{7,23},{8,72},{9,... | collective-permute-start | bytes 98312 | tf_op jit(solution)/shard_map/ppermute | solution.py:821
  96.4 2.0 %collective-permute-done.13.refs_7_ = bf16[4,32,128]{2,1,0:T(8,128)(2,1)S(1)} collective-permute-done((bf16[4,32,128]{2,1,0:T(8,128)(2,1)S(1)}, bf16[4,32,128]{2,1,0:T(8,128)(2,1)S(1)}, u32[]{:S(2)}, u32[]{:S(2)}) %collective-permute-start.13) | collective-permute-done | bytes 32800 | tf_op jit(solution)/shard_map/ppermute | solution.py:821
  99.5 1.6 collective-permute-start.14
  101.1 6.5 %reduce-scatter.5.cloned.1.call-done = bf16[128,1536]{1,0:T(8,128)(2,1)} async-done(((bf16[1024,1536]{1,0:T(8,128)(2,1)}), bf16[128,1536]{1,0:T(8,128)(2,1)}) %reduce-scatter.5.cloned.1.call-update) | async-done | bytes 393232 | tf_op jit(solution)/shard_map/reduce_scatter | solution.py:1087
  107.6 1.7 collective-permute-start.15
  110.6 3.9 %collective-permute-done.15.refs_2_ = bf16[96,1280]{1,0:T(8,128)(2,1)S(1)} collective-permute-done((bf16[96,1280]{1,0:T(8,128)(2,1)S(1)}, bf16[96,1280]{1,0:T(8,128)(2,1)S(1)}, u32[]{:S(2)}, u32[]{:S(2)}) %collective-permute-start.15) | collective-permute-done | bytes 245792 | tf_op jit(solution)/shard_map/ppermute | solution.py:821
  114.5 2.0 %collective-permute-done.16.refs_3_ = bf16[96,1280]{1,0:T(8,128)(2,1)S(1)} collective-permute-done((bf16[96,1280]{1,0:T(8,128)(2,1)S(1)}, bf16[96,1280]{1,0:T(8,128)(2,1)S(1)}, u32[]{:S(2)}, u32[]{:S(2)}) %collective-permute-start.16) | collective-permute-done | bytes 245792 | tf_op jit(solution)/shard_map/ppermute | solution.py:821
  116.7 2.4 %collective-permute-start.19 = (bf16[96,1280]{1,0:T(8,128)(2,1)S(1)}, bf16[96,1280]{1,0:T(8,128)(2,1)S(1)}, u32[]{:S(2)}, u32[]{:S(2)}) collective-permute-start(bf16[96,1280]{1,0:T(8,128)(2,1)S(1)} %shard_map.284.refs_0_), channel_id=1, source_target_pairs={{0,24},{1,97},{2,26},{3,99},{4,28},{5,101},{6,30},{7,103},{8,0},{9... | collective-permute-start | bytes 737288 | tf_op jit(solution)/shard_map/ppermute | solution.py:821
  119.8 5.1 %collective-permute-done.19.refs_3_ = bf16[96,1280]{1,0:T(8,128)(2,1)S(1)} collective-permute-done((bf16[96,1280]{1,0:T(8,128)(2,1)S(1)}, bf16[96,1280]{1,0:T(8,128)(2,1)S(1)}, u32[]{:S(2)}, u32[]{:S(2)}) %collective-permute-start.19) | collective-permute-done | bytes 245792 | tf_op jit(solution)/shard_map/ppermute | solution.py:821
  125.8 2.9 %collective-permute-done.17.refs_1_ = bf16[96,1280]{1,0:T(8,128)(2,1)S(1)} collective-permute-done((bf16[96,1280]{1,0:T(8,128)(2,1)S(1)}, bf16[96,1280]{1,0:T(8,128)(2,1)S(1)}, u32[]{:S(2)}, u32[]{:S(2)}) %collective-permute-start.17) | collective-permute-done | bytes 245792 | tf_op jit(solution)/shard_map/ppermute | solution.py:821
  129.3 2.3 %collective-permute-start.22 = (bf16[4,96,1280]{2,1,0:T(8,128)(2,1)S(1)}, bf16[4,96,1280]{2,1,0:T(8,128)(2,1)S(1)}, u32[]{:S(2)}, u32[]{:S(2)}) collective-permute-start(bf16[4,96,1280]{2,1,0:T(8,128)(2,1)S(1)} %shard_map.287.refs_0_), channel_id=1, source_target_pairs={{0,96},{1,25},{2,98},{3,27},{4,100},{5,29},{6,102},{7,31},{8,104},... | collective-permute-start | bytes 2949128 | tf_op jit(solution)/shard_map/ppermute | solution.py:821
  132.6 5.3 %all-gather.5.cloned.1.call-done.total = bf16[1024,1536]{1,0:T(8,128)(2,1)} async-done(((bf16[128,1536]{1,0:T(8,128)(2,1)}), bf16[1024,1536]{1,0:T(8,128)(2,1)}) %all-gather.5.cloned.1.call-update) | async-done | bytes 3145744 | tf_op jit(solution)/shard_map/all_gather | solution.py:1126
  137.9 6.9 %shard_map.285 = bf16[1024,1536]{1,0:T(8,128)(2,1)} custom-call(bf16[1024,1536]{1,0:T(8,128)(2,1)} %all-gather.5.cloned.1.call-done.total, bf16[1024,1536]{1,0:T(8,128)(2,1)} %tokens.5, bf16[1024,1536]{1,0:T(8,128)(2,1)} %cotangent.5, f32[1536]{0:T(1024)} %norm_gain.5), custom_call_target="tpu_custom_call" | custom-call | tf_op jit(solution)/shard_map/pallas_call | solution.py:1151
  144.7 8.5 %collective-permute-done.22.refs_3_ = bf16[4,96,1280]{2,1,0:T(8,128)(2,1)S(1)} collective-permute-done((bf16[4,96,1280]{2,1,0:T(8,128)(2,1)S(1)}, bf16[4,96,1280]{2,1,0:T(8,128)(2,1)S(1)}, u32[]{:S(2)}, u32[]{:S(2)}) %collective-permute-start.22) | collective-permute-done | bytes 983072 | tf_op jit(solution)/shard_map/ppermute | solution.py:821
  153.2 3.8 %collective-permute-done.20.refs_1_ = bf16[4,96,1280]{2,1,0:T(8,128)(2,1)} collective-permute-done((bf16[4,96,1280]{2,1,0:T(8,128)(2,1)S(1)}, bf16[4,96,1280]{2,1,0:T(8,128)(2,1)}, u32[]{:S(2)}, u32[]{:S(2)}) %collective-permute-start.20) | collective-permute-done | bytes 983072 | tf_op jit(solution)/shard_map/ppermute | solution.py:821
  157.0 2.5 %shard_map.288 = (f32[6,1536]{1,0:T(8,128)}, f32[1,6]{1,0:T(1,128)}, f32[1,6]{1,0:T(1,128)}, f32[1,6]{1,0:T(1,128)}, f32[4,384]{1,0:T(4,128)}, /*index=5*/f32[38...) custom-call(s32[5]{0:T(128)S(1)} %copy-done.3, bf16[4,96,1280]{2,1,0:T(8,128)(2,1)S(1)} %shard_map.287.refs_0_, ...), custom_call_target="tpu_custom_call" | custom-call | tf_op jit(solution)/shard_map/pallas_call | solution.py:832
  159.5 3.6 %collective-permute-start.25 = (bf16[224,256]{1,0:T(8,128)(2,1)S(1)}, bf16[224,256]{1,0:T(8,128)(2,1)S(1)}, u32[]{:S(2)}, u32[]{:S(2)}) collective-permute-start(bf16[224,256]{1,0:T(8,128)(2,1)S(1)} %get-tuple-element.118.refs_0_), channel_id=1, source_target_pairs={{0,6},{1,7},{2,0},{3,1},{4,2},{5,3},{6,4},{7,5},{8,14},{9,15},{10,... | collective-permute-start | bytes 344072 | tf_op jit(solution)/shard_map/ppermute | solution.py:808
  163.8 3.9 %all-gather.3.cloned.1.call-done.total = bf16[1024,1536]{1,0:T(8,128)(2,1)} async-done(((bf16[128,1536]{1,0:T(8,128)(2,1)}), bf16[1024,1536]{1,0:T(8,128)(2,1)}) %all-gather.3.cloned.1.call-update) | async-done | bytes 3145744 | tf_op jit(solution)/shard_map/all_gather | solution.py:1137
  167.6 4.6 %shard_map.286 = bf16[1024,1536]{1,0:T(8,128)(2,1)} custom-call(bf16[1024,1536]{1,0:T(8,128)(2,1)} %all-gather.3.cloned.1.call-done.total, bf16[1024,1536]{1,0:T(8,128)(2,1)} %tokens.5, f32[8,1024]{1,0:T(8,128)} %add_add_fusion.stats), custom_call_target="tpu_custom_call" | custom-call | tf_op jit(solution)/shard_map/pallas_call | solution.py:1160
  172.3 5.1 %shard_map.289 = (f32[1536,384]{1,0:T(8,128)}, f32[1536,384]{1,0:T(8,128)}, f32[384,1536]{1,0:T(8,128)}) custom-call(s32[5]{0:T(128)S(1)} %copy-done.3, bf16[4,96,1280]{2,1,0:T(8,128)(2,1)S(1)} %shard_map.287.refs_0_, bf16[4,96,1280]{2,1,0:T(8,128)(2,1)} %collective-permute-done.20.refs_1_, bf16[4,96,1280]{2,1,0:T(8,128)(2,1)S(1)} %collective-permute-done.21.refs_2_, ...), custom_call_target="tpu_custom_call" | custom-call | tf_op jit(solution)/shard_map/pallas_call | solution.py:832
  180.3 1.8 shard_map.290
  (69 shorter events, 22.6 us)
Async XLA Ops:
  7.2 61.6 %reduce-scatter.3.cloned.1.call-start = ((), (), s32[]{:S(2)}) async-start(), calls=%async_computation.2 | async-start | bytes 3538944 | tf_op jit(solution)/shard_map/reduce_scatter | solution.py:982
  26.0 81.6 %reduce-scatter.5.cloned.1.call-start = ((), (), s32[]{:S(2)}) async-start(), calls=%async_computation.4 | async-start | bytes 3538944 | tf_op jit(solution)/shard_map/reduce_scatter | solution.py:1087
  26.7 2.3 %collective-permute-start = (f32[8,1024]{1,0:T(8,128)S(1)}, f32[8,1024]{1,0:T(8,128)S(1)}, u32[]{:S(2)}, u32[]{:S(2)}) collective-permute-start(f32[8,1024]{1,0:T(8,128)S(1)} %copy-done.4), channel_id=1, source_target_pairs={{0,1},{1,0},{2,3},{3,2},{4,5},{5,4},{6,7},{7,6},{8,9},{9,8},{10,11... | collective-permute-start | bytes 98312 | tf_op jit(solution)/shard_map/ppermute | solution.py:804
  29.0 5.8 %collective-permute-start.3 = (f32[8,1024]{1,0:T(8,128)S(1)}, f32[8,1024]{1,0:T(8,128)S(1)}, u32[]{:S(2)}, u32[]{:S(2)}) collective-permute-start(f32[8,1024]{1,0:T(8,128)S(1)} %add.27), channel_id=1, source_target_pairs={{0,6},{1,7},{2,0},{3,1},{4,2},{5,3},{6,4},{7,5},{8,14},{9,15},{10,... | collective-permute-start | bytes 98312 | tf_op jit(solution)/shard_map/ppermute | solution.py:808
  32.8 4.0 %collective-permute-start.2 = (f32[8,1024]{1,0:T(8,128)S(1)}, f32[8,1024]{1,0:T(8,128)S(1)}, u32[]{:S(2)}, u32[]{:S(2)}) collective-permute-start(f32[8,1024]{1,0:T(8,128)S(1)} %add.27), channel_id=1, source_target_pairs={{0,2},{1,3},{2,4},{3,5},{4,6},{5,7},{6,0},{7,1},{8,10},{9,11},{10,... | collective-permute-start | bytes 98312 | tf_op jit(solution)/shard_map/ppermute | solution.py:808
  32.8 4.3 %collective-permute-start.1 = (f32[8,1024]{1,0:T(8,128)S(1)}, f32[8,1024]{1,0:T(8,128)S(1)}, u32[]{:S(2)}, u32[]{:S(2)}) collective-permute-start(f32[8,1024]{1,0:T(8,128)S(1)} %add.27), channel_id=1, source_target_pairs={{0,4},{1,5},{2,6},{3,7},{4,0},{5,1},{6,2},{7,3},{8,12},{9,13},{10,... | collective-permute-start | bytes 98312 | tf_op jit(solution)/shard_map/ppermute | solution.py:808
  68.8 69.1 %all-gather.5.cloned.1.call-start = ((), (), s32[]{:S(2)}) async-start(), calls=%async_computation.5 | async-start | bytes 3538944 | tf_op jit(solution)/shard_map/all_gather | solution.py:1126
  68.8 29.6 %collective-permute-start.4 = (bf16[4,96,1280]{2,1,0:T(8,128)(2,1)}, bf16[4,96,1280]{2,1,0:T(8,128)(2,1)S(1)}, u32[]{:S(2)}, u32[]{:S(2)}) collective-permute-start(bf16[4,96,1280]{2,1,0:T(8,128)(2,1)} %get-tuple-element.91), channel_id=1, source_target_pairs={{0,32},{1,9},{2,34},{3,11},{4,36},{5,13},{6,38},{7,15},{8,40},{9,1... | collective-permute-start | bytes 2949128 | tf_op jit(solution)/shard_map/ppermute | solution.py:821
  70.1 28.3 %collective-permute-start.5 = (bf16[4,96,1280]{2,1,0:T(8,128)(2,1)}, bf16[4,96,1280]{2,1,0:T(8,128)(2,1)S(1)}, u32[]{:S(2)}, u32[]{:S(2)}) collective-permute-start(bf16[4,96,1280]{2,1,0:T(8,128)(2,1)} %get-tuple-element.93), channel_id=1, source_target_pairs={{0,64},{1,17},{2,66},{3,19},{4,68},{5,21},{6,70},{7,23},{8,72},{9,... | collective-permute-start | bytes 2949128 | tf_op jit(solution)/shard_map/ppermute | solution.py:821
  72.6 25.9 %collective-permute-start.6 = (bf16[4,96,1280]{2,1,0:T(8,128)(2,1)S(1)}, bf16[4,96,1280]{2,1,0:T(8,128)(2,1)S(1)}, u32[]{:S(2)}, u32[]{:S(2)}) collective-permute-start(bf16[4,96,1280]{2,1,0:T(8,128)(2,1)S(1)} %copy-done.5), channel_id=1, source_target_pairs={{0,96},{1,25},{2,98},{3,27},{4,100},{5,29},{6,102},{7,31},{8,104},... | collective-permute-start | bytes 2949128 | tf_op jit(solution)/shard_map/ppermute | solution.py:821
  73.7 4.1 %collective-permute-start.7 = (bf16[4,192,256]{2,1,0:T(8,128)(2,1)S(1)}, bf16[4,192,256]{2,1,0:T(8,128)(2,1)S(1)}, u32[]{:S(2)}, u32[]{:S(2)}) collective-permute-start(bf16[4,192,256]{2,1,0:T(8,128)(2,1)S(1)} %copy-done.6), channel_id=1, source_target_pairs={{0,1},{1,0},{2,3},{3,2},{4,5},{5,4},{6,7},{7,6},{8,9},{9,8},{10,11... | collective-permute-start | bytes 1179656 | tf_op jit(solution)/shard_map/ppermute | solution.py:804
  78.5 6.1 %collective-permute-start.8 = (bf16[192,256]{1,0:T(8,128)(2,1)S(1)}, bf16[192,256]{1,0:T(8,128)(2,1)S(1)}, u32[]{:S(2)}, u32[]{:S(2)}) collective-permute-start(bf16[192,256]{1,0:T(8,128)(2,1)S(1)} %get-tuple-element.99), channel_id=1, source_target_pairs={{0,2},{1,3},{2,4},{3,5},{4,6},{5,7},{6,0},{7,1},{8,10},{9,11},{10,... | collective-permute-start | bytes 294920 | tf_op jit(solution)/shard_map/ppermute | solution.py:808
  78.8 11.0 %collective-permute-start.9 = (bf16[192,256]{1,0:T(8,128)(2,1)S(1)}, bf16[192,256]{1,0:T(8,128)(2,1)S(1)}, u32[]{:S(2)}, u32[]{:S(2)}) collective-permute-start(bf16[192,256]{1,0:T(8,128)(2,1)S(1)} %get-tuple-element.100), channel_id=1, source_target_pairs={{0,4},{1,5},{2,6},{3,7},{4,0},{5,1},{6,2},{7,3},{8,12},{9,13},{10,... | collective-permute-start | bytes 294920 | tf_op jit(solution)/shard_map/ppermute | solution.py:808
  84.6 5.2 %collective-permute-start.10 = (bf16[192,256]{1,0:T(8,128)(2,1)S(1)}, bf16[192,256]{1,0:T(8,128)(2,1)S(1)}, u32[]{:S(2)}, u32[]{:S(2)}) collective-permute-start(bf16[192,256]{1,0:T(8,128)(2,1)S(1)} %get-tuple-element.101), channel_id=1, source_target_pairs={{0,6},{1,7},{2,0},{3,1},{4,2},{5,3},{6,4},{7,5},{8,14},{9,15},{10,... | collective-permute-start | bytes 294920 | tf_op jit(solution)/shard_map/ppermute | solution.py:808
  90.5 5.1 %collective-permute-start.11 = (bf16[4,32,128]{2,1,0:T(8,128)(2,1)S(1)}, bf16[4,32,128]{2,1,0:T(8,128)(2,1)S(1)}, u32[]{:S(2)}, u32[]{:S(2)}) collective-permute-start(bf16[4,32,128]{2,1,0:T(8,128)(2,1)S(1)} %get-tuple-element.103), channel_id=1, source_target_pairs={{0,32},{1,9},{2,34},{3,11},{4,36},{5,13},{6,38},{7,15},{8,40},{9,1... | collective-permute-start | bytes 98312 | tf_op jit(solution)/shard_map/ppermute | solution.py:821
  91.8 4.6 %collective-permute-start.12 = (bf16[4,32,128]{2,1,0:T(8,128)(2,1)S(1)}, bf16[4,32,128]{2,1,0:T(8,128)(2,1)S(1)}, u32[]{:S(2)}, u32[]{:S(2)}) collective-permute-start(bf16[4,32,128]{2,1,0:T(8,128)(2,1)S(1)} %get-tuple-element.104), channel_id=1, source_target_pairs={{0,64},{1,17},{2,66},{3,19},{4,68},{5,21},{6,70},{7,23},{8,72},{9,... | collective-permute-start | bytes 98312 | tf_op jit(solution)/shard_map/ppermute | solution.py:821
  95.5 2.9 %collective-permute-start.13 = (bf16[4,32,128]{2,1,0:T(8,128)(2,1)S(1)}, bf16[4,32,128]{2,1,0:T(8,128)(2,1)S(1)}, u32[]{:S(2)}, u32[]{:S(2)}) collective-permute-start(bf16[4,32,128]{2,1,0:T(8,128)(2,1)S(1)} %get-tuple-element.105), channel_id=1, source_target_pairs={{0,96},{1,25},{2,98},{3,27},{4,100},{5,29},{6,102},{7,31},{8,104},... | collective-permute-start | bytes 98312 | tf_op jit(solution)/shard_map/ppermute | solution.py:821
  99.5 8.1 %collective-permute-start.14 = (bf16[96,1280]{1,0:T(8,128)(2,1)S(1)}, bf16[96,1280]{1,0:T(8,128)(2,1)S(1)}, u32[]{:S(2)}, u32[]{:S(2)}) collective-permute-start(bf16[96,1280]{1,0:T(8,128)(2,1)S(1)} %get-tuple-element.107), channel_id=1, source_target_pairs={{0,8},{1,33},{2,10},{3,35},{4,12},{5,37},{6,14},{7,39},{8,16},{9,4... | collective-permute-start | bytes 737288 | tf_op jit(solution)/shard_map/ppermute | solution.py:821
  107.6 60.1 %all-gather.3.cloned.1.call-start = ((), (), s32[]{:S(2)}) async-start(), calls=%async_computation.3 | async-start | bytes 3538944 | tf_op jit(solution)/shard_map/all_gather | solution.py:1137
  107.6 6.9 %collective-permute-start.15 = (bf16[96,1280]{1,0:T(8,128)(2,1)S(1)}, bf16[96,1280]{1,0:T(8,128)(2,1)S(1)}, u32[]{:S(2)}, u32[]{:S(2)}) collective-permute-start(bf16[96,1280]{1,0:T(8,128)(2,1)S(1)} %get-tuple-element.108), channel_id=1, source_target_pairs={{0,16},{1,65},{2,18},{3,67},{4,20},{5,69},{6,22},{7,71},{8,24},{9,... | collective-permute-start | bytes 737288 | tf_op jit(solution)/shard_map/ppermute | solution.py:821
  109.3 7.2 %collective-permute-start.16 = (bf16[96,1280]{1,0:T(8,128)(2,1)S(1)}, bf16[96,1280]{1,0:T(8,128)(2,1)S(1)}, u32[]{:S(2)}, u32[]{:S(2)}) collective-permute-start(bf16[96,1280]{1,0:T(8,128)(2,1)S(1)} %get-tuple-element.109), channel_id=1, source_target_pairs={{0,24},{1,97},{2,26},{3,99},{4,28},{5,101},{6,30},{7,103},{8,0},{9... | collective-permute-start | bytes 737288 | tf_op jit(solution)/shard_map/ppermute | solution.py:821
  116.7 8.2 %collective-permute-start.19 = (bf16[96,1280]{1,0:T(8,128)(2,1)S(1)}, bf16[96,1280]{1,0:T(8,128)(2,1)S(1)}, u32[]{:S(2)}, u32[]{:S(2)}) collective-permute-start(bf16[96,1280]{1,0:T(8,128)(2,1)S(1)} %shard_map.284.refs_0_), channel_id=1, source_target_pairs={{0,24},{1,97},{2,26},{3,99},{4,28},{5,101},{6,30},{7,103},{8,0},{9... | collective-permute-start | bytes 737288 | tf_op jit(solution)/shard_map/ppermute | solution.py:821
  119.1 6.7 %collective-permute-start.18 = (bf16[96,1280]{1,0:T(8,128)(2,1)S(1)}, bf16[96,1280]{1,0:T(8,128)(2,1)S(1)}, u32[]{:S(2)}, u32[]{:S(2)}) collective-permute-start(bf16[96,1280]{1,0:T(8,128)(2,1)S(1)} %shard_map.284.refs_0_), channel_id=1, source_target_pairs={{0,16},{1,65},{2,18},{3,67},{4,20},{5,69},{6,22},{7,71},{8,24},{9,... | collective-permute-start | bytes 737288 | tf_op jit(solution)/shard_map/ppermute | solution.py:821
  119.7 9.0 %collective-permute-start.17 = (bf16[96,1280]{1,0:T(8,128)(2,1)S(1)}, bf16[96,1280]{1,0:T(8,128)(2,1)S(1)}, u32[]{:S(2)}, u32[]{:S(2)}) collective-permute-start(bf16[96,1280]{1,0:T(8,128)(2,1)S(1)} %shard_map.284.refs_0_), channel_id=1, source_target_pairs={{0,8},{1,33},{2,10},{3,35},{4,12},{5,37},{6,14},{7,39},{8,16},{9,4... | collective-permute-start | bytes 737288 | tf_op jit(solution)/shard_map/ppermute | solution.py:821
  129.3 23.9 %collective-permute-start.22 = (bf16[4,96,1280]{2,1,0:T(8,128)(2,1)S(1)}, bf16[4,96,1280]{2,1,0:T(8,128)(2,1)S(1)}, u32[]{:S(2)}, u32[]{:S(2)}) collective-permute-start(bf16[4,96,1280]{2,1,0:T(8,128)(2,1)S(1)} %shard_map.287.refs_0_), channel_id=1, source_target_pairs={{0,96},{1,25},{2,98},{3,27},{4,100},{5,29},{6,102},{7,31},{8,104},... | collective-permute-start | bytes 2949128 | tf_op jit(solution)/shard_map/ppermute | solution.py:821
  131.6 21.6 %collective-permute-start.21 = (bf16[4,96,1280]{2,1,0:T(8,128)(2,1)S(1)}, bf16[4,96,1280]{2,1,0:T(8,128)(2,1)S(1)}, u32[]{:S(2)}, u32[]{:S(2)}) collective-permute-start(bf16[4,96,1280]{2,1,0:T(8,128)(2,1)S(1)} %shard_map.287.refs_0_), channel_id=1, source_target_pairs={{0,64},{1,17},{2,66},{3,19},{4,68},{5,21},{6,70},{7,23},{8,72},{9,... | collective-permute-start | bytes 2949128 | tf_op jit(solution)/shard_map/ppermute | solution.py:821
  132.0 25.1 %collective-permute-start.20 = (bf16[4,96,1280]{2,1,0:T(8,128)(2,1)S(1)}, bf16[4,96,1280]{2,1,0:T(8,128)(2,1)}, u32[]{:S(2)}, u32[]{:S(2)}) collective-permute-start(bf16[4,96,1280]{2,1,0:T(8,128)(2,1)S(1)} %shard_map.287.refs_0_), channel_id=1, source_target_pairs={{0,32},{1,9},{2,34},{3,11},{4,36},{5,13},{6,38},{7,15},{8,40},{9,1... | collective-permute-start | bytes 2949128 | tf_op jit(solution)/shard_map/ppermute | solution.py:821
  159.5 18.9 %collective-permute-start.25 = (bf16[224,256]{1,0:T(8,128)(2,1)S(1)}, bf16[224,256]{1,0:T(8,128)(2,1)S(1)}, u32[]{:S(2)}, u32[]{:S(2)}) collective-permute-start(bf16[224,256]{1,0:T(8,128)(2,1)S(1)} %get-tuple-element.118.refs_0_), channel_id=1, source_target_pairs={{0,6},{1,7},{2,0},{3,1},{4,2},{5,3},{6,4},{7,5},{8,14},{9,15},{10,... | collective-permute-start | bytes 344072 | tf_op jit(solution)/shard_map/ppermute | solution.py:808
  163.1 15.5 %collective-permute-start.24 = (bf16[224,256]{1,0:T(8,128)(2,1)S(1)}, bf16[224,256]{1,0:T(8,128)(2,1)S(1)}, u32[]{:S(2)}, u32[]{:S(2)}) collective-permute-start(bf16[224,256]{1,0:T(8,128)(2,1)S(1)} %get-tuple-element.118.refs_0_), channel_id=1, source_target_pairs={{0,4},{1,5},{2,6},{3,7},{4,0},{5,1},{6,2},{7,3},{8,12},{9,13},{10,... | collective-permute-start | bytes 344072 | tf_op jit(solution)/shard_map/ppermute | solution.py:808
  163.1 15.9 %collective-permute-start.23 = (bf16[224,256]{1,0:T(8,128)(2,1)S(1)}, bf16[224,256]{1,0:T(8,128)(2,1)S(1)}, u32[]{:S(2)}, u32[]{:S(2)}) collective-permute-start(bf16[224,256]{1,0:T(8,128)(2,1)S(1)} %get-tuple-element.118.refs_0_), channel_id=1, source_target_pairs={{0,2},{1,3},{2,4},{3,5},{4,6},{5,7},{6,0},{7,1},{8,10},{9,11},{10,... | collective-permute-start | bytes 344072 | tf_op jit(solution)/shard_map/ppermute | solution.py:808
  177.3 2.1 %collective-permute-start.26 = (bf16[224,256]{1,0:T(8,128)(2,1)S(1)}, bf16[224,256]{1,0:T(8,128)(2,1)S(1)}, u32[]{:S(2)}, u32[]{:S(2)}) collective-permute-start(bf16[224,256]{1,0:T(8,128)(2,1)S(1)} %get-tuple-element.118.refs_0_), channel_id=1, source_target_pairs={{0,1},{1,0},{2,3},{3,2},{4,5},{5,4},{6,7},{7,6},{8,9},{9,8},{10,11... | collective-permute-start | bytes 344072 | tf_op jit(solution)/shard_map/ppermute | solution.py:804
  178.6 1.4 collective-permute-start.28
  (9 other events, 87.0 us)
Sparse Core Ops, SparseCore 0:
  26.1 35.8 reduce-scatter.2
  68.9 38.6 reduce-scatter.4
  109.2 28.5 all-gather.4
  139.4 28.1 all-gather.2

commit v4 on v3

--- a/solution.py
+++ b/solution.py
@@ -296,15 +296,18 @@
         local_rows,
         shared_rows,
         slabs,
-        in_gate,
-        in_value,
-        in_state,
+        in_all,
         sems,
     ) = refs[side:]
+    wide = in_gate_at.shape[1]
     weights = [
         pltpu.make_async_copy(source, target, sems.at[i])
         for i, (source, target) in enumerate(
-            ((in_gate_at, in_gate), (in_value_at, in_value), (in_state_at, in_state))
+            (
+                (in_value_at, in_all.at[:, pl.ds(0, wide)]),
+                (in_gate_at, in_all.at[:, pl.ds(wide, wide)]),
+                (in_state_at, in_all.at[:, pl.ds(2 * wide, 2 * STATE)]),
+            )
         )
     ]
 
@@ -343,8 +346,9 @@
     round_gate = (grad_gated * mixed * (bent * (1.0 + pre * (1.0 - bent)))).astype(bf16)
     outgoing = (scaled * gain).astype(bf16)
     width = out_total.shape[2]
+    out_terms = mm_tn(outgoing, cotangent[...])
     for x in range(side):
-        out_total[x] += mm_tn(outgoing, cotangent[:, x * width : (x + 1) * width])
+        out_total[x] += out_terms[:, x * width : (x + 1) * width]
 
     value_at = value_conv[...]
     value_bent = sigmoid(value_at)
@@ -485,17 +489,11 @@
         for copy in weights:
             copy.wait()
 
-    total = (
-        mm_nt(round_gate, in_gate[...])
-        + mm_nt(round_value, in_value[...])
-        + mm_nt(round_state, in_state[...])
-        + mm(round_step, all_lanes(in_step[...]))
-    )
+    rounds = jnp.concatenate([round_value, round_gate, round_state], axis=1)
+    total = mm_nt(rounds, in_all[...]) + mm(round_step, all_lanes(in_step[...]))
     part_out[...] = total.astype(bf16)
     add_row(norm_gain_out, 0, total * normed[...].astype(f32))
-    weight_total[...] += mm_tn(
-        normed[...], jnp.concatenate([round_value, round_gate, round_state], axis=1)
-    )
+    weight_total[...] += mm_tn(normed[...], rounds)
     step_total[...] += mm_tn(round_step, normed[...])
 
     @pl.when(pl.program_id(0) == steps - 1)
@@ -1046,9 +1044,7 @@
             pltpu.VMEM((LOCAL, channels), f32),
             pltpu.VMEM((SHARED, 2 * STATE), f32),
             pltpu.VMEM((dp, tall, LANES), f32),
-            pltpu.VMEM((features, channels), bf16),
-            pltpu.VMEM((features, channels), bf16),
-            pltpu.VMEM((features, 2 * STATE), bf16),
+            pltpu.VMEM((features, 2 * channels + 2 * STATE), bf16),
             pltpu.SemaphoreType.DMA((3,)),
         ],
         compiler_params=params,

time: 191 us -> 189 us (0.990)
  no operation moved by 1% of the time
where the time goes in v4:
time: 189 us; the launch traced here: 187 us
  Pallas kernels  72 us (38%)
  waiting for transfers between devices  56.7 us (30%)
  starting transfers between devices  42.3 us (22%)
  between operations  13.9 us (7%)
    ppermute x15, waiting for transfers between devices, move_dp(): return lax.ppermute(x, ('dp', 'tensor'), pairs)  29.9 us
    pallas_call x1, Pallas kernels, on_device(): pl.pallas_call(partial(backward_kernel, heads, inner, steps, side), grid=...  29.3 us
    ppermute x15, starting transfers between devices, move_dp(): return lax.ppermute(x, ('dp', 'tensor'), pairs)  20.4 us
    pallas_call x1, Pallas kernels, on_device(): pl.pallas_call(partial(forward_kernel, heads), grid=(steps,), in_specs=[b...  18.7 us
    ppermute x9, starting transfers between devices, move_z(): return lax.ppermute(x, 'tensor', [(i, (i + 2 * k) % 8) for i in range(8)])  16 us
    pallas_call x7, Pallas kernels, at_place(): pl.pallas_call(kernel, grid_spec=pltpu.PrefetchScalarGridSpec(num_scalar_...  12.3 us
    ppermute x9, waiting for transfers between devices, move_z(): return lax.ppermute(x, 'tensor', [(i, (i + 2 * k) % 8) for i in range(8)])  7.19 us
    pallas_call x1, Pallas kernels, on_device(): pl.pallas_call(grad_kernel, grid=(LEN // wide,), in_specs=[wide_rows] * 3...  6.86 us
  transfers between devices with their start and end apart: 34, of which 23 were waited for; matrix products, arithmetic and copies ran while one was open for 1% of the time, Pallas kernels for 28%

profile of v4, /device:TPU:1, one launch (start us, length us, event | category | flops | bytes accessed | tf_op | source)
XLA Modules:
  0.0 186.8 jit_solution(16651574791180198108)
XLA Ops:
  7.2 18.7 %shard_map.279 = (bf16[1024,1536]{1,0:T(8,128)(2,1)}, f32[1024,384]{1,0:T(8,128)}, f32[1024,384]{1,0:T(8,128)}, f32[1024,384]{1,0:T(8,128)}, f32[1024,256]{1,0:T...) custom-call(bf16[1024,1536]{1,0:T(8,128)(2,1)} %tokens.5, ...), custom_call_target="tpu_custom_call" | custom-call | tf_op jit(solution)/shard_map/pallas_call | solution.py:905
  26.7 1.4 collective-permute-start
  29.0 3.8 %collective-permute-start.3 = (f32[8,1024]{1,0:T(8,128)S(1)}, f32[8,1024]{1,0:T(8,128)S(1)}, u32[]{:S(2)}, u32[]{:S(2)}) collective-permute-start(f32[8,1024]{1,0:T(8,128)S(1)} %add.27), channel_id=1, source_target_pairs={{0,6},{1,7},{2,0},{3,1},{4,2},{5,3},{6,4},{7,5},{8,14},{9,15},{10,... | collective-permute-start | bytes 98312 | tf_op jit(solution)/shard_map/ppermute | solution.py:806
  34.8 2.1 %collective-permute-done.2 = f32[8,1024]{1,0:T(8,128)S(1)} collective-permute-done((f32[8,1024]{1,0:T(8,128)S(1)}, f32[8,1024]{1,0:T(8,128)S(1)}, u32[]{:S(2)}, u32[]{:S(2)}) %collective-permute-start.2) | collective-permute-done | bytes 32800 | tf_op jit(solution)/shard_map/ppermute | solution.py:806
  37.8 29.3 %shard_map.280 = (bf16[1024,1536]{1,0:T(8,128)(2,1)}, f32[8,1536]{1,0:T(8,128)}, bf16[4,192,256]{2,1,0:T(8,128)(2,1)}, bf16[4,192,256]{2,1,0:T(8,128)(2,1)}, bf1...) custom-call(s32[5]{0:T(128)} %stack.23.place, ...), custom_call_target="tpu_custom_call" | custom-call | tf_op jit(solution)/shard_map/pallas_call | solution.py:990
  68.6 2.4 %collective-permute-start.5 = (bf16[4,96,1280]{2,1,0:T(8,128)(2,1)}, bf16[4,96,1280]{2,1,0:T(8,128)(2,1)S(1)}, u32[]{:S(2)}, u32[]{:S(2)}) collective-permute-start(bf16[4,96,1280]{2,1,0:T(8,128)(2,1)} %get-tuple-element.93), channel_id=1, source_target_pairs={{0,64},{1,17},{2,66},{3,19},{4,68},{5,21},{6,70},{7,23},{8,72},{9,... | collective-permute-start | bytes 2949128 | tf_op jit(solution)/shard_map/ppermute | solution.py:819
  72.2 2.8 %collective-permute-start.7 = (bf16[4,192,256]{2,1,0:T(8,128)(2,1)S(1)}, bf16[4,192,256]{2,1,0:T(8,128)(2,1)S(1)}, u32[]{:S(2)}, u32[]{:S(2)}) collective-permute-start(bf16[4,192,256]{2,1,0:T(8,128)(2,1)S(1)} %copy-done.6), channel_id=1, source_target_pairs={{0,1},{1,0},{2,3},{3,2},{4,5},{5,4},{6,7},{7,6},{8,9},{9,8},{10,11... | collective-permute-start | bytes 1179656 | tf_op jit(solution)/shard_map/ppermute | solution.py:802
  77.3 3.9 %collective-permute-start.9 = (bf16[192,256]{1,0:T(8,128)(2,1)S(1)}, bf16[192,256]{1,0:T(8,128)(2,1)S(1)}, u32[]{:S(2)}, u32[]{:S(2)}) collective-permute-start(bf16[192,256]{1,0:T(8,128)(2,1)S(1)} %get-tuple-element.100), channel_id=1, source_target_pairs={{0,4},{1,5},{2,6},{3,7},{4,0},{5,1},{6,2},{7,3},{8,12},{9,13},{10,... | collective-permute-start | bytes 294920 | tf_op jit(solution)/shard_map/ppermute | solution.py:806
  81.1 2.0 %collective-permute-done.8.one = bf16[192,256]{1,0:T(8,128)(2,1)S(1)} collective-permute-done((bf16[192,256]{1,0:T(8,128)(2,1)S(1)}, bf16[192,256]{1,0:T(8,128)(2,1)S(1)}, u32[]{:S(2)}, u32[]{:S(2)}) %collective-permute-start.8) | collective-permute-done | bytes 98336 | tf_op jit(solution)/shard_map/ppermute | solution.py:806
  83.1 2.4 %collective-permute-start.10 = (bf16[192,256]{1,0:T(8,128)(2,1)S(1)}, bf16[192,256]{1,0:T(8,128)(2,1)S(1)}, u32[]{:S(2)}, u32[]{:S(2)}) collective-permute-start(bf16[192,256]{1,0:T(8,128)(2,1)S(1)} %get-tuple-element.101), channel_id=1, source_target_pairs={{0,6},{1,7},{2,0},{3,1},{4,2},{5,3},{6,4},{7,5},{8,14},{9,15},{10,... | collective-permute-start | bytes 294920 | tf_op jit(solution)/shard_map/ppermute | solution.py:806
  85.5 2.8 %collective-permute-done.9.two = bf16[192,256]{1,0:T(8,128)(2,1)S(1)} collective-permute-done((bf16[192,256]{1,0:T(8,128)(2,1)S(1)}, bf16[192,256]{1,0:T(8,128)(2,1)S(1)}, u32[]{:S(2)}, u32[]{:S(2)}) %collective-permute-start.9) | collective-permute-done | bytes 98336 | tf_op jit(solution)/shard_map/ppermute | solution.py:806
  90.2 2.5 %collective-permute-start.12 = (bf16[4,32,128]{2,1,0:T(8,128)(2,1)S(1)}, bf16[4,32,128]{2,1,0:T(8,128)(2,1)S(1)}, u32[]{:S(2)}, u32[]{:S(2)}) collective-permute-start(bf16[4,32,128]{2,1,0:T(8,128)(2,1)S(1)} %get-tuple-element.104), channel_id=1, source_target_pairs={{0,64},{1,17},{2,66},{3,19},{4,68},{5,21},{6,70},{7,23},{8,72},{9,... | collective-permute-start | bytes 98312 | tf_op jit(solution)/shard_map/ppermute | solution.py:819
  94.8 2.1 %collective-permute-done.13.refs_7_ = bf16[4,32,128]{2,1,0:T(8,128)(2,1)S(1)} collective-permute-done((bf16[4,32,128]{2,1,0:T(8,128)(2,1)S(1)}, bf16[4,32,128]{2,1,0:T(8,128)(2,1)S(1)}, u32[]{:S(2)}, u32[]{:S(2)}) %collective-permute-start.13) | collective-permute-done | bytes 32800 | tf_op jit(solution)/shard_map/ppermute | solution.py:819
  97.9 1.6 collective-permute-start.14
  99.5 6.6 %reduce-scatter.5.cloned.1.call-done = bf16[128,1536]{1,0:T(8,128)(2,1)} async-done(((bf16[1024,1536]{1,0:T(8,128)(2,1)}), bf16[128,1536]{1,0:T(8,128)(2,1)}) %reduce-scatter.5.cloned.1.call-update) | async-done | bytes 393232 | tf_op jit(solution)/shard_map/reduce_scatter | solution.py:1083
  107.3 1.6 collective-permute-start.16
  108.9 3.9 %collective-permute-done.15.refs_2_ = bf16[96,1280]{1,0:T(8,128)(2,1)S(1)} collective-permute-done((bf16[96,1280]{1,0:T(8,128)(2,1)S(1)}, bf16[96,1280]{1,0:T(8,128)(2,1)S(1)}, u32[]{:S(2)}, u32[]{:S(2)}) %collective-permute-start.15) | collective-permute-done | bytes 245792 | tf_op jit(solution)/shard_map/ppermute | solution.py:819
  112.8 1.8 collective-permute-done.16.refs_3_
  114.7 2.5 %collective-permute-start.19 = (bf16[96,1280]{1,0:T(8,128)(2,1)S(1)}, bf16[96,1280]{1,0:T(8,128)(2,1)S(1)}, u32[]{:S(2)}, u32[]{:S(2)}) collective-permute-start(bf16[96,1280]{1,0:T(8,128)(2,1)S(1)} %shard_map.284.refs_0_), channel_id=1, source_target_pairs={{0,24},{1,97},{2,26},{3,99},{4,28},{5,101},{6,30},{7,103},{8,0},{9... | collective-permute-start | bytes 737288 | tf_op jit(solution)/shard_map/ppermute | solution.py:819
  118.0 5.0 %collective-permute-done.19.refs_3_ = bf16[96,1280]{1,0:T(8,128)(2,1)S(1)} collective-permute-done((bf16[96,1280]{1,0:T(8,128)(2,1)S(1)}, bf16[96,1280]{1,0:T(8,128)(2,1)S(1)}, u32[]{:S(2)}, u32[]{:S(2)}) %collective-permute-start.19) | collective-permute-done | bytes 245792 | tf_op jit(solution)/shard_map/ppermute | solution.py:819
  123.9 2.9 %collective-permute-done.17.refs_1_ = bf16[96,1280]{1,0:T(8,128)(2,1)S(1)} collective-permute-done((bf16[96,1280]{1,0:T(8,128)(2,1)S(1)}, bf16[96,1280]{1,0:T(8,128)(2,1)S(1)}, u32[]{:S(2)}, u32[]{:S(2)}) %collective-permute-start.17) | collective-permute-done | bytes 245792 | tf_op jit(solution)/shard_map/ppermute | solution.py:819
  127.4 2.4 %collective-permute-start.22 = (bf16[4,96,1280]{2,1,0:T(8,128)(2,1)S(1)}, bf16[4,96,1280]{2,1,0:T(8,128)(2,1)S(1)}, u32[]{:S(2)}, u32[]{:S(2)}) collective-permute-start(bf16[4,96,1280]{2,1,0:T(8,128)(2,1)S(1)} %shard_map.287.refs_0_), channel_id=1, source_target_pairs={{0,96},{1,25},{2,98},{3,27},{4,100},{5,29},{6,102},{7,31},{8,104},... | collective-permute-start | bytes 2949128 | tf_op jit(solution)/shard_map/ppermute | solution.py:819
  130.8 5.5 %all-gather.5.cloned.1.call-done.total = bf16[1024,1536]{1,0:T(8,128)(2,1)} async-done(((bf16[128,1536]{1,0:T(8,128)(2,1)}), bf16[1024,1536]{1,0:T(8,128)(2,1)}) %all-gather.5.cloned.1.call-update) | async-done | bytes 3145744 | tf_op jit(solution)/shard_map/all_gather | solution.py:1122
  136.3 6.9 %shard_map.285 = bf16[1024,1536]{1,0:T(8,128)(2,1)} custom-call(bf16[1024,1536]{1,0:T(8,128)(2,1)} %all-gather.5.cloned.1.call-done.total, bf16[1024,1536]{1,0:T(8,128)(2,1)} %tokens.5, bf16[1024,1536]{1,0:T(8,128)(2,1)} %cotangent.5, f32[1536]{0:T(1024)} %norm_gain.5), custom_call_target="tpu_custom_call" | custom-call | tf_op jit(solution)/shard_map/pallas_call | solution.py:1147
  143.2 8.2 %collective-permute-done.22.refs_3_ = bf16[4,96,1280]{2,1,0:T(8,128)(2,1)S(1)} collective-permute-done((bf16[4,96,1280]{2,1,0:T(8,128)(2,1)S(1)}, bf16[4,96,1280]{2,1,0:T(8,128)(2,1)S(1)}, u32[]{:S(2)}, u32[]{:S(2)}) %collective-permute-start.22) | collective-permute-done | bytes 983072 | tf_op jit(solution)/shard_map/ppermute | solution.py:819
  151.4 3.8 %collective-permute-done.20.refs_1_ = bf16[4,96,1280]{2,1,0:T(8,128)(2,1)} collective-permute-done((bf16[4,96,1280]{2,1,0:T(8,128)(2,1)S(1)}, bf16[4,96,1280]{2,1,0:T(8,128)(2,1)}, u32[]{:S(2)}, u32[]{:S(2)}) %collective-permute-start.20) | collective-permute-done | bytes 983072 | tf_op jit(solution)/shard_map/ppermute | solution.py:819
  155.2 2.5 %shard_map.288 = (f32[6,1536]{1,0:T(8,128)}, f32[1,6]{1,0:T(1,128)}, f32[1,6]{1,0:T(1,128)}, f32[1,6]{1,0:T(1,128)}, f32[4,384]{1,0:T(4,128)}, /*index=5*/f32[38...) custom-call(s32[5]{0:T(128)S(1)} %copy-done.3, bf16[4,96,1280]{2,1,0:T(8,128)(2,1)S(1)} %shard_map.287.refs_0_, ...), custom_call_target="tpu_custom_call" | custom-call | tf_op jit(solution)/shard_map/pallas_call | solution.py:830
  157.7 3.6 %collective-permute-start.25 = (bf16[224,256]{1,0:T(8,128)(2,1)S(1)}, bf16[224,256]{1,0:T(8,128)(2,1)S(1)}, u32[]{:S(2)}, u32[]{:S(2)}) collective-permute-start(bf16[224,256]{1,0:T(8,128)(2,1)S(1)} %get-tuple-element.118.refs_0_), channel_id=1, source_target_pairs={{0,6},{1,7},{2,0},{3,1},{4,2},{5,3},{6,4},{7,5},{8,14},{9,15},{10,... | collective-permute-start | bytes 344072 | tf_op jit(solution)/shard_map/ppermute | solution.py:806
  162.0 4.1 %all-gather.3.cloned.1.call-done.total = bf16[1024,1536]{1,0:T(8,128)(2,1)} async-done(((bf16[128,1536]{1,0:T(8,128)(2,1)}), bf16[1024,1536]{1,0:T(8,128)(2,1)}) %all-gather.3.cloned.1.call-update) | async-done | bytes 3145744 | tf_op jit(solution)/shard_map/all_gather | solution.py:1133
  166.1 4.6 %shard_map.286 = bf16[1024,1536]{1,0:T(8,128)(2,1)} custom-call(bf16[1024,1536]{1,0:T(8,128)(2,1)} %all-gather.3.cloned.1.call-done.total, bf16[1024,1536]{1,0:T(8,128)(2,1)} %tokens.5, f32[8,1024]{1,0:T(8,128)} %add_add_fusion.stats), custom_call_target="tpu_custom_call" | custom-call | tf_op jit(solution)/shard_map/pallas_call | solution.py:1156
  170.7 5.1 %shard_map.289 = (f32[1536,384]{1,0:T(8,128)}, f32[1536,384]{1,0:T(8,128)}, f32[384,1536]{1,0:T(8,128)}) custom-call(s32[5]{0:T(128)S(1)} %copy-done.3, bf16[4,96,1280]{2,1,0:T(8,128)(2,1)S(1)} %shard_map.287.refs_0_, bf16[4,96,1280]{2,1,0:T(8,128)(2,1)} %collective-permute-done.20.refs_1_, bf16[4,96,1280]{2,1,0:T(8,128)(2,1)S(1)} %collective-permute-done.21.refs_2_, ...), custom_call_target="tpu_custom_call" | custom-call | tf_op jit(solution)/shard_map/pallas_call | solution.py:830
  178.5 1.8 shard_map.290
  (69 shorter events, 22.5 us)
Async XLA Ops:
  7.2 60.1 %reduce-scatter.3.cloned.1.call-start = ((), (), s32[]{:S(2)}) async-start(), calls=%async_computation.2 | async-start | bytes 3538944 | tf_op jit(solution)/shard_map/reduce_scatter | solution.py:980
  26.0 80.1 %reduce-scatter.5.cloned.1.call-start = ((), (), s32[]{:S(2)}) async-start(), calls=%async_computation.4 | async-start | bytes 3538944 | tf_op jit(solution)/shard_map/reduce_scatter | solution.py:1083
  26.7 2.3 %collective-permute-start = (f32[8,1024]{1,0:T(8,128)S(1)}, f32[8,1024]{1,0:T(8,128)S(1)}, u32[]{:S(2)}, u32[]{:S(2)}) collective-permute-start(f32[8,1024]{1,0:T(8,128)S(1)} %copy-done.4), channel_id=1, source_target_pairs={{0,1},{1,0},{2,3},{3,2},{4,5},{5,4},{6,7},{7,6},{8,9},{9,8},{10,11... | collective-permute-start | bytes 98312 | tf_op jit(solution)/shard_map/ppermute | solution.py:802
  29.0 5.8 %collective-permute-start.3 = (f32[8,1024]{1,0:T(8,128)S(1)}, f32[8,1024]{1,0:T(8,128)S(1)}, u32[]{:S(2)}, u32[]{:S(2)}) collective-permute-start(f32[8,1024]{1,0:T(8,128)S(1)} %add.27), channel_id=1, source_target_pairs={{0,6},{1,7},{2,0},{3,1},{4,2},{5,3},{6,4},{7,5},{8,14},{9,15},{10,... | collective-permute-start | bytes 98312 | tf_op jit(solution)/shard_map/ppermute | solution.py:806
  32.8 4.0 %collective-permute-start.2 = (f32[8,1024]{1,0:T(8,128)S(1)}, f32[8,1024]{1,0:T(8,128)S(1)}, u32[]{:S(2)}, u32[]{:S(2)}) collective-permute-start(f32[8,1024]{1,0:T(8,128)S(1)} %add.27), channel_id=1, source_target_pairs={{0,2},{1,3},{2,4},{3,5},{4,6},{5,7},{6,0},{7,1},{8,10},{9,11},{10,... | collective-permute-start | bytes 98312 | tf_op jit(solution)/shard_map/ppermute | solution.py:806
  32.8 4.3 %collective-permute-start.1 = (f32[8,1024]{1,0:T(8,128)S(1)}, f32[8,1024]{1,0:T(8,128)S(1)}, u32[]{:S(2)}, u32[]{:S(2)}) collective-permute-start(f32[8,1024]{1,0:T(8,128)S(1)} %add.27), channel_id=1, source_target_pairs={{0,4},{1,5},{2,6},{3,7},{4,0},{5,1},{6,2},{7,3},{8,12},{9,13},{10,... | collective-permute-start | bytes 98312 | tf_op jit(solution)/shard_map/ppermute | solution.py:806
  67.2 69.1 %all-gather.5.cloned.1.call-start = ((), (), s32[]{:S(2)}) async-start(), calls=%async_computation.5 | async-start | bytes 3538944 | tf_op jit(solution)/shard_map/all_gather | solution.py:1122
  67.3 29.6 %collective-permute-start.4 = (bf16[4,96,1280]{2,1,0:T(8,128)(2,1)}, bf16[4,96,1280]{2,1,0:T(8,128)(2,1)S(1)}, u32[]{:S(2)}, u32[]{:S(2)}) collective-permute-start(bf16[4,96,1280]{2,1,0:T(8,128)(2,1)} %get-tuple-element.91), channel_id=1, source_target_pairs={{0,32},{1,9},{2,34},{3,11},{4,36},{5,13},{6,38},{7,15},{8,40},{9,1... | collective-permute-start | bytes 2949128 | tf_op jit(solution)/shard_map/ppermute | solution.py:819
  68.6 28.3 %collective-permute-start.5 = (bf16[4,96,1280]{2,1,0:T(8,128)(2,1)}, bf16[4,96,1280]{2,1,0:T(8,128)(2,1)S(1)}, u32[]{:S(2)}, u32[]{:S(2)}) collective-permute-start(bf16[4,96,1280]{2,1,0:T(8,128)(2,1)} %get-tuple-element.93), channel_id=1, source_target_pairs={{0,64},{1,17},{2,66},{3,19},{4,68},{5,21},{6,70},{7,23},{8,72},{9,... | collective-permute-start | bytes 2949128 | tf_op jit(solution)/shard_map/ppermute | solution.py:819
  71.0 25.9 %collective-permute-start.6 = (bf16[4,96,1280]{2,1,0:T(8,128)(2,1)S(1)}, bf16[4,96,1280]{2,1,0:T(8,128)(2,1)S(1)}, u32[]{:S(2)}, u32[]{:S(2)}) collective-permute-start(bf16[4,96,1280]{2,1,0:T(8,128)(2,1)S(1)} %copy-done.5), channel_id=1, source_target_pairs={{0,96},{1,25},{2,98},{3,27},{4,100},{5,29},{6,102},{7,31},{8,104},... | collective-permute-start | bytes 2949128 | tf_op jit(solution)/shard_map/ppermute | solution.py:819
  72.2 4.1 %collective-permute-start.7 = (bf16[4,192,256]{2,1,0:T(8,128)(2,1)S(1)}, bf16[4,192,256]{2,1,0:T(8,128)(2,1)S(1)}, u32[]{:S(2)}, u32[]{:S(2)}) collective-permute-start(bf16[4,192,256]{2,1,0:T(8,128)(2,1)S(1)} %copy-done.6), channel_id=1, source_target_pairs={{0,1},{1,0},{2,3},{3,2},{4,5},{5,4},{6,7},{7,6},{8,9},{9,8},{10,11... | collective-permute-start | bytes 1179656 | tf_op jit(solution)/shard_map/ppermute | solution.py:802
  76.9 6.1 %collective-permute-start.8 = (bf16[192,256]{1,0:T(8,128)(2,1)S(1)}, bf16[192,256]{1,0:T(8,128)(2,1)S(1)}, u32[]{:S(2)}, u32[]{:S(2)}) collective-permute-start(bf16[192,256]{1,0:T(8,128)(2,1)S(1)} %get-tuple-element.99), channel_id=1, source_target_pairs={{0,2},{1,3},{2,4},{3,5},{4,6},{5,7},{6,0},{7,1},{8,10},{9,11},{10,... | collective-permute-start | bytes 294920 | tf_op jit(solution)/shard_map/ppermute | solution.py:806
  77.3 11.0 %collective-permute-start.9 = (bf16[192,256]{1,0:T(8,128)(2,1)S(1)}, bf16[192,256]{1,0:T(8,128)(2,1)S(1)}, u32[]{:S(2)}, u32[]{:S(2)}) collective-permute-start(bf16[192,256]{1,0:T(8,128)(2,1)S(1)} %get-tuple-element.100), channel_id=1, source_target_pairs={{0,4},{1,5},{2,6},{3,7},{4,0},{5,1},{6,2},{7,3},{8,12},{9,13},{10,... | collective-permute-start | bytes 294920 | tf_op jit(solution)/shard_map/ppermute | solution.py:806
  83.1 5.2 %collective-permute-start.10 = (bf16[192,256]{1,0:T(8,128)(2,1)S(1)}, bf16[192,256]{1,0:T(8,128)(2,1)S(1)}, u32[]{:S(2)}, u32[]{:S(2)}) collective-permute-start(bf16[192,256]{1,0:T(8,128)(2,1)S(1)} %get-tuple-element.101), channel_id=1, source_target_pairs={{0,6},{1,7},{2,0},{3,1},{4,2},{5,3},{6,4},{7,5},{8,14},{9,15},{10,... | collective-permute-start | bytes 294920 | tf_op jit(solution)/shard_map/ppermute | solution.py:806
  88.9 5.1 %collective-permute-start.11 = (bf16[4,32,128]{2,1,0:T(8,128)(2,1)S(1)}, bf16[4,32,128]{2,1,0:T(8,128)(2,1)S(1)}, u32[]{:S(2)}, u32[]{:S(2)}) collective-permute-start(bf16[4,32,128]{2,1,0:T(8,128)(2,1)S(1)} %get-tuple-element.103), channel_id=1, source_target_pairs={{0,32},{1,9},{2,34},{3,11},{4,36},{5,13},{6,38},{7,15},{8,40},{9,1... | collective-permute-start | bytes 98312 | tf_op jit(solution)/shard_map/ppermute | solution.py:819
  90.2 4.6 %collective-permute-start.12 = (bf16[4,32,128]{2,1,0:T(8,128)(2,1)S(1)}, bf16[4,32,128]{2,1,0:T(8,128)(2,1)S(1)}, u32[]{:S(2)}, u32[]{:S(2)}) collective-permute-start(bf16[4,32,128]{2,1,0:T(8,128)(2,1)S(1)} %get-tuple-element.104), channel_id=1, source_target_pairs={{0,64},{1,17},{2,66},{3,19},{4,68},{5,21},{6,70},{7,23},{8,72},{9,... | collective-permute-start | bytes 98312 | tf_op jit(solution)/shard_map/ppermute | solution.py:819
  94.0 2.9 %collective-permute-start.13 = (bf16[4,32,128]{2,1,0:T(8,128)(2,1)S(1)}, bf16[4,32,128]{2,1,0:T(8,128)(2,1)S(1)}, u32[]{:S(2)}, u32[]{:S(2)}) collective-permute-start(bf16[4,32,128]{2,1,0:T(8,128)(2,1)S(1)} %get-tuple-element.105), channel_id=1, source_target_pairs={{0,96},{1,25},{2,98},{3,27},{4,100},{5,29},{6,102},{7,31},{8,104},... | collective-permute-start | bytes 98312 | tf_op jit(solution)/shard_map/ppermute | solution.py:819
  97.9 8.2 %collective-permute-start.14 = (bf16[96,1280]{1,0:T(8,128)(2,1)S(1)}, bf16[96,1280]{1,0:T(8,128)(2,1)S(1)}, u32[]{:S(2)}, u32[]{:S(2)}) collective-permute-start(bf16[96,1280]{1,0:T(8,128)(2,1)S(1)} %get-tuple-element.107), channel_id=1, source_target_pairs={{0,8},{1,33},{2,10},{3,35},{4,12},{5,37},{6,14},{7,39},{8,16},{9,4... | collective-permute-start | bytes 737288 | tf_op jit(solution)/shard_map/ppermute | solution.py:819
  106.1 60.0 %all-gather.3.cloned.1.call-start = ((), (), s32[]{:S(2)}) async-start(), calls=%async_computation.3 | async-start | bytes 3538944 | tf_op jit(solution)/shard_map/all_gather | solution.py:1133
  106.1 6.6 %collective-permute-start.15 = (bf16[96,1280]{1,0:T(8,128)(2,1)S(1)}, bf16[96,1280]{1,0:T(8,128)(2,1)S(1)}, u32[]{:S(2)}, u32[]{:S(2)}) collective-permute-start(bf16[96,1280]{1,0:T(8,128)(2,1)S(1)} %get-tuple-element.108), channel_id=1, source_target_pairs={{0,16},{1,65},{2,18},{3,67},{4,20},{5,69},{6,22},{7,71},{8,24},{9,... | collective-permute-start | bytes 737288 | tf_op jit(solution)/shard_map/ppermute | solution.py:819
  107.3 7.2 %collective-permute-start.16 = (bf16[96,1280]{1,0:T(8,128)(2,1)S(1)}, bf16[96,1280]{1,0:T(8,128)(2,1)S(1)}, u32[]{:S(2)}, u32[]{:S(2)}) collective-permute-start(bf16[96,1280]{1,0:T(8,128)(2,1)S(1)} %get-tuple-element.109), channel_id=1, source_target_pairs={{0,24},{1,97},{2,26},{3,99},{4,28},{5,101},{6,30},{7,103},{8,0},{9... | collective-permute-start | bytes 737288 | tf_op jit(solution)/shard_map/ppermute | solution.py:819
  114.7 8.2 %collective-permute-start.19 = (bf16[96,1280]{1,0:T(8,128)(2,1)S(1)}, bf16[96,1280]{1,0:T(8,128)(2,1)S(1)}, u32[]{:S(2)}, u32[]{:S(2)}) collective-permute-start(bf16[96,1280]{1,0:T(8,128)(2,1)S(1)} %shard_map.284.refs_0_), channel_id=1, source_target_pairs={{0,24},{1,97},{2,26},{3,99},{4,28},{5,101},{6,30},{7,103},{8,0},{9... | collective-permute-start | bytes 737288 | tf_op jit(solution)/shard_map/ppermute | solution.py:819
  117.2 6.7 %collective-permute-start.18 = (bf16[96,1280]{1,0:T(8,128)(2,1)S(1)}, bf16[96,1280]{1,0:T(8,128)(2,1)S(1)}, u32[]{:S(2)}, u32[]{:S(2)}) collective-permute-start(bf16[96,1280]{1,0:T(8,128)(2,1)S(1)} %shard_map.284.refs_0_), channel_id=1, source_target_pairs={{0,16},{1,65},{2,18},{3,67},{4,20},{5,69},{6,22},{7,71},{8,24},{9,... | collective-permute-start | bytes 737288 | tf_op jit(solution)/shard_map/ppermute | solution.py:819
  118.0 8.8 %collective-permute-start.17 = (bf16[96,1280]{1,0:T(8,128)(2,1)S(1)}, bf16[96,1280]{1,0:T(8,128)(2,1)S(1)}, u32[]{:S(2)}, u32[]{:S(2)}) collective-permute-start(bf16[96,1280]{1,0:T(8,128)(2,1)S(1)} %shard_map.284.refs_0_), channel_id=1, source_target_pairs={{0,8},{1,33},{2,10},{3,35},{4,12},{5,37},{6,14},{7,39},{8,16},{9,4... | collective-permute-start | bytes 737288 | tf_op jit(solution)/shard_map/ppermute | solution.py:819
  127.4 24.0 %collective-permute-start.22 = (bf16[4,96,1280]{2,1,0:T(8,128)(2,1)S(1)}, bf16[4,96,1280]{2,1,0:T(8,128)(2,1)S(1)}, u32[]{:S(2)}, u32[]{:S(2)}) collective-permute-start(bf16[4,96,1280]{2,1,0:T(8,128)(2,1)S(1)} %shard_map.287.refs_0_), channel_id=1, source_target_pairs={{0,96},{1,25},{2,98},{3,27},{4,100},{5,29},{6,102},{7,31},{8,104},... | collective-permute-start | bytes 2949128 | tf_op jit(solution)/shard_map/ppermute | solution.py:819
  129.8 21.6 %collective-permute-start.21 = (bf16[4,96,1280]{2,1,0:T(8,128)(2,1)S(1)}, bf16[4,96,1280]{2,1,0:T(8,128)(2,1)S(1)}, u32[]{:S(2)}, u32[]{:S(2)}) collective-permute-start(bf16[4,96,1280]{2,1,0:T(8,128)(2,1)S(1)} %shard_map.287.refs_0_), channel_id=1, source_target_pairs={{0,64},{1,17},{2,66},{3,19},{4,68},{5,21},{6,70},{7,23},{8,72},{9,... | collective-permute-start | bytes 2949128 | tf_op jit(solution)/shard_map/ppermute | solution.py:819
  130.2 25.0 %collective-permute-start.20 = (bf16[4,96,1280]{2,1,0:T(8,128)(2,1)S(1)}, bf16[4,96,1280]{2,1,0:T(8,128)(2,1)}, u32[]{:S(2)}, u32[]{:S(2)}) collective-permute-start(bf16[4,96,1280]{2,1,0:T(8,128)(2,1)S(1)} %shard_map.287.refs_0_), channel_id=1, source_target_pairs={{0,32},{1,9},{2,34},{3,11},{4,36},{5,13},{6,38},{7,15},{8,40},{9,1... | collective-permute-start | bytes 2949128 | tf_op jit(solution)/shard_map/ppermute | solution.py:819
  157.7 19.0 %collective-permute-start.25 = (bf16[224,256]{1,0:T(8,128)(2,1)S(1)}, bf16[224,256]{1,0:T(8,128)(2,1)S(1)}, u32[]{:S(2)}, u32[]{:S(2)}) collective-permute-start(bf16[224,256]{1,0:T(8,128)(2,1)S(1)} %get-tuple-element.118.refs_0_), channel_id=1, source_target_pairs={{0,6},{1,7},{2,0},{3,1},{4,2},{5,3},{6,4},{7,5},{8,14},{9,15},{10,... | collective-permute-start | bytes 344072 | tf_op jit(solution)/shard_map/ppermute | solution.py:806
  161.3 15.4 %collective-permute-start.24 = (bf16[224,256]{1,0:T(8,128)(2,1)S(1)}, bf16[224,256]{1,0:T(8,128)(2,1)S(1)}, u32[]{:S(2)}, u32[]{:S(2)}) collective-permute-start(bf16[224,256]{1,0:T(8,128)(2,1)S(1)} %get-tuple-element.118.refs_0_), channel_id=1, source_target_pairs={{0,4},{1,5},{2,6},{3,7},{4,0},{5,1},{6,2},{7,3},{8,12},{9,13},{10,... | collective-permute-start | bytes 344072 | tf_op jit(solution)/shard_map/ppermute | solution.py:806
  161.3 15.8 %collective-permute-start.23 = (bf16[224,256]{1,0:T(8,128)(2,1)S(1)}, bf16[224,256]{1,0:T(8,128)(2,1)S(1)}, u32[]{:S(2)}, u32[]{:S(2)}) collective-permute-start(bf16[224,256]{1,0:T(8,128)(2,1)S(1)} %get-tuple-element.118.refs_0_), channel_id=1, source_target_pairs={{0,2},{1,3},{2,4},{3,5},{4,6},{5,7},{6,0},{7,1},{8,10},{9,11},{10,... | collective-permute-start | bytes 344072 | tf_op jit(solution)/shard_map/ppermute | solution.py:806
  175.8 1.9 %collective-permute-start.26 = (bf16[224,256]{1,0:T(8,128)(2,1)S(1)}, bf16[224,256]{1,0:T(8,128)(2,1)S(1)}, u32[]{:S(2)}, u32[]{:S(2)}) collective-permute-start(bf16[224,256]{1,0:T(8,128)(2,1)S(1)} %get-tuple-element.118.refs_0_), channel_id=1, source_target_pairs={{0,1},{1,0},{2,3},{3,2},{4,5},{5,4},{6,7},{7,6},{8,9},{9,8},{10,11... | collective-permute-start | bytes 344072 | tf_op jit(solution)/shard_map/ppermute | solution.py:802
  176.8 1.4 collective-permute-start.28
  (9 other events, 86.6 us)
Sparse Core Ops, SparseCore 0:
  26.1 35.8 reduce-scatter.2
  67.3 38.7 reduce-scatter.4
  107.8 28.4 all-gather.4
  137.8 28.1 all-gather.2

commit v5 on v4

--- a/solution.py
+++ b/solution.py
@@ -638,9 +638,9 @@
     return [high, rows - high]
 
 
-def unpack_kernel(side, place, *refs):
-    pieces = refs[:side]
-    value_out, gate_out, out_out, wide, sems = refs[side:]
+def unpack_kernel(side, steps_back, place, *refs):
+    pieces = refs[: len(steps_back)]
+    value_out, gate_out, out_out, wide, sems = refs[-5:]
     _, _, tall, channels = wide.shape
     rows, width = out_out.shape[0] // side, out_out.shape[1] // side
     copies = []
@@ -650,7 +650,7 @@
         copies[-1].start()
 
     for k, piece in enumerate(pieces):
-        first = lax.rem(place[3 + place[1]] + side - k, side)
+        first = lax.rem(place[3 + place[1]] + side - steps_back[k], side)
         for j in range(side):
             y, x = block_of(place, first, j)
             at = k * side + j
@@ -826,7 +826,9 @@
 free = pl.CostEstimate(flops=0, bytes_accessed=0, transcendentals=0)
 
 
-def at_place(kernel, place, operands, grid, in_specs, out_specs, out_shape, scratch=()):
+def at_place(
+    kernel, place, operands, grid, in_specs, out_specs, out_shape, scratch=(), aliases=None
+):
     return pl.pallas_call(
         kernel,
         grid_spec=pltpu.PrefetchScalarGridSpec(
@@ -840,6 +842,7 @@
         compiler_params=pltpu.CompilerParams(
             dimension_semantics=("arbitrary",) * len(grid), vmem_limit_bytes=SMALL_VMEM
         ),
+        input_output_aliases=aliases or {},
         cost_estimate=free,
     )(place, *operands)
 
@@ -1162,7 +1165,34 @@
         compiler_params=params,
         cost_estimate=free,
     )(after(out_sum, grad_tokens), tokens, stats)
-    weights[0] = after(weights[0], grad_tokens)
+    across = features // side // channels
+
+    def unpack(steps_back, *operands):
+        count = len(steps_back)
+        shapes = [
+            sds((features, channels), f32),
+            sds((features, channels), f32),
+            sds((channels, features), f32),
+        ]
+        return at_place(
+            partial(unpack_kernel, side, steps_back),
+            place,
+            operands,
+            (1,),
+            [in_vmem] * count + [anywhere] * (len(operands) - count),
+            [anywhere] * 3,
+            shapes,
+            [
+                pltpu.VMEM((count * side, 3, tall, channels), f32),
+                pltpu.SemaphoreType.DMA((count * side * (2 + across),)),
+            ],
+            {1 + count + i: i for i in range(len(operands) - count)},
+        )
+
+    unpacked = unpack([0], after(weights[0], grad_tokens))
+    others = list(range(2, side))
+    unpacked = unpack(others, *[weights[k] for k in others], *unpacked)
+    weights[1] = after(weights[1], unpacked[0])
 
     smalls = [
         (heads, features),
@@ -1198,24 +1228,8 @@
         grad_gate_gain,
     ) = (a[0] if a.shape[0] == 1 else a for a in smalls[1:])
     state = [state] + [move_z(state, k) for k in (1, 2, 3)]
-    across = features // side // channels
-    weights[0] = after(weights[0], state[0])
-    grad_in_value, grad_in_gate, grad_out_weight = at_place(
-        partial(unpack_kernel, side),
-        place,
-        weights,
-        (1,),
-        [in_vmem] * side,
-        [anywhere] * 3,
-        [
-            sds((features, channels), f32),
-            sds((features, channels), f32),
-            sds((channels, features), f32),
-        ],
-        [
-            pltpu.VMEM((dp, 3, tall, channels), f32),
-            pltpu.SemaphoreType.DMA((dp * (2 + across),)),
-        ],
+    grad_in_value, grad_in_gate, grad_out_weight = unpack(
+        [1], after(weights[1], state[0]), *unpacked
     )
     state[0] = after(state[0], grad_in_value, block_output)
     grad_in_state, grad_norm_gain, grad_conv_state_kernel, grad_conv_state_bias = at_place(

time: 189 us -> 187 us (0.989)
  waiting for transfers between devices: 56.7 us -> 52.4 us
  Pallas kernels: 72 us -> 74.4 us
    ppermute x15, waiting for transfers between devices: 29.9 us -> 25.6 us  [move_dp(): return lax.ppermute(x, ('dp', 'tensor'), pairs)]
    pallas_call x7 -> x9, Pallas kernels: 12.3 us -> 14.7 us  [at_place(): pl.pallas_call(kernel, grid_spec=pltpu.PrefetchScalarGridSpec(num_scalar_...]
  transfers between devices with their start and end apart: 34 -> 34, of which waited for: 23 -> 23; matrix products, arithmetic and copies ran while one was open for 1% -> 1% of each run, Pallas kernels for 28% -> 29%
where the time goes in v5:
time: 187 us; the launch traced here: 185 us
  Pallas kernels  74.4 us (40%)
  waiting for transfers between devices  52.4 us (28%)
  starting transfers between devices  42.1 us (23%)
  between operations  13.9 us (7%)
    pallas_call x1, Pallas kernels, on_device(): pl.pallas_call(partial(backward_kernel, heads, inner, steps, side), grid=...  29.3 us
    ppermute x15, waiting for transfers between devices, move_dp(): return lax.ppermute(x, ('dp', 'tensor'), pairs)  25.6 us
    ppermute x15, starting transfers between devices, move_dp(): return lax.ppermute(x, ('dp', 'tensor'), pairs)  20.3 us
    pallas_call x1, Pallas kernels, on_device(): pl.pallas_call(partial(forward_kernel, heads), grid=(steps,), in_specs=[b...  18.7 us
    ppermute x9, starting transfers between devices, move_z(): return lax.ppermute(x, 'tensor', [(i, (i + 2 * k) % 8) for i in range(8)])  16 us
    pallas_call x9, Pallas kernels, at_place(): pl.pallas_call(kernel, grid_spec=pltpu.PrefetchScalarGridSpec(num_scalar_...  14.7 us
    ppermute x9, waiting for transfers between devices, move_z(): return lax.ppermute(x, 'tensor', [(i, (i + 2 * k) % 8) for i in range(8)])  7.16 us
    pallas_call x1, Pallas kernels, on_device(): pl.pallas_call(grad_kernel, grid=(LEN // wide,), in_specs=[wide_rows] * 3...  6.88 us
  transfers between devices with their start and end apart: 34, of which 23 were waited for; matrix products, arithmetic and copies ran while one was open for 1% of the time, Pallas kernels for 29%

profile of v5, /device:TPU:1, one launch (start us, length us, event | category | flops | bytes accessed | tf_op | source)
XLA Modules:
  0.0 184.8 jit_solution(10852115432250077852)
XLA Ops:
  7.2 18.7 %shard_map.279 = (bf16[1024,1536]{1,0:T(8,128)(2,1)}, f32[1024,384]{1,0:T(8,128)}, f32[1024,384]{1,0:T(8,128)}, f32[1024,384]{1,0:T(8,128)}, f32[1024,256]{1,0:T...) custom-call(bf16[1024,1536]{1,0:T(8,128)(2,1)} %tokens.5, ...), custom_call_target="tpu_custom_call" | custom-call | tf_op jit(solution)/shard_map/pallas_call | solution.py:908
  29.0 3.8 %collective-permute-start.3 = (f32[8,1024]{1,0:T(8,128)S(1)}, f32[8,1024]{1,0:T(8,128)S(1)}, u32[]{:S(2)}, u32[]{:S(2)}) collective-permute-start(f32[8,1024]{1,0:T(8,128)S(1)} %add.27), channel_id=1, source_target_pairs={{0,6},{1,7},{2,0},{3,1},{4,2},{5,3},{6,4},{7,5},{8,14},{9,15},{10,... | collective-permute-start | bytes 98312 | tf_op jit(solution)/shard_map/ppermute | solution.py:806
  34.8 2.1 %collective-permute-done.2 = f32[8,1024]{1,0:T(8,128)S(1)} collective-permute-done((f32[8,1024]{1,0:T(8,128)S(1)}, f32[8,1024]{1,0:T(8,128)S(1)}, u32[]{:S(2)}, u32[]{:S(2)}) %collective-permute-start.2) | collective-permute-done | bytes 32800 | tf_op jit(solution)/shard_map/ppermute | solution.py:806
  37.8 29.3 %shard_map.280 = (bf16[1024,1536]{1,0:T(8,128)(2,1)}, f32[8,1536]{1,0:T(8,128)}, bf16[4,192,256]{2,1,0:T(8,128)(2,1)}, bf16[4,192,256]{2,1,0:T(8,128)(2,1)}, bf1...) custom-call(s32[5]{0:T(128)} %stack.23.place, ...), custom_call_target="tpu_custom_call" | custom-call | tf_op jit(solution)/shard_map/pallas_call | solution.py:993
  68.6 2.4 %collective-permute-start.5 = (bf16[4,96,1280]{2,1,0:T(8,128)(2,1)}, bf16[4,96,1280]{2,1,0:T(8,128)(2,1)S(1)}, u32[]{:S(2)}, u32[]{:S(2)}) collective-permute-start(bf16[4,96,1280]{2,1,0:T(8,128)(2,1)} %get-tuple-element.100), channel_id=1, source_target_pairs={{0,64},{1,17},{2,66},{3,19},{4,68},{5,21},{6,70},{7,23},{8,72},{9,... | collective-permute-start | bytes 2949128 | tf_op jit(solution)/shard_map/ppermute | solution.py:819
  72.2 2.8 %collective-permute-start.7 = (bf16[4,192,256]{2,1,0:T(8,128)(2,1)S(1)}, bf16[4,192,256]{2,1,0:T(8,128)(2,1)S(1)}, u32[]{:S(2)}, u32[]{:S(2)}) collective-permute-start(bf16[4,192,256]{2,1,0:T(8,128)(2,1)S(1)} %copy-done.6), channel_id=1, source_target_pairs={{0,1},{1,0},{2,3},{3,2},{4,5},{5,4},{6,7},{7,6},{8,9},{9,8},{10,11... | collective-permute-start | bytes 1179656 | tf_op jit(solution)/shard_map/ppermute | solution.py:802
  77.2 3.9 %collective-permute-start.9 = (bf16[192,256]{1,0:T(8,128)(2,1)S(1)}, bf16[192,256]{1,0:T(8,128)(2,1)S(1)}, u32[]{:S(2)}, u32[]{:S(2)}) collective-permute-start(bf16[192,256]{1,0:T(8,128)(2,1)S(1)} %get-tuple-element.107), channel_id=1, source_target_pairs={{0,4},{1,5},{2,6},{3,7},{4,0},{5,1},{6,2},{7,3},{8,12},{9,13},{10,... | collective-permute-start | bytes 294920 | tf_op jit(solution)/shard_map/ppermute | solution.py:806
  81.1 2.0 %collective-permute-done.8.one = bf16[192,256]{1,0:T(8,128)(2,1)S(1)} collective-permute-done((bf16[192,256]{1,0:T(8,128)(2,1)S(1)}, bf16[192,256]{1,0:T(8,128)(2,1)S(1)}, u32[]{:S(2)}, u32[]{:S(2)}) %collective-permute-start.8) | collective-permute-done | bytes 98336 | tf_op jit(solution)/shard_map/ppermute | solution.py:806
  83.0 2.4 %collective-permute-start.10 = (bf16[192,256]{1,0:T(8,128)(2,1)S(1)}, bf16[192,256]{1,0:T(8,128)(2,1)S(1)}, u32[]{:S(2)}, u32[]{:S(2)}) collective-permute-start(bf16[192,256]{1,0:T(8,128)(2,1)S(1)} %get-tuple-element.108), channel_id=1, source_target_pairs={{0,6},{1,7},{2,0},{3,1},{4,2},{5,3},{6,4},{7,5},{8,14},{9,15},{10,... | collective-permute-start | bytes 294920 | tf_op jit(solution)/shard_map/ppermute | solution.py:806
  85.5 2.8 %collective-permute-done.9.two = bf16[192,256]{1,0:T(8,128)(2,1)S(1)} collective-permute-done((bf16[192,256]{1,0:T(8,128)(2,1)S(1)}, bf16[192,256]{1,0:T(8,128)(2,1)S(1)}, u32[]{:S(2)}, u32[]{:S(2)}) %collective-permute-start.9) | collective-permute-done | bytes 98336 | tf_op jit(solution)/shard_map/ppermute | solution.py:806
  90.2 2.5 %collective-permute-start.12 = (bf16[4,32,128]{2,1,0:T(8,128)(2,1)S(1)}, bf16[4,32,128]{2,1,0:T(8,128)(2,1)S(1)}, u32[]{:S(2)}, u32[]{:S(2)}) collective-permute-start(bf16[4,32,128]{2,1,0:T(8,128)(2,1)S(1)} %get-tuple-element.111), channel_id=1, source_target_pairs={{0,64},{1,17},{2,66},{3,19},{4,68},{5,21},{6,70},{7,23},{8,72},{9,... | collective-permute-start | bytes 98312 | tf_op jit(solution)/shard_map/ppermute | solution.py:819
  94.8 2.0 %collective-permute-done.13.refs_7_ = bf16[4,32,128]{2,1,0:T(8,128)(2,1)S(1)} collective-permute-done((bf16[4,32,128]{2,1,0:T(8,128)(2,1)S(1)}, bf16[4,32,128]{2,1,0:T(8,128)(2,1)S(1)}, u32[]{:S(2)}, u32[]{:S(2)}) %collective-permute-start.13) | collective-permute-done | bytes 32800 | tf_op jit(solution)/shard_map/ppermute | solution.py:819
  97.9 1.6 collective-permute-start.14
  99.5 6.6 %reduce-scatter.5.cloned.1.call-done = bf16[128,1536]{1,0:T(8,128)(2,1)} async-done(((bf16[1024,1536]{1,0:T(8,128)(2,1)}), bf16[128,1536]{1,0:T(8,128)(2,1)}) %reduce-scatter.5.cloned.1.call-update) | async-done | bytes 393232 | tf_op jit(solution)/shard_map/reduce_scatter | solution.py:1086
  107.3 1.5 collective-permute-start.16
  108.8 3.9 %collective-permute-done.15.refs_2_ = bf16[96,1280]{1,0:T(8,128)(2,1)S(1)} collective-permute-done((bf16[96,1280]{1,0:T(8,128)(2,1)S(1)}, bf16[96,1280]{1,0:T(8,128)(2,1)S(1)}, u32[]{:S(2)}, u32[]{:S(2)}) %collective-permute-start.15) | collective-permute-done | bytes 245792 | tf_op jit(solution)/shard_map/ppermute | solution.py:819
  112.7 1.8 collective-permute-done.16.refs_3_
  114.7 2.5 %collective-permute-start.19 = (bf16[96,1280]{1,0:T(8,128)(2,1)S(1)}, bf16[96,1280]{1,0:T(8,128)(2,1)S(1)}, u32[]{:S(2)}, u32[]{:S(2)}) collective-permute-start(bf16[96,1280]{1,0:T(8,128)(2,1)S(1)} %shard_map.284.refs_0_), channel_id=1, source_target_pairs={{0,24},{1,97},{2,26},{3,99},{4,28},{5,101},{6,30},{7,103},{8,0},{9... | collective-permute-start | bytes 737288 | tf_op jit(solution)/shard_map/ppermute | solution.py:819
  117.9 5.1 %collective-permute-done.19.refs_3_ = bf16[96,1280]{1,0:T(8,128)(2,1)S(1)} collective-permute-done((bf16[96,1280]{1,0:T(8,128)(2,1)S(1)}, bf16[96,1280]{1,0:T(8,128)(2,1)S(1)}, u32[]{:S(2)}, u32[]{:S(2)}) %collective-permute-start.19) | collective-permute-done | bytes 245792 | tf_op jit(solution)/shard_map/ppermute | solution.py:819
  123.9 2.9 %collective-permute-done.17.refs_1_ = bf16[96,1280]{1,0:T(8,128)(2,1)S(1)} collective-permute-done((bf16[96,1280]{1,0:T(8,128)(2,1)S(1)}, bf16[96,1280]{1,0:T(8,128)(2,1)S(1)}, u32[]{:S(2)}, u32[]{:S(2)}) %collective-permute-start.17) | collective-permute-done | bytes 245792 | tf_op jit(solution)/shard_map/ppermute | solution.py:819
  127.4 2.4 %collective-permute-start.22 = (bf16[4,96,1280]{2,1,0:T(8,128)(2,1)S(1)}, bf16[4,96,1280]{2,1,0:T(8,128)(2,1)S(1)}, u32[]{:S(2)}, u32[]{:S(2)}) collective-permute-start(bf16[4,96,1280]{2,1,0:T(8,128)(2,1)S(1)} %shard_map.287.refs_0_), channel_id=1, source_target_pairs={{0,96},{1,25},{2,98},{3,27},{4,100},{5,29},{6,102},{7,31},{8,104},... | collective-permute-start | bytes 2949128 | tf_op jit(solution)/shard_map/ppermute | solution.py:819
  130.8 5.5 %all-gather.5.cloned.1.call-done.total = bf16[1024,1536]{1,0:T(8,128)(2,1)} async-done(((bf16[128,1536]{1,0:T(8,128)(2,1)}), bf16[1024,1536]{1,0:T(8,128)(2,1)}) %all-gather.5.cloned.1.call-update) | async-done | bytes 3145744 | tf_op jit(solution)/shard_map/all_gather | solution.py:1125
  136.3 6.9 %shard_map.285 = bf16[1024,1536]{1,0:T(8,128)(2,1)} custom-call(bf16[1024,1536]{1,0:T(8,128)(2,1)} %all-gather.5.cloned.1.call-done.total, bf16[1024,1536]{1,0:T(8,128)(2,1)} %tokens.5, bf16[1024,1536]{1,0:T(8,128)(2,1)} %cotangent.5, f32[1536]{0:T(1024)} %norm_gain.5), custom_call_target="tpu_custom_call" | custom-call | tf_op jit(solution)/shard_map/pallas_call | solution.py:1150
  143.2 1.9 %shard_map.288 = (f32[1536,384]{1,0:T(8,128)}, f32[1536,384]{1,0:T(8,128)}, f32[384,1536]{1,0:T(8,128)}) custom-call(s32[5]{0:T(128)S(1)} %copy-done.2, bf16[4,96,1280]{2,1,0:T(8,128)(2,1)S(1)} %shard_map.287.refs_0_), custom_call_target="tpu_custom_call" | custom-call | tf_op jit(solution)/shard_map/pallas_call | solution.py:832
  145.0 6.4 %collective-permute-done.22.refs_1_.refs_3_ = bf16[4,96,1280]{2,1,0:T(8,128)(2,1)S(1)} collective-permute-done((bf16[4,96,1280]{2,1,0:T(8,128)(2,1)S(1)}, bf16[4,96,1280]{2,1,0:T(8,128)(2,1)S(1)}, u32[]{:S(2)}, u32[]{:S(2)}) %collective-permute-start.22) | collective-permute-done | bytes 983072 | tf_op jit(solution)/shard_map/ppermute | solution.py:819
  151.4 2.6 %shard_map.289 = (f32[1536,384]{1,0:T(8,128)}, f32[1536,384]{1,0:T(8,128)}, f32[384,1536]{1,0:T(8,128)}) custom-call(s32[5]{0:T(128)S(1)} %copy-done.2, bf16[4,96,1280]{2,1,0:T(8,128)(2,1)S(1)} %collective-permute-done.21.refs_0_.refs_2_, ...), custom_call_target="tpu_custom_call", output_to_operand_aliasing={{0}: (3, {}), {1}: (4, {}), {2}: (5, {})} | custom-call | tf_op jit(solution)/shard_map/pallas_call | solution.py:832
  155.2 2.5 %shard_map.290 = (f32[6,1536]{1,0:T(8,128)}, f32[1,6]{1,0:T(1,128)}, f32[1,6]{1,0:T(1,128)}, f32[1,6]{1,0:T(1,128)}, f32[4,384]{1,0:T(4,128)}, /*index=5*/f32[38...) custom-call(s32[5]{0:T(128)S(1)} %copy-done.2, bf16[4,96,1280]{2,1,0:T(8,128)(2,1)S(1)} %shard_map.287.refs_0_, ...), custom_call_target="tpu_custom_call" | custom-call | tf_op jit(solution)/shard_map/pallas_call | solution.py:832
  157.7 3.6 %collective-permute-start.25 = (bf16[224,256]{1,0:T(8,128)(2,1)S(1)}, bf16[224,256]{1,0:T(8,128)(2,1)S(1)}, u32[]{:S(2)}, u32[]{:S(2)}) collective-permute-start(bf16[224,256]{1,0:T(8,128)(2,1)S(1)} %get-tuple-element.132.refs_0_), channel_id=1, source_target_pairs={{0,6},{1,7},{2,0},{3,1},{4,2},{5,3},{6,4},{7,5},{8,14},{9,15},{10,... | collective-permute-start | bytes 344072 | tf_op jit(solution)/shard_map/ppermute | solution.py:806
  162.0 4.1 %all-gather.3.cloned.1.call-done.total = bf16[1024,1536]{1,0:T(8,128)(2,1)} async-done(((bf16[128,1536]{1,0:T(8,128)(2,1)}), bf16[1024,1536]{1,0:T(8,128)(2,1)}) %all-gather.3.cloned.1.call-update) | async-done | bytes 3145744 | tf_op jit(solution)/shard_map/all_gather | solution.py:1136
  166.1 4.6 %shard_map.286 = bf16[1024,1536]{1,0:T(8,128)(2,1)} custom-call(bf16[1024,1536]{1,0:T(8,128)(2,1)} %all-gather.3.cloned.1.call-done.total, bf16[1024,1536]{1,0:T(8,128)(2,1)} %tokens.5, f32[8,1024]{1,0:T(8,128)} %add_add_fusion.stats), custom_call_target="tpu_custom_call" | custom-call | tf_op jit(solution)/shard_map/pallas_call | solution.py:1159
  170.7 3.1 %shard_map.291 = (f32[1536,384]{1,0:T(8,128)}, f32[1536,384]{1,0:T(8,128)}, f32[384,1536]{1,0:T(8,128)}) custom-call(s32[5]{0:T(128)S(1)} %copy-done.2, bf16[4,96,1280]{2,1,0:T(8,128)(2,1)} %collective-permute-done.20.refs_1_.refs_0_, f32[1536,384]{1,0:T(8,128)} %get-tuple-element.125.refs_1_, ...), custom_call_target="tpu_custom_call", output_to_operand_aliasing={{0}: (2, {}), {1}: (3, {}), {2}: (4, {})} | custom-call | tf_op jit(solution)/shard_map/pallas_call | solution.py:832
  176.5 1.8 shard_map.292
  (71 shorter events, 25.1 us)
Async XLA Ops:
  7.2 60.1 %reduce-scatter.3.cloned.1.call-start = ((), (), s32[]{:S(2)}) async-start(), calls=%async_computation.2 | async-start | bytes 3538944 | tf_op jit(solution)/shard_map/reduce_scatter | solution.py:983
  26.0 80.1 %reduce-scatter.5.cloned.1.call-start = ((), (), s32[]{:S(2)}) async-start(), calls=%async_computation.4 | async-start | bytes 3538944 | tf_op jit(solution)/shard_map/reduce_scatter | solution.py:1086
  26.7 2.3 %collective-permute-start = (f32[8,1024]{1,0:T(8,128)S(1)}, f32[8,1024]{1,0:T(8,128)S(1)}, u32[]{:S(2)}, u32[]{:S(2)}) collective-permute-start(f32[8,1024]{1,0:T(8,128)S(1)} %copy-done.4), channel_id=1, source_target_pairs={{0,1},{1,0},{2,3},{3,2},{4,5},{5,4},{6,7},{7,6},{8,9},{9,8},{10,11... | collective-permute-start | bytes 98312 | tf_op jit(solution)/shard_map/ppermute | solution.py:802
  29.0 5.8 %collective-permute-start.3 = (f32[8,1024]{1,0:T(8,128)S(1)}, f32[8,1024]{1,0:T(8,128)S(1)}, u32[]{:S(2)}, u32[]{:S(2)}) collective-permute-start(f32[8,1024]{1,0:T(8,128)S(1)} %add.27), channel_id=1, source_target_pairs={{0,6},{1,7},{2,0},{3,1},{4,2},{5,3},{6,4},{7,5},{8,14},{9,15},{10,... | collective-permute-start | bytes 98312 | tf_op jit(solution)/shard_map/ppermute | solution.py:806
  32.8 4.0 %collective-permute-start.2 = (f32[8,1024]{1,0:T(8,128)S(1)}, f32[8,1024]{1,0:T(8,128)S(1)}, u32[]{:S(2)}, u32[]{:S(2)}) collective-permute-start(f32[8,1024]{1,0:T(8,128)S(1)} %add.27), channel_id=1, source_target_pairs={{0,2},{1,3},{2,4},{3,5},{4,6},{5,7},{6,0},{7,1},{8,10},{9,11},{10,... | collective-permute-start | bytes 98312 | tf_op jit(solution)/shard_map/ppermute | solution.py:806
  32.8 4.3 %collective-permute-start.1 = (f32[8,1024]{1,0:T(8,128)S(1)}, f32[8,1024]{1,0:T(8,128)S(1)}, u32[]{:S(2)}, u32[]{:S(2)}) collective-permute-start(f32[8,1024]{1,0:T(8,128)S(1)} %add.27), channel_id=1, source_target_pairs={{0,4},{1,5},{2,6},{3,7},{4,0},{5,1},{6,2},{7,3},{8,12},{9,13},{10,... | collective-permute-start | bytes 98312 | tf_op jit(solution)/shard_map/ppermute | solution.py:806
  67.2 69.1 %all-gather.5.cloned.1.call-start = ((), (), s32[]{:S(2)}) async-start(), calls=%async_computation.5 | async-start | bytes 3538944 | tf_op jit(solution)/shard_map/all_gather | solution.py:1125
  67.3 29.6 %collective-permute-start.4 = (bf16[4,96,1280]{2,1,0:T(8,128)(2,1)}, bf16[4,96,1280]{2,1,0:T(8,128)(2,1)S(1)}, u32[]{:S(2)}, u32[]{:S(2)}) collective-permute-start(bf16[4,96,1280]{2,1,0:T(8,128)(2,1)} %get-tuple-element.98), channel_id=1, source_target_pairs={{0,32},{1,9},{2,34},{3,11},{4,36},{5,13},{6,38},{7,15},{8,40},{9,1... | collective-permute-start | bytes 2949128 | tf_op jit(solution)/shard_map/ppermute | solution.py:819
  68.6 28.3 %collective-permute-start.5 = (bf16[4,96,1280]{2,1,0:T(8,128)(2,1)}, bf16[4,96,1280]{2,1,0:T(8,128)(2,1)S(1)}, u32[]{:S(2)}, u32[]{:S(2)}) collective-permute-start(bf16[4,96,1280]{2,1,0:T(8,128)(2,1)} %get-tuple-element.100), channel_id=1, source_target_pairs={{0,64},{1,17},{2,66},{3,19},{4,68},{5,21},{6,70},{7,23},{8,72},{9,... | collective-permute-start | bytes 2949128 | tf_op jit(solution)/shard_map/ppermute | solution.py:819
  71.0 25.8 %collective-permute-start.6 = (bf16[4,96,1280]{2,1,0:T(8,128)(2,1)S(1)}, bf16[4,96,1280]{2,1,0:T(8,128)(2,1)S(1)}, u32[]{:S(2)}, u32[]{:S(2)}) collective-permute-start(bf16[4,96,1280]{2,1,0:T(8,128)(2,1)S(1)} %copy-done.5), channel_id=1, source_target_pairs={{0,96},{1,25},{2,98},{3,27},{4,100},{5,29},{6,102},{7,31},{8,104},... | collective-permute-start | bytes 2949128 | tf_op jit(solution)/shard_map/ppermute | solution.py:819
  72.2 4.1 %collective-permute-start.7 = (bf16[4,192,256]{2,1,0:T(8,128)(2,1)S(1)}, bf16[4,192,256]{2,1,0:T(8,128)(2,1)S(1)}, u32[]{:S(2)}, u32[]{:S(2)}) collective-permute-start(bf16[4,192,256]{2,1,0:T(8,128)(2,1)S(1)} %copy-done.6), channel_id=1, source_target_pairs={{0,1},{1,0},{2,3},{3,2},{4,5},{5,4},{6,7},{7,6},{8,9},{9,8},{10,11... | collective-permute-start | bytes 1179656 | tf_op jit(solution)/shard_map/ppermute | solution.py:802
  76.9 6.1 %collective-permute-start.8 = (bf16[192,256]{1,0:T(8,128)(2,1)S(1)}, bf16[192,256]{1,0:T(8,128)(2,1)S(1)}, u32[]{:S(2)}, u32[]{:S(2)}) collective-permute-start(bf16[192,256]{1,0:T(8,128)(2,1)S(1)} %get-tuple-element.106), channel_id=1, source_target_pairs={{0,2},{1,3},{2,4},{3,5},{4,6},{5,7},{6,0},{7,1},{8,10},{9,11},{10,... | collective-permute-start | bytes 294920 | tf_op jit(solution)/shard_map/ppermute | solution.py:806
  77.2 11.0 %collective-permute-start.9 = (bf16[192,256]{1,0:T(8,128)(2,1)S(1)}, bf16[192,256]{1,0:T(8,128)(2,1)S(1)}, u32[]{:S(2)}, u32[]{:S(2)}) collective-permute-start(bf16[192,256]{1,0:T(8,128)(2,1)S(1)} %get-tuple-element.107), channel_id=1, source_target_pairs={{0,4},{1,5},{2,6},{3,7},{4,0},{5,1},{6,2},{7,3},{8,12},{9,13},{10,... | collective-permute-start | bytes 294920 | tf_op jit(solution)/shard_map/ppermute | solution.py:806
  83.0 5.2 %collective-permute-start.10 = (bf16[192,256]{1,0:T(8,128)(2,1)S(1)}, bf16[192,256]{1,0:T(8,128)(2,1)S(1)}, u32[]{:S(2)}, u32[]{:S(2)}) collective-permute-start(bf16[192,256]{1,0:T(8,128)(2,1)S(1)} %get-tuple-element.108), channel_id=1, source_target_pairs={{0,6},{1,7},{2,0},{3,1},{4,2},{5,3},{6,4},{7,5},{8,14},{9,15},{10,... | collective-permute-start | bytes 294920 | tf_op jit(solution)/shard_map/ppermute | solution.py:806
  88.9 5.1 %collective-permute-start.11 = (bf16[4,32,128]{2,1,0:T(8,128)(2,1)S(1)}, bf16[4,32,128]{2,1,0:T(8,128)(2,1)S(1)}, u32[]{:S(2)}, u32[]{:S(2)}) collective-permute-start(bf16[4,32,128]{2,1,0:T(8,128)(2,1)S(1)} %get-tuple-element.110), channel_id=1, source_target_pairs={{0,32},{1,9},{2,34},{3,11},{4,36},{5,13},{6,38},{7,15},{8,40},{9,1... | collective-permute-start | bytes 98312 | tf_op jit(solution)/shard_map/ppermute | solution.py:819
  90.2 4.6 %collective-permute-start.12 = (bf16[4,32,128]{2,1,0:T(8,128)(2,1)S(1)}, bf16[4,32,128]{2,1,0:T(8,128)(2,1)S(1)}, u32[]{:S(2)}, u32[]{:S(2)}) collective-permute-start(bf16[4,32,128]{2,1,0:T(8,128)(2,1)S(1)} %get-tuple-element.111), channel_id=1, source_target_pairs={{0,64},{1,17},{2,66},{3,19},{4,68},{5,21},{6,70},{7,23},{8,72},{9,... | collective-permute-start | bytes 98312 | tf_op jit(solution)/shard_map/ppermute | solution.py:819
  94.0 2.9 %collective-permute-start.13 = (bf16[4,32,128]{2,1,0:T(8,128)(2,1)S(1)}, bf16[4,32,128]{2,1,0:T(8,128)(2,1)S(1)}, u32[]{:S(2)}, u32[]{:S(2)}) collective-permute-start(bf16[4,32,128]{2,1,0:T(8,128)(2,1)S(1)} %get-tuple-element.112), channel_id=1, source_target_pairs={{0,96},{1,25},{2,98},{3,27},{4,100},{5,29},{6,102},{7,31},{8,104},... | collective-permute-start | bytes 98312 | tf_op jit(solution)/shard_map/ppermute | solution.py:819
  97.9 8.2 %collective-permute-start.14 = (bf16[96,1280]{1,0:T(8,128)(2,1)S(1)}, bf16[96,1280]{1,0:T(8,128)(2,1)S(1)}, u32[]{:S(2)}, u32[]{:S(2)}) collective-permute-start(bf16[96,1280]{1,0:T(8,128)(2,1)S(1)} %get-tuple-element.114), channel_id=1, source_target_pairs={{0,8},{1,33},{2,10},{3,35},{4,12},{5,37},{6,14},{7,39},{8,16},{9,4... | collective-permute-start | bytes 737288 | tf_op jit(solution)/shard_map/ppermute | solution.py:819
  106.1 60.0 %all-gather.3.cloned.1.call-start = ((), (), s32[]{:S(2)}) async-start(), calls=%async_computation.3 | async-start | bytes 3538944 | tf_op jit(solution)/shard_map/all_gather | solution.py:1136
  106.1 6.6 %collective-permute-start.15 = (bf16[96,1280]{1,0:T(8,128)(2,1)S(1)}, bf16[96,1280]{1,0:T(8,128)(2,1)S(1)}, u32[]{:S(2)}, u32[]{:S(2)}) collective-permute-start(bf16[96,1280]{1,0:T(8,128)(2,1)S(1)} %get-tuple-element.115), channel_id=1, source_target_pairs={{0,16},{1,65},{2,18},{3,67},{4,20},{5,69},{6,22},{7,71},{8,24},{9,... | collective-permute-start | bytes 737288 | tf_op jit(solution)/shard_map/ppermute | solution.py:819
  107.3 7.3 %collective-permute-start.16 = (bf16[96,1280]{1,0:T(8,128)(2,1)S(1)}, bf16[96,1280]{1,0:T(8,128)(2,1)S(1)}, u32[]{:S(2)}, u32[]{:S(2)}) collective-permute-start(bf16[96,1280]{1,0:T(8,128)(2,1)S(1)} %get-tuple-element.116), channel_id=1, source_target_pairs={{0,24},{1,97},{2,26},{3,99},{4,28},{5,101},{6,30},{7,103},{8,0},{9... | collective-permute-start | bytes 737288 | tf_op jit(solution)/shard_map/ppermute | solution.py:819
  114.7 8.2 %collective-permute-start.19 = (bf16[96,1280]{1,0:T(8,128)(2,1)S(1)}, bf16[96,1280]{1,0:T(8,128)(2,1)S(1)}, u32[]{:S(2)}, u32[]{:S(2)}) collective-permute-start(bf16[96,1280]{1,0:T(8,128)(2,1)S(1)} %shard_map.284.refs_0_), channel_id=1, source_target_pairs={{0,24},{1,97},{2,26},{3,99},{4,28},{5,101},{6,30},{7,103},{8,0},{9... | collective-permute-start | bytes 737288 | tf_op jit(solution)/shard_map/ppermute | solution.py:819
  117.2 6.7 %collective-permute-start.18 = (bf16[96,1280]{1,0:T(8,128)(2,1)S(1)}, bf16[96,1280]{1,0:T(8,128)(2,1)S(1)}, u32[]{:S(2)}, u32[]{:S(2)}) collective-permute-start(bf16[96,1280]{1,0:T(8,128)(2,1)S(1)} %shard_map.284.refs_0_), channel_id=1, source_target_pairs={{0,16},{1,65},{2,18},{3,67},{4,20},{5,69},{6,22},{7,71},{8,24},{9,... | collective-permute-start | bytes 737288 | tf_op jit(solution)/shard_map/ppermute | solution.py:819
  117.9 8.9 %collective-permute-start.17 = (bf16[96,1280]{1,0:T(8,128)(2,1)S(1)}, bf16[96,1280]{1,0:T(8,128)(2,1)S(1)}, u32[]{:S(2)}, u32[]{:S(2)}) collective-permute-start(bf16[96,1280]{1,0:T(8,128)(2,1)S(1)} %shard_map.284.refs_0_), channel_id=1, source_target_pairs={{0,8},{1,33},{2,10},{3,35},{4,12},{5,37},{6,14},{7,39},{8,16},{9,4... | collective-permute-start | bytes 737288 | tf_op jit(solution)/shard_map/ppermute | solution.py:819
  127.4 24.0 %collective-permute-start.22 = (bf16[4,96,1280]{2,1,0:T(8,128)(2,1)S(1)}, bf16[4,96,1280]{2,1,0:T(8,128)(2,1)S(1)}, u32[]{:S(2)}, u32[]{:S(2)}) collective-permute-start(bf16[4,96,1280]{2,1,0:T(8,128)(2,1)S(1)} %shard_map.287.refs_0_), channel_id=1, source_target_pairs={{0,96},{1,25},{2,98},{3,27},{4,100},{5,29},{6,102},{7,31},{8,104},... | collective-permute-start | bytes 2949128 | tf_op jit(solution)/shard_map/ppermute | solution.py:819
  129.8 21.6 %collective-permute-start.21 = (bf16[4,96,1280]{2,1,0:T(8,128)(2,1)S(1)}, bf16[4,96,1280]{2,1,0:T(8,128)(2,1)S(1)}, u32[]{:S(2)}, u32[]{:S(2)}) collective-permute-start(bf16[4,96,1280]{2,1,0:T(8,128)(2,1)S(1)} %shard_map.287.refs_0_), channel_id=1, source_target_pairs={{0,64},{1,17},{2,66},{3,19},{4,68},{5,21},{6,70},{7,23},{8,72},{9,... | collective-permute-start | bytes 2949128 | tf_op jit(solution)/shard_map/ppermute | solution.py:819
  130.2 25.0 %collective-permute-start.20 = (bf16[4,96,1280]{2,1,0:T(8,128)(2,1)S(1)}, bf16[4,96,1280]{2,1,0:T(8,128)(2,1)}, u32[]{:S(2)}, u32[]{:S(2)}) collective-permute-start(bf16[4,96,1280]{2,1,0:T(8,128)(2,1)S(1)} %shard_map.287.refs_0_), channel_id=1, source_target_pairs={{0,32},{1,9},{2,34},{3,11},{4,36},{5,13},{6,38},{7,15},{8,40},{9,1... | collective-permute-start | bytes 2949128 | tf_op jit(solution)/shard_map/ppermute | solution.py:819
  157.7 17.0 %collective-permute-start.25 = (bf16[224,256]{1,0:T(8,128)(2,1)S(1)}, bf16[224,256]{1,0:T(8,128)(2,1)S(1)}, u32[]{:S(2)}, u32[]{:S(2)}) collective-permute-start(bf16[224,256]{1,0:T(8,128)(2,1)S(1)} %get-tuple-element.132.refs_0_), channel_id=1, source_target_pairs={{0,6},{1,7},{2,0},{3,1},{4,2},{5,3},{6,4},{7,5},{8,14},{9,15},{10,... | collective-permute-start | bytes 344072 | tf_op jit(solution)/shard_map/ppermute | solution.py:806
  161.3 13.4 %collective-permute-start.24 = (bf16[224,256]{1,0:T(8,128)(2,1)S(1)}, bf16[224,256]{1,0:T(8,128)(2,1)S(1)}, u32[]{:S(2)}, u32[]{:S(2)}) collective-permute-start(bf16[224,256]{1,0:T(8,128)(2,1)S(1)} %get-tuple-element.132.refs_0_), channel_id=1, source_target_pairs={{0,4},{1,5},{2,6},{3,7},{4,0},{5,1},{6,2},{7,3},{8,12},{9,13},{10,... | collective-permute-start | bytes 344072 | tf_op jit(solution)/shard_map/ppermute | solution.py:806
  161.3 13.9 %collective-permute-start.23 = (bf16[224,256]{1,0:T(8,128)(2,1)S(1)}, bf16[224,256]{1,0:T(8,128)(2,1)S(1)}, u32[]{:S(2)}, u32[]{:S(2)}) collective-permute-start(bf16[224,256]{1,0:T(8,128)(2,1)S(1)} %get-tuple-element.132.refs_0_), channel_id=1, source_target_pairs={{0,2},{1,3},{2,4},{3,5},{4,6},{5,7},{6,0},{7,1},{8,10},{9,11},{10,... | collective-permute-start | bytes 344072 | tf_op jit(solution)/shard_map/ppermute | solution.py:806
  173.8 1.9 %collective-permute-start.26 = (bf16[224,256]{1,0:T(8,128)(2,1)S(1)}, bf16[224,256]{1,0:T(8,128)(2,1)S(1)}, u32[]{:S(2)}, u32[]{:S(2)}) collective-permute-start(bf16[224,256]{1,0:T(8,128)(2,1)S(1)} %get-tuple-element.132.refs_0_), channel_id=1, source_target_pairs={{0,1},{1,0},{2,3},{3,2},{4,5},{5,4},{6,7},{7,6},{8,9},{9,8},{10,11... | collective-permute-start | bytes 344072 | tf_op jit(solution)/shard_map/ppermute | solution.py:802
  174.8 1.4 collective-permute-start.28
  (9 other events, 86.6 us)
Sparse Core Ops, SparseCore 0:
  26.1 35.8 reduce-scatter.2
  67.3 38.6 reduce-scatter.4
  107.7 28.5 all-gather.4
  137.8 28.1 all-gather.2

commit v6 on v5

--- a/solution.py
+++ b/solution.py
@@ -771,13 +771,14 @@
 
 def output_kernel(inner, total, tokens, stats, out):
     scale, _ = stats_columns(stats[...], inner)
-    out[...] = (tokens[...].astype(f32) + scale * total[...].astype(f32)).astype(bf16)
+    terms = total[...].astype(f32).reshape(tokens.shape)
+    out[...] = (tokens[...].astype(f32) + scale * terms).astype(bf16)
 
 
 def grad_kernel(total, tokens, cotangent, norm_gain, out):
     x = tokens[...].astype(f32)
     inverse = lax.rsqrt(jnp.mean(x * x, axis=1, keepdims=True) + epsilon)
-    scaled = total[...].astype(f32) * row_of(norm_gain)
+    scaled = total[...].astype(f32).reshape(tokens.shape) * row_of(norm_gain)
     moment = jnp.mean(scaled * x, axis=1, keepdims=True)
     grad = inverse * scaled - x * (inverse * inverse * inverse * moment)
     out[...] = (cotangent[...].astype(f32) + grad).astype(bf16)
@@ -1122,7 +1123,6 @@
         [sds((tall, lanes), bf16)] * side,
     )
     weights = [weights[0]] + [move_dp(weights[k], k, side, 1) for k in range(1, side)]
-    grad_sum = lax.all_gather(after(grad_sum, weights[1]), "tensor", tiled=True)
 
 
     vmem = pltpu.CompilerParams(vmem_limit_bytes=SMALL_VMEM)
@@ -1133,7 +1133,9 @@
         compiler_params=vmem,
         cost_estimate=free,
     )(*weights, norm_gain_part)
-    out_sum = lax.all_gather(after(out_sum, weights), "tensor", tiled=True)
+    sums = lax.all_gather(
+        jnp.concatenate([after(grad_sum, weights), out_sum], axis=0), "tensor"
+    )
     weights = [weights] + [move_dp(weights, k, side, 1) for k in range(1, side)]
     weights = at_place(
         line_kernel,
@@ -1147,24 +1149,27 @@
     weights = [weights] + [move_dp(weights, k, side, 0) for k in range(1, side)]
     wide = LEN // 2
     wide_rows = by_rows(features, rows=wide)
+    sum_rows_at = lambda which: pl.BlockSpec(
+        (wide * 8 // LEN, LEN // 8, features), lambda i: (i, which, 0)
+    )
     grad_tokens = pl.pallas_call(
         grad_kernel,
         grid=(LEN // wide,),
-        in_specs=[wide_rows] * 3 + [whole(norm_gain)],
+        in_specs=[sum_rows_at(0), wide_rows, wide_rows, whole(norm_gain)],
         out_specs=wide_rows,
         out_shape=sds((LEN, features), bf16),
         compiler_params=params,
         cost_estimate=free,
-    )(grad_sum, tokens, cotangent, norm_gain)
+    )(sums, tokens, cotangent, norm_gain)
     block_output = pl.pallas_call(
         partial(output_kernel, inner),
         grid=(LEN // wide,),
-        in_specs=[wide_rows, wide_rows, pl.BlockSpec((8, wide), lambda i: (0, i))],
+        in_specs=[sum_rows_at(1), wide_rows, pl.BlockSpec((8, wide), lambda i: (0, i))],
         out_specs=wide_rows,
         out_shape=sds((LEN, features), bf16),
         compiler_params=params,
         cost_estimate=free,
-    )(after(out_sum, grad_tokens), tokens, stats)
+    )(after(sums, grad_tokens), tokens, stats)
     across = features // side // channels
 
     def unpack(steps_back, *operands):
@@ -1189,7 +1194,7 @@
             {1 + count + i: i for i in range(len(operands) - count)},
         )
 
-    unpacked = unpack([0], after(weights[0], grad_tokens))
+    unpacked = unpack([0], weights[0])
     others = list(range(2, side))
     unpacked = unpack(others, *[weights[k] for k in others], *unpacked)
     weights[1] = after(weights[1], unpacked[0])

time: 187 us -> 198 us (1.059)
  starting transfers between devices: 42.1 us -> 60.8 us
  waiting for transfers between devices: 52.4 us -> 47.7 us
  Pallas kernels: 74.4 us -> 71.3 us
    ppermute x6, starting transfers between devices: 5.7 us -> 24.1 us  [swap_core(): return lax.ppermute(x, 'tensor', [(i, i ^ 1) for i in range(8)])]
    ppermute x15, waiting for transfers between devices: 25.6 us -> 36.4 us  [move_dp(): return lax.ppermute(x, ('dp', 'tensor'), pairs)]
    all_gather x2 -> x1, waiting for transfers between devices: 9.57 us -> 0.01 us  [on_device(): lax.all_gather(jnp.concatenate([after(grad_sum, weights), out_sum], axis=...]
    reduce_scatter x1, waiting for transfers between devices: 6.56 us -> 0.02 us  [on_device(): grad_sum = lax.psum_scatter(part, 'tensor', scatter_dimension=0, tiled=True)]
    pallas_call x9, Pallas kernels: 14.7 us -> 12.3 us  [at_place(): pl.pallas_call(kernel, grid_spec=pltpu.PrefetchScalarGridSpec(num_scalar_...]
  transfers between devices with their start and end apart: 34 -> 33, of which waited for: 23 -> 18; matrix products, arithmetic and copies ran while one was open for 1% -> 1% of each run, Pallas kernels for 29% -> 26%
where the time goes in v6:
time: 198 us
  Pallas kernels  71.3 us (36%)
  starting transfers between devices  60.8 us (31%)
  waiting for transfers between devices  47.7 us (24%)
  between operations  14 us (7%)
  other arithmetic  2.54 us (1%)
    ppermute x15, waiting for transfers between devices, move_dp(): return lax.ppermute(x, ('dp', 'tensor'), pairs)  36.4 us
    pallas_call x1, Pallas kernels, on_device(): pl.pallas_call(partial(backward_kernel, heads, inner, steps, side), grid=...  29.3 us
    ppermute x6, starting transfers between devices, swap_core(): return lax.ppermute(x, 'tensor', [(i, i ^ 1) for i in range(8)])  24.1 us
    ppermute x15, starting transfers between devices, move_dp(): return lax.ppermute(x, ('dp', 'tensor'), pairs)  21.1 us
    pallas_call x1, Pallas kernels, on_device(): pl.pallas_call(partial(forward_kernel, heads), grid=(steps,), in_specs=[b...  18.7 us
    ppermute x9, starting transfers between devices, move_z(): return lax.ppermute(x, 'tensor', [(i, (i + 2 * k) % 8) for i in range(8)])  15.5 us
    pallas_call x9, Pallas kernels, at_place(): pl.pallas_call(kernel, grid_spec=pltpu.PrefetchScalarGridSpec(num_scalar_...  12.3 us
    ppermute x9, waiting for transfers between devices, move_z(): return lax.ppermute(x, 'tensor', [(i, (i + 2 * k) % 8) for i in range(8)])  7.63 us
  transfers between devices with their start and end apart: 33, of which 18 were waited for; matrix products, arithmetic and copies ran while one was open for 1% of the time, Pallas kernels for 26%

profile of v6, /device:TPU:1, one launch (start us, length us, event | category | flops | bytes accessed | tf_op | source)
XLA Modules:
  0.0 197.6 jit_solution(3589136358321940780)
XLA Ops:
  7.2 18.7 %shard_map.279 = (bf16[1024,1536]{1,0:T(8,128)(2,1)}, f32[1024,384]{1,0:T(8,128)}, f32[1024,384]{1,0:T(8,128)}, f32[1024,384]{1,0:T(8,128)}, f32[1024,256]{1,0:T...) custom-call(bf16[1024,1536]{1,0:T(8,128)(2,1)} %tokens.5, ...), custom_call_target="tpu_custom_call" | custom-call | tf_op jit(solution)/shard_map/pallas_call | solution.py:909
  26.7 1.4 collective-permute-start
  29.0 3.8 %collective-permute-start.3 = (f32[8,1024]{1,0:T(8,128)S(1)}, f32[8,1024]{1,0:T(8,128)S(1)}, u32[]{:S(2)}, u32[]{:S(2)}) collective-permute-start(f32[8,1024]{1,0:T(8,128)S(1)} %add.27), channel_id=1, source_target_pairs={{0,6},{1,7},{2,0},{3,1},{4,2},{5,3},{6,4},{7,5},{8,14},{9,15},{10,... | collective-permute-start | bytes 98312 | tf_op jit(solution)/shard_map/ppermute | solution.py:807
  34.8 2.1 %collective-permute-done.2 = f32[8,1024]{1,0:T(8,128)S(1)} collective-permute-done((f32[8,1024]{1,0:T(8,128)S(1)}, f32[8,1024]{1,0:T(8,128)S(1)}, u32[]{:S(2)}, u32[]{:S(2)}) %collective-permute-start.2) | collective-permute-done | bytes 32800 | tf_op jit(solution)/shard_map/ppermute | solution.py:807
  37.8 29.3 %shard_map.280 = (bf16[1024,1536]{1,0:T(8,128)(2,1)}, f32[8,1536]{1,0:T(8,128)}, bf16[4,192,256]{2,1,0:T(8,128)(2,1)}, bf16[4,192,256]{2,1,0:T(8,128)(2,1)}, bf1...) custom-call(s32[5]{0:T(128)} %stack.23.place, ...), custom_call_target="tpu_custom_call" | custom-call | tf_op jit(solution)/shard_map/pallas_call | solution.py:994
  68.6 2.4 %collective-permute-start.5 = (bf16[4,96,1280]{2,1,0:T(8,128)(2,1)}, bf16[4,96,1280]{2,1,0:T(8,128)(2,1)S(1)}, u32[]{:S(2)}, u32[]{:S(2)}) collective-permute-start(bf16[4,96,1280]{2,1,0:T(8,128)(2,1)} %get-tuple-element.98), channel_id=1, source_target_pairs={{0,64},{1,17},{2,66},{3,19},{4,68},{5,21},{6,70},{7,23},{8,72},{9,... | collective-permute-start | bytes 2949128 | tf_op jit(solution)/shard_map/ppermute | solution.py:820
  72.2 2.8 %collective-permute-start.7 = (bf16[4,192,256]{2,1,0:T(8,128)(2,1)S(1)}, bf16[4,192,256]{2,1,0:T(8,128)(2,1)S(1)}, u32[]{:S(2)}, u32[]{:S(2)}) collective-permute-start(bf16[4,192,256]{2,1,0:T(8,128)(2,1)S(1)} %copy-done.7), channel_id=1, source_target_pairs={{0,1},{1,0},{2,3},{3,2},{4,5},{5,4},{6,7},{7,6},{8,9},{9,8},{10,11... | collective-permute-start | bytes 1179656 | tf_op jit(solution)/shard_map/ppermute | solution.py:803
  77.3 3.9 %collective-permute-start.9 = (bf16[192,256]{1,0:T(8,128)(2,1)S(1)}, bf16[192,256]{1,0:T(8,128)(2,1)S(1)}, u32[]{:S(2)}, u32[]{:S(2)}) collective-permute-start(bf16[192,256]{1,0:T(8,128)(2,1)S(1)} %get-tuple-element.105), channel_id=1, source_target_pairs={{0,4},{1,5},{2,6},{3,7},{4,0},{5,1},{6,2},{7,3},{8,12},{9,13},{10,... | collective-permute-start | bytes 294920 | tf_op jit(solution)/shard_map/ppermute | solution.py:807
  81.1 2.0 %collective-permute-done.8.one = bf16[192,256]{1,0:T(8,128)(2,1)S(1)} collective-permute-done((bf16[192,256]{1,0:T(8,128)(2,1)S(1)}, bf16[192,256]{1,0:T(8,128)(2,1)S(1)}, u32[]{:S(2)}, u32[]{:S(2)}) %collective-permute-start.8) | collective-permute-done | bytes 98336 | tf_op jit(solution)/shard_map/ppermute | solution.py:807
  83.1 2.4 %collective-permute-start.10 = (bf16[192,256]{1,0:T(8,128)(2,1)S(1)}, bf16[192,256]{1,0:T(8,128)(2,1)S(1)}, u32[]{:S(2)}, u32[]{:S(2)}) collective-permute-start(bf16[192,256]{1,0:T(8,128)(2,1)S(1)} %get-tuple-element.106), channel_id=1, source_target_pairs={{0,6},{1,7},{2,0},{3,1},{4,2},{5,3},{6,4},{7,5},{8,14},{9,15},{10,... | collective-permute-start | bytes 294920 | tf_op jit(solution)/shard_map/ppermute | solution.py:807
  85.5 2.8 %collective-permute-done.9.two = bf16[192,256]{1,0:T(8,128)(2,1)S(1)} collective-permute-done((bf16[192,256]{1,0:T(8,128)(2,1)S(1)}, bf16[192,256]{1,0:T(8,128)(2,1)S(1)}, u32[]{:S(2)}, u32[]{:S(2)}) %collective-permute-start.9) | collective-permute-done | bytes 98336 | tf_op jit(solution)/shard_map/ppermute | solution.py:807
  90.3 2.5 %collective-permute-start.12 = (bf16[4,32,128]{2,1,0:T(8,128)(2,1)S(1)}, bf16[4,32,128]{2,1,0:T(8,128)(2,1)S(1)}, u32[]{:S(2)}, u32[]{:S(2)}) collective-permute-start(bf16[4,32,128]{2,1,0:T(8,128)(2,1)S(1)} %get-tuple-element.109), channel_id=1, source_target_pairs={{0,64},{1,17},{2,66},{3,19},{4,68},{5,21},{6,70},{7,23},{8,72},{9,... | collective-permute-start | bytes 98312 | tf_op jit(solution)/shard_map/ppermute | solution.py:820
  94.8 2.0 %collective-permute-done.13.refs_7_ = bf16[4,32,128]{2,1,0:T(8,128)(2,1)S(1)} collective-permute-done((bf16[4,32,128]{2,1,0:T(8,128)(2,1)S(1)}, bf16[4,32,128]{2,1,0:T(8,128)(2,1)S(1)}, u32[]{:S(2)}, u32[]{:S(2)}) %collective-permute-start.13) | collective-permute-done | bytes 32800 | tf_op jit(solution)/shard_map/ppermute | solution.py:820
  97.9 1.6 collective-permute-start.14
  99.5 2.3 %collective-permute-start.15 = (bf16[96,1280]{1,0:T(8,128)(2,1)S(1)}, bf16[96,1280]{1,0:T(8,128)(2,1)S(1)}, u32[]{:S(2)}, u32[]{:S(2)}) collective-permute-start(bf16[96,1280]{1,0:T(8,128)(2,1)S(1)} %get-tuple-element.113), channel_id=1, source_target_pairs={{0,16},{1,65},{2,18},{3,67},{4,20},{5,69},{6,22},{7,71},{8,24},{9,... | collective-permute-start | bytes 737288 | tf_op jit(solution)/shard_map/ppermute | solution.py:820
  102.9 1.8 collective-permute-done.14.refs_1_
  104.7 3.4 %collective-permute-done.15.refs_2_ = bf16[96,1280]{1,0:T(8,128)(2,1)S(1)} collective-permute-done((bf16[96,1280]{1,0:T(8,128)(2,1)S(1)}, bf16[96,1280]{1,0:T(8,128)(2,1)S(1)}, u32[]{:S(2)}, u32[]{:S(2)}) %collective-permute-start.15) | collective-permute-done | bytes 245792 | tf_op jit(solution)/shard_map/ppermute | solution.py:820
  108.2 1.9 pad_maximum_fusion
  110.2 2.2 %collective-permute-start.19 = (bf16[96,1280]{1,0:T(8,128)(2,1)S(1)}, bf16[96,1280]{1,0:T(8,128)(2,1)S(1)}, u32[]{:S(2)}, u32[]{:S(2)}) collective-permute-start(bf16[96,1280]{1,0:T(8,128)(2,1)S(1)} %shard_map.284.refs_0_), channel_id=1, source_target_pairs={{0,24},{1,97},{2,26},{3,99},{4,28},{5,101},{6,30},{7,103},{8,0},{9... | collective-permute-start | bytes 737288 | tf_op jit(solution)/shard_map/ppermute | solution.py:820
  113.7 4.5 %collective-permute-done.19.refs_3_ = bf16[96,1280]{1,0:T(8,128)(2,1)S(1)} collective-permute-done((bf16[96,1280]{1,0:T(8,128)(2,1)S(1)}, bf16[96,1280]{1,0:T(8,128)(2,1)S(1)}, u32[]{:S(2)}, u32[]{:S(2)}) %collective-permute-start.19) | collective-permute-done | bytes 245792 | tf_op jit(solution)/shard_map/ppermute | solution.py:820
  119.1 2.5 %collective-permute-done.17.refs_1_ = bf16[96,1280]{1,0:T(8,128)(2,1)S(1)} collective-permute-done((bf16[96,1280]{1,0:T(8,128)(2,1)S(1)}, bf16[96,1280]{1,0:T(8,128)(2,1)S(1)}, u32[]{:S(2)}, u32[]{:S(2)}) %collective-permute-start.17) | collective-permute-done | bytes 245792 | tf_op jit(solution)/shard_map/ppermute | solution.py:820
  122.2 2.5 %collective-permute-start.22 = (bf16[4,96,1280]{2,1,0:T(8,128)(2,1)S(1)}, bf16[4,96,1280]{2,1,0:T(8,128)(2,1)S(1)}, u32[]{:S(2)}, u32[]{:S(2)}) collective-permute-start(bf16[4,96,1280]{2,1,0:T(8,128)(2,1)S(1)} %shard_map.287.refs_0_), channel_id=1, source_target_pairs={{0,96},{1,25},{2,98},{3,27},{4,100},{5,29},{6,102},{7,31},{8,104},... | collective-permute-start | bytes 2949128 | tf_op jit(solution)/shard_map/ppermute | solution.py:820
  125.4 1.9 shard_map.288
  127.3 19.0 %collective-permute-done.22.refs_1_.refs_3_ = bf16[4,96,1280]{2,1,0:T(8,128)(2,1)S(1)} collective-permute-done((bf16[4,96,1280]{2,1,0:T(8,128)(2,1)S(1)}, bf16[4,96,1280]{2,1,0:T(8,128)(2,1)S(1)}, u32[]{:S(2)}, u32[]{:S(2)}) %collective-permute-start.22) | collective-permute-done | bytes 983072 | tf_op jit(solution)/shard_map/ppermute | solution.py:820
  146.3 2.6 %shard_map.289 = (f32[1536,384]{1,0:T(8,128)}, f32[1536,384]{1,0:T(8,128)}, f32[384,1536]{1,0:T(8,128)}) custom-call(s32[5]{0:T(128)S(1)} %copy-done.2, bf16[4,96,1280]{2,1,0:T(8,128)(2,1)S(1)} %collective-permute-done.21.refs_0_.refs_2_, ...), custom_call_target="tpu_custom_call", output_to_operand_aliasing={{0}: (3, {}), {1}: (4, {}), {2}: (5, {})} | custom-call | tf_op jit(solution)/shard_map/pallas_call | solution.py:833
  151.1 3.2 %collective-permute-start.25 = (bf16[224,256]{1,0:T(8,128)(2,1)S(1)}, bf16[224,256]{1,0:T(8,128)(2,1)S(1)}, u32[]{:S(2)}, u32[]{:S(2)}) collective-permute-start(bf16[224,256]{1,0:T(8,128)(2,1)S(1)} %get-tuple-element.128.refs_0_), channel_id=1, source_target_pairs={{0,6},{1,7},{2,0},{3,1},{4,2},{5,3},{6,4},{7,5},{8,14},{9,15},{10,... | collective-permute-start | bytes 344072 | tf_op jit(solution)/shard_map/ppermute | solution.py:807
  154.9 1.9 shard_map.291
  157.2 16.4 %collective-permute-start.29 = (bf16[224,256]{1,0:T(8,128)(2,1)S(1)}, bf16[224,256]{1,0:T(8,128)(2,1)S(1)}, u32[]{:S(2)}, u32[]{:S(2)}) collective-permute-start(bf16[224,256]{1,0:T(8,128)(2,1)S(1)} %collective-permute-done.25.refs_3_), channel_id=1, source_target_pairs={{0,1},{1,0},{2,3},{3,2},{4,5},{5,4},{6,7},{7,6},{8,9},{9,8},{10,11... | collective-permute-start | bytes 344072 | tf_op jit(solution)/shard_map/ppermute | solution.py:803
  173.9 3.2 %collective-permute-start.27 = (bf16[224,256]{1,0:T(8,128)(2,1)S(1)}, bf16[224,256]{1,0:T(8,128)(2,1)S(1)}, u32[]{:S(2)}, u32[]{:S(2)}) collective-permute-start(bf16[224,256]{1,0:T(8,128)(2,1)S(1)} %collective-permute-done.23.refs_1_), channel_id=1, source_target_pairs={{0,1},{1,0},{2,3},{3,2},{4,5},{5,4},{6,7},{7,6},{8,9},{9,8},{10,11... | collective-permute-start | bytes 344072 | tf_op jit(solution)/shard_map/ppermute | solution.py:803
  177.1 6.2 %shard_map.285 = bf16[1024,1536]{1,0:T(8,128)(2,1)} custom-call(bf16[8,256,1536]{2,1,0:T(8,128)(2,1)} %bitcast.11, bf16[1024,1536]{1,0:T(8,128)(2,1)} %tokens.5, bf16[1024,1536]{1,0:T(8,128)(2,1)} %cotangent.5, f32[1536]{0:T(1024)} %norm_gain.5), custom_call_target="tpu_custom_call" | custom-call | tf_op jit(solution)/shard_map/pallas_call | solution.py:1155
  183.4 4.6 %shard_map.286 = bf16[1024,1536]{1,0:T(8,128)(2,1)} custom-call(bf16[8,256,1536]{2,1,0:T(8,128)(2,1)} %bitcast.12, bf16[1024,1536]{1,0:T(8,128)(2,1)} %tokens.5, f32[8,1024]{1,0:T(8,128)} %add_add_fusion.stats), custom_call_target="tpu_custom_call" | custom-call | tf_op jit(solution)/shard_map/pallas_call | solution.py:1164
  189.3 1.8 shard_map.292
  (71 shorter events, 24.0 us)
Async XLA Ops:
  7.2 60.1 %reduce-scatter.5.cloned.1.call-start = ((), (), s32[]{:S(2)}) async-start(), calls=%async_computation.3 | async-start | bytes 3538944 | tf_op jit(solution)/shard_map/reduce_scatter | solution.py:984
  26.0 82.2 %reduce-scatter.3.cloned.1.call-start = ((), (), s32[]{:S(2)}) async-start(), calls=%async_computation.2 | async-start | bytes 3538944 | tf_op jit(solution)/shard_map/reduce_scatter | solution.py:1087
  26.7 2.3 %collective-permute-start = (f32[8,1024]{1,0:T(8,128)S(1)}, f32[8,1024]{1,0:T(8,128)S(1)}, u32[]{:S(2)}, u32[]{:S(2)}) collective-permute-start(f32[8,1024]{1,0:T(8,128)S(1)} %copy-done.5), channel_id=1, source_target_pairs={{0,1},{1,0},{2,3},{3,2},{4,5},{5,4},{6,7},{7,6},{8,9},{9,8},{10,11... | collective-permute-start | bytes 98312 | tf_op jit(solution)/shard_map/ppermute | solution.py:803
  29.0 5.8 %collective-permute-start.3 = (f32[8,1024]{1,0:T(8,128)S(1)}, f32[8,1024]{1,0:T(8,128)S(1)}, u32[]{:S(2)}, u32[]{:S(2)}) collective-permute-start(f32[8,1024]{1,0:T(8,128)S(1)} %add.27), channel_id=1, source_target_pairs={{0,6},{1,7},{2,0},{3,1},{4,2},{5,3},{6,4},{7,5},{8,14},{9,15},{10,... | collective-permute-start | bytes 98312 | tf_op jit(solution)/shard_map/ppermute | solution.py:807
  32.8 4.0 %collective-permute-start.2 = (f32[8,1024]{1,0:T(8,128)S(1)}, f32[8,1024]{1,0:T(8,128)S(1)}, u32[]{:S(2)}, u32[]{:S(2)}) collective-permute-start(f32[8,1024]{1,0:T(8,128)S(1)} %add.27), channel_id=1, source_target_pairs={{0,2},{1,3},{2,4},{3,5},{4,6},{5,7},{6,0},{7,1},{8,10},{9,11},{10,... | collective-permute-start | bytes 98312 | tf_op jit(solution)/shard_map/ppermute | solution.py:807
  32.8 4.3 %collective-permute-start.1 = (f32[8,1024]{1,0:T(8,128)S(1)}, f32[8,1024]{1,0:T(8,128)S(1)}, u32[]{:S(2)}, u32[]{:S(2)}) collective-permute-start(f32[8,1024]{1,0:T(8,128)S(1)} %add.27), channel_id=1, source_target_pairs={{0,4},{1,5},{2,6},{3,7},{4,0},{5,1},{6,2},{7,3},{8,12},{9,13},{10,... | collective-permute-start | bytes 98312 | tf_op jit(solution)/shard_map/ppermute | solution.py:807
  67.2 109.9 %all-gather.3.cloned.1.call-start = ((), (), s32[]{:S(2)}) async-start(), calls=%async_computation.4 | async-start | bytes 7077888 | tf_op jit(solution)/shard_map/all_gather | solution.py:1136
  67.3 29.6 %collective-permute-start.4 = (bf16[4,96,1280]{2,1,0:T(8,128)(2,1)}, bf16[4,96,1280]{2,1,0:T(8,128)(2,1)S(1)}, u32[]{:S(2)}, u32[]{:S(2)}) collective-permute-start(bf16[4,96,1280]{2,1,0:T(8,128)(2,1)} %get-tuple-element.96), channel_id=1, source_target_pairs={{0,32},{1,9},{2,34},{3,11},{4,36},{5,13},{6,38},{7,15},{8,40},{9,1... | collective-permute-start | bytes 2949128 | tf_op jit(solution)/shard_map/ppermute | solution.py:820
  68.6 28.3 %collective-permute-start.5 = (bf16[4,96,1280]{2,1,0:T(8,128)(2,1)}, bf16[4,96,1280]{2,1,0:T(8,128)(2,1)S(1)}, u32[]{:S(2)}, u32[]{:S(2)}) collective-permute-start(bf16[4,96,1280]{2,1,0:T(8,128)(2,1)} %get-tuple-element.98), channel_id=1, source_target_pairs={{0,64},{1,17},{2,66},{3,19},{4,68},{5,21},{6,70},{7,23},{8,72},{9,... | collective-permute-start | bytes 2949128 | tf_op jit(solution)/shard_map/ppermute | solution.py:820
  71.0 25.9 %collective-permute-start.6 = (bf16[4,96,1280]{2,1,0:T(8,128)(2,1)S(1)}, bf16[4,96,1280]{2,1,0:T(8,128)(2,1)S(1)}, u32[]{:S(2)}, u32[]{:S(2)}) collective-permute-start(bf16[4,96,1280]{2,1,0:T(8,128)(2,1)S(1)} %copy-done.6), channel_id=1, source_target_pairs={{0,96},{1,25},{2,98},{3,27},{4,100},{5,29},{6,102},{7,31},{8,104},... | collective-permute-start | bytes 2949128 | tf_op jit(solution)/shard_map/ppermute | solution.py:820
  72.2 4.1 %collective-permute-start.7 = (bf16[4,192,256]{2,1,0:T(8,128)(2,1)S(1)}, bf16[4,192,256]{2,1,0:T(8,128)(2,1)S(1)}, u32[]{:S(2)}, u32[]{:S(2)}) collective-permute-start(bf16[4,192,256]{2,1,0:T(8,128)(2,1)S(1)} %copy-done.7), channel_id=1, source_target_pairs={{0,1},{1,0},{2,3},{3,2},{4,5},{5,4},{6,7},{7,6},{8,9},{9,8},{10,11... | collective-permute-start | bytes 1179656 | tf_op jit(solution)/shard_map/ppermute | solution.py:803
  77.0 6.2 %collective-permute-start.8 = (bf16[192,256]{1,0:T(8,128)(2,1)S(1)}, bf16[192,256]{1,0:T(8,128)(2,1)S(1)}, u32[]{:S(2)}, u32[]{:S(2)}) collective-permute-start(bf16[192,256]{1,0:T(8,128)(2,1)S(1)} %get-tuple-element.104), channel_id=1, source_target_pairs={{0,2},{1,3},{2,4},{3,5},{4,6},{5,7},{6,0},{7,1},{8,10},{9,11},{10,... | collective-permute-start | bytes 294920 | tf_op jit(solution)/shard_map/ppermute | solution.py:807
  77.3 11.0 %collective-permute-start.9 = (bf16[192,256]{1,0:T(8,128)(2,1)S(1)}, bf16[192,256]{1,0:T(8,128)(2,1)S(1)}, u32[]{:S(2)}, u32[]{:S(2)}) collective-permute-start(bf16[192,256]{1,0:T(8,128)(2,1)S(1)} %get-tuple-element.105), channel_id=1, source_target_pairs={{0,4},{1,5},{2,6},{3,7},{4,0},{5,1},{6,2},{7,3},{8,12},{9,13},{10,... | collective-permute-start | bytes 294920 | tf_op jit(solution)/shard_map/ppermute | solution.py:807
  83.1 5.2 %collective-permute-start.10 = (bf16[192,256]{1,0:T(8,128)(2,1)S(1)}, bf16[192,256]{1,0:T(8,128)(2,1)S(1)}, u32[]{:S(2)}, u32[]{:S(2)}) collective-permute-start(bf16[192,256]{1,0:T(8,128)(2,1)S(1)} %get-tuple-element.106), channel_id=1, source_target_pairs={{0,6},{1,7},{2,0},{3,1},{4,2},{5,3},{6,4},{7,5},{8,14},{9,15},{10,... | collective-permute-start | bytes 294920 | tf_op jit(solution)/shard_map/ppermute | solution.py:807
  88.9 5.0 %collective-permute-start.11 = (bf16[4,32,128]{2,1,0:T(8,128)(2,1)S(1)}, bf16[4,32,128]{2,1,0:T(8,128)(2,1)S(1)}, u32[]{:S(2)}, u32[]{:S(2)}) collective-permute-start(bf16[4,32,128]{2,1,0:T(8,128)(2,1)S(1)} %get-tuple-element.108), channel_id=1, source_target_pairs={{0,32},{1,9},{2,34},{3,11},{4,36},{5,13},{6,38},{7,15},{8,40},{9,1... | collective-permute-start | bytes 98312 | tf_op jit(solution)/shard_map/ppermute | solution.py:820
  90.3 4.6 %collective-permute-start.12 = (bf16[4,32,128]{2,1,0:T(8,128)(2,1)S(1)}, bf16[4,32,128]{2,1,0:T(8,128)(2,1)S(1)}, u32[]{:S(2)}, u32[]{:S(2)}) collective-permute-start(bf16[4,32,128]{2,1,0:T(8,128)(2,1)S(1)} %get-tuple-element.109), channel_id=1, source_target_pairs={{0,64},{1,17},{2,66},{3,19},{4,68},{5,21},{6,70},{7,23},{8,72},{9,... | collective-permute-start | bytes 98312 | tf_op jit(solution)/shard_map/ppermute | solution.py:820
  94.0 2.9 %collective-permute-start.13 = (bf16[4,32,128]{2,1,0:T(8,128)(2,1)S(1)}, bf16[4,32,128]{2,1,0:T(8,128)(2,1)S(1)}, u32[]{:S(2)}, u32[]{:S(2)}) collective-permute-start(bf16[4,32,128]{2,1,0:T(8,128)(2,1)S(1)} %get-tuple-element.110), channel_id=1, source_target_pairs={{0,96},{1,25},{2,98},{3,27},{4,100},{5,29},{6,102},{7,31},{8,104},... | collective-permute-start | bytes 98312 | tf_op jit(solution)/shard_map/ppermute | solution.py:820
  97.9 6.7 %collective-permute-start.14 = (bf16[96,1280]{1,0:T(8,128)(2,1)S(1)}, bf16[96,1280]{1,0:T(8,128)(2,1)S(1)}, u32[]{:S(2)}, u32[]{:S(2)}) collective-permute-start(bf16[96,1280]{1,0:T(8,128)(2,1)S(1)} %get-tuple-element.112), channel_id=1, source_target_pairs={{0,8},{1,33},{2,10},{3,35},{4,12},{5,37},{6,14},{7,39},{8,16},{9,4... | collective-permute-start | bytes 737288 | tf_op jit(solution)/shard_map/ppermute | solution.py:820
  99.5 8.5 %collective-permute-start.15 = (bf16[96,1280]{1,0:T(8,128)(2,1)S(1)}, bf16[96,1280]{1,0:T(8,128)(2,1)S(1)}, u32[]{:S(2)}, u32[]{:S(2)}) collective-permute-start(bf16[96,1280]{1,0:T(8,128)(2,1)S(1)} %get-tuple-element.113), channel_id=1, source_target_pairs={{0,16},{1,65},{2,18},{3,67},{4,20},{5,69},{6,22},{7,71},{8,24},{9,... | collective-permute-start | bytes 737288 | tf_op jit(solution)/shard_map/ppermute | solution.py:820
  101.8 6.2 %collective-permute-start.16 = (bf16[96,1280]{1,0:T(8,128)(2,1)S(1)}, bf16[96,1280]{1,0:T(8,128)(2,1)S(1)}, u32[]{:S(2)}, u32[]{:S(2)}) collective-permute-start(bf16[96,1280]{1,0:T(8,128)(2,1)S(1)} %get-tuple-element.114), channel_id=1, source_target_pairs={{0,24},{1,97},{2,26},{3,99},{4,28},{5,101},{6,30},{7,103},{8,0},{9... | collective-permute-start | bytes 737288 | tf_op jit(solution)/shard_map/ppermute | solution.py:820
  110.2 8.0 %collective-permute-start.19 = (bf16[96,1280]{1,0:T(8,128)(2,1)S(1)}, bf16[96,1280]{1,0:T(8,128)(2,1)S(1)}, u32[]{:S(2)}, u32[]{:S(2)}) collective-permute-start(bf16[96,1280]{1,0:T(8,128)(2,1)S(1)} %shard_map.284.refs_0_), channel_id=1, source_target_pairs={{0,24},{1,97},{2,26},{3,99},{4,28},{5,101},{6,30},{7,103},{8,0},{9... | collective-permute-start | bytes 737288 | tf_op jit(solution)/shard_map/ppermute | solution.py:820
  112.4 6.7 %collective-permute-start.18 = (bf16[96,1280]{1,0:T(8,128)(2,1)S(1)}, bf16[96,1280]{1,0:T(8,128)(2,1)S(1)}, u32[]{:S(2)}, u32[]{:S(2)}) collective-permute-start(bf16[96,1280]{1,0:T(8,128)(2,1)S(1)} %shard_map.284.refs_0_), channel_id=1, source_target_pairs={{0,16},{1,65},{2,18},{3,67},{4,20},{5,69},{6,22},{7,71},{8,24},{9,... | collective-permute-start | bytes 737288 | tf_op jit(solution)/shard_map/ppermute | solution.py:820
  113.3 8.3 %collective-permute-start.17 = (bf16[96,1280]{1,0:T(8,128)(2,1)S(1)}, bf16[96,1280]{1,0:T(8,128)(2,1)S(1)}, u32[]{:S(2)}, u32[]{:S(2)}) collective-permute-start(bf16[96,1280]{1,0:T(8,128)(2,1)S(1)} %shard_map.284.refs_0_), channel_id=1, source_target_pairs={{0,8},{1,33},{2,10},{3,35},{4,12},{5,37},{6,14},{7,39},{8,16},{9,4... | collective-permute-start | bytes 737288 | tf_op jit(solution)/shard_map/ppermute | solution.py:820
  122.2 24.1 %collective-permute-start.22 = (bf16[4,96,1280]{2,1,0:T(8,128)(2,1)S(1)}, bf16[4,96,1280]{2,1,0:T(8,128)(2,1)S(1)}, u32[]{:S(2)}, u32[]{:S(2)}) collective-permute-start(bf16[4,96,1280]{2,1,0:T(8,128)(2,1)S(1)} %shard_map.287.refs_0_), channel_id=1, source_target_pairs={{0,96},{1,25},{2,98},{3,27},{4,100},{5,29},{6,102},{7,31},{8,104},... | collective-permute-start | bytes 2949128 | tf_op jit(solution)/shard_map/ppermute | solution.py:820
  124.7 21.6 %collective-permute-start.21 = (bf16[4,96,1280]{2,1,0:T(8,128)(2,1)S(1)}, bf16[4,96,1280]{2,1,0:T(8,128)(2,1)S(1)}, u32[]{:S(2)}, u32[]{:S(2)}) collective-permute-start(bf16[4,96,1280]{2,1,0:T(8,128)(2,1)S(1)} %shard_map.287.refs_0_), channel_id=1, source_target_pairs={{0,64},{1,17},{2,66},{3,19},{4,68},{5,21},{6,70},{7,23},{8,72},{9,... | collective-permute-start | bytes 2949128 | tf_op jit(solution)/shard_map/ppermute | solution.py:820
  124.8 25.1 %collective-permute-start.20 = (bf16[4,96,1280]{2,1,0:T(8,128)(2,1)S(1)}, bf16[4,96,1280]{2,1,0:T(8,128)(2,1)S(1)}, u32[]{:S(2)}, u32[]{:S(2)}) collective-permute-start(bf16[4,96,1280]{2,1,0:T(8,128)(2,1)S(1)} %shard_map.287.refs_0_), channel_id=1, source_target_pairs={{0,32},{1,9},{2,34},{3,11},{4,36},{5,13},{6,38},{7,15},{8,40},{9,1... | collective-permute-start | bytes 2949128 | tf_op jit(solution)/shard_map/ppermute | solution.py:820
  151.1 6.1 %collective-permute-start.25 = (bf16[224,256]{1,0:T(8,128)(2,1)S(1)}, bf16[224,256]{1,0:T(8,128)(2,1)S(1)}, u32[]{:S(2)}, u32[]{:S(2)}) collective-permute-start(bf16[224,256]{1,0:T(8,128)(2,1)S(1)} %get-tuple-element.128.refs_0_), channel_id=1, source_target_pairs={{0,6},{1,7},{2,0},{3,1},{4,2},{5,3},{6,4},{7,5},{8,14},{9,15},{10,... | collective-permute-start | bytes 344072 | tf_op jit(solution)/shard_map/ppermute | solution.py:807
  154.3 19.3 %collective-permute-start.24 = (bf16[224,256]{1,0:T(8,128)(2,1)S(1)}, bf16[224,256]{1,0:T(8,128)(2,1)S(1)}, u32[]{:S(2)}, u32[]{:S(2)}) collective-permute-start(bf16[224,256]{1,0:T(8,128)(2,1)S(1)} %get-tuple-element.128.refs_0_), channel_id=1, source_target_pairs={{0,4},{1,5},{2,6},{3,7},{4,0},{5,1},{6,2},{7,3},{8,12},{9,13},{10,... | collective-permute-start | bytes 344072 | tf_op jit(solution)/shard_map/ppermute | solution.py:807
  154.3 19.6 %collective-permute-start.23 = (bf16[224,256]{1,0:T(8,128)(2,1)S(1)}, bf16[224,256]{1,0:T(8,128)(2,1)S(1)}, u32[]{:S(2)}, u32[]{:S(2)}) collective-permute-start(bf16[224,256]{1,0:T(8,128)(2,1)S(1)} %get-tuple-element.128.refs_0_), channel_id=1, source_target_pairs={{0,2},{1,3},{2,4},{3,5},{4,6},{5,7},{6,0},{7,1},{8,10},{9,11},{10,... | collective-permute-start | bytes 344072 | tf_op jit(solution)/shard_map/ppermute | solution.py:807
  157.2 30.8 %collective-permute-start.29 = (bf16[224,256]{1,0:T(8,128)(2,1)S(1)}, bf16[224,256]{1,0:T(8,128)(2,1)S(1)}, u32[]{:S(2)}, u32[]{:S(2)}) collective-permute-start(bf16[224,256]{1,0:T(8,128)(2,1)S(1)} %collective-permute-done.25.refs_3_), channel_id=1, source_target_pairs={{0,1},{1,0},{2,3},{3,2},{4,5},{5,4},{6,7},{7,6},{8,9},{9,8},{10,11... | collective-permute-start | bytes 344072 | tf_op jit(solution)/shard_map/ppermute | solution.py:803
  173.6 14.4 %collective-permute-start.28 = (bf16[224,256]{1,0:T(8,128)(2,1)S(1)}, bf16[224,256]{1,0:T(8,128)(2,1)S(1)}, u32[]{:S(2)}, u32[]{:S(2)}) collective-permute-start(bf16[224,256]{1,0:T(8,128)(2,1)S(1)} %collective-permute-done.24.refs_2_), channel_id=1, source_target_pairs={{0,1},{1,0},{2,3},{3,2},{4,5},{5,4},{6,7},{7,6},{8,9},{9,8},{10,11... | collective-permute-start | bytes 344072 | tf_op jit(solution)/shard_map/ppermute | solution.py:803
  173.9 14.1 %collective-permute-start.27 = (bf16[224,256]{1,0:T(8,128)(2,1)S(1)}, bf16[224,256]{1,0:T(8,128)(2,1)S(1)}, u32[]{:S(2)}, u32[]{:S(2)}) collective-permute-start(bf16[224,256]{1,0:T(8,128)(2,1)S(1)} %collective-permute-done.23.refs_1_), channel_id=1, source_target_pairs={{0,1},{1,0},{2,3},{3,2},{4,5},{5,4},{6,7},{7,6},{8,9},{9,8},{10,11... | collective-permute-start | bytes 344072 | tf_op jit(solution)/shard_map/ppermute | solution.py:803
  (9 other events, 101.4 us)
Sparse Core Ops, SparseCore 0:
  26.1 35.8 reduce-scatter.4
  67.3 38.7 reduce-scatter.2
  110.3 45.7 all-gather.2
